TPU v7x, 256 devices: a whole 4x4x8 slice. The times are simulated.
256 devices in a mesh: rows: 128 (over z, x, y), rep: 2 (over core).
Axes of the slice: x: 4, y: 4, z: 8, core: 2. Of those that a mesh axis runs over, the one named last changes fastest.
Arguments:
- features: bfloat16 [196608, 256], P('rows'), may hold values from -6 to 6
- degrees: int32 [196608], P('rows'), may hold values from 32 to 512
- weight: bfloat16 [256, 256], replicated, may hold values from -0.375 to 0.375
- tile_values: bfloat16 [128, 8, 22, 256, 256], P('rows', None, 'rep'), may hold values from 0.25 to 4
- tile_pos: int32 [128, 8, 22], P('rows'), may hold values from 0 to 35, as said below
- live: int32 [128, 8], P('rows'), may hold values from 1 to 22, as said below
Outputs:
- updated: bfloat16 [196608, 256], P('rows')
Inputs may be any that keep to these rules, and one draw needn't show every extreme that they name: `tile_pos`: within one row block and one column block the 22 positions are distinct. `live`: some row block has 22 used slots in every column block.
All inputs are finite; a program needn't handle non-finite values.
Results may differ from a plain program's by a relative error of at most 0.0052.
Values may be sent and summed in bfloat16 or wider, within the bound.
No kernel may reach another device: no remote copies, remote signals or barrier semaphores. Data moves between devices by JAX's collectives and lax.ppermute only.
A program may use at most 128 MiB of HBM per device.

v0:
```python
import jax
import jax.numpy as jnp
from jax import lax
from jax.sharding import PartitionSpec as P


def from_root(x, axis, root):
    mine = lax.axis_index(axis) == root
    return lax.psum(jnp.where(mine, x, jnp.zeros_like(x)), axis)


def fetch(scaled, root):
    return from_root(scaled, "rows", root)


def add_block(total, tiles, places, slots, count, source):
    side = total.shape[0]
    stacked = source.reshape(side, tiles.shape[1], source.shape[1])
    pieces = jnp.take(stacked, places % side, axis=0)
    product = jnp.einsum("mab,mbf->maf", tiles, pieces, preferred_element_type=jnp.float32)
    active = (slots < count).astype(jnp.float32)
    target = ((places // side)[:, None] == jnp.arange(side)[None, :]).astype(jnp.float32) * active[
        :, None
    ]
    return total + jnp.einsum("mk,maf->kaf", target, product, precision=lax.Precision.HIGHEST)


def finish(summed, features, inverse, weight):
    combined = (summed * inverse[:, None] + features.astype(jnp.float32)).astype(jnp.bfloat16)
    result = jnp.dot(combined, weight, preferred_element_type=jnp.float32)
    return jax.nn.relu(result).astype(jnp.bfloat16)


def on_device(features, degrees, weight, tile_values, tile_pos, live):
    rows_dev, width = features.shape
    blocks = tile_values.shape[1]
    half_slots = tile_values.shape[2]
    tile = tile_values.shape[3]
    side = rows_dev // tile
    teams = lax.axis_size("rep")
    sections = blocks // teams
    stride = lax.axis_size("rows") // blocks
    team = lax.axis_index("rep")
    inverse = lax.rsqrt(degrees.astype(jnp.float32))
    scaled = (features.astype(jnp.float32) * inverse[:, None]).astype(jnp.bfloat16)
    total = jnp.zeros((side, tile, width), jnp.float32)
    mine = lax.all_to_all(tile_values, "rep", split_axis=1, concat_axis=2, tiled=True)
    places = lax.dynamic_slice_in_dim(tile_pos[0], team * sections, sections, 0)
    counts = lax.dynamic_slice_in_dim(live[0], team * sections, sections, 0)
    slots = jnp.arange(half_slots * teams)
    for section in range(sections):
        source = fetch(scaled, (team * sections + section) * stride)
        total = add_block(total, mine[0, section], places[section], slots, counts[section], source)
    flat = total.reshape(rows_dev, width)
    summed = lax.psum(flat, "rep")
    return finish(summed, features, inverse, weight)


def solution(mesh):
    placed = (
        P("rows", None),
        P("rows"),
        P(),
        P("rows", None, "rep", None, None),
        P("rows", None, None),
        P("rows", None),
    )
    return jax.shard_map(
        on_device, mesh=mesh, in_specs=placed, out_specs=P("rows", None), check_vma=False
    )
```

profile of v0, /device:TPU:1, one launch (start us, length us, event | category | flops | bytes accessed | tf_op | source)
XLA Modules:
  0.0 362.5 jit_solution(227818464504072547)
XLA Ops:
  6.5 0.7 convert_rsqrt_fusion
  7.3 3.2 broadcast_select_fusion
  10.4 0.0 all-reduce.6.cloned.1.call-update
  10.5 0.0 all-reduce.4.cloned.1.call-start
  10.5 17.7 %all_to_all.18 = bf16[1,8,11,256,256]{4,3,2,0,1:T(8,128)(2,1)S(1)} all-to-all(bf16[1,8,11,256,256]{4,3,2,0,1:T(8,128)(2,1)} %bitcast.108), channel_id=1, replica_groups=mesh['rows'=128,'rep'=2] {'rep'}, dimensions={1} | all-to-all | bytes 23068672 | tf_op jit(solution)/shard_map/all_to_all | solution.py:47
  28.2 5.0 %copy.25 = bf16[1,4,2,11,256,256]{5,4,3,2,1,0:T(8,128)(2,1)} copy(bf16[1,4,2,11,256,256]{5,4,3,1,2,0:T(8,128)(2,1)S(1)} %bitcast.99) | data formatting | bytes 23068672 | tf_op jit(solution)/shard_map/all_to_all | solution.py:47
  33.2 0.1 constant_dynamic-slice_fusion
  33.3 0.7 fusion.68
  33.9 0.6 compare_convert_fusion.1
  34.6 0.7 compare_convert_fusion.3
  35.3 0.7 compare_convert_fusion.2
  36.0 0.6 compare_convert_fusion
  36.6 208.1 %all-reduce.6.cloned.1.call-done = (bf16[6,256,256]{2,1,0:T(8,128)(2,1)}, bf16[6,256,256]{2,1,0:T(8,128)(2,1)}, bf16[6,256,256]{2,1,0:T(8,128)(2,1)}, bf16[6,256,256]{2,1,0:T(8,128)(2,1)}) async-done(((bf16[6,256,256]{2,1,0:T(8,128)(2,1)}, bf16[6,256,256]{2,1,0:T(8,128)(2,1)}, bf16[6,256,256]{2,1,0:T(8,128)(2,1)}, bf16[6,256,256]{2,1,0:T(8,128)(2,1)}), (bf16[6,256,256]{2,1,0:T(8,128)(2,1)}, ...) | async-done | bytes 3145744 | tf_op jit(solution)/shard_map/psum | solution.py:9
  244.8 1.9 gather_fusion.2
  246.6 5.4 %fusion.19 = f32[22,256,256]{1,2,0:T(8,128)} fusion(bf16[1,4,22,256,256]{4,3,2,1,0:T(8,128)(2,1)} %bitcast.100, bf16[22,256,256]{2,1,0:T(8,128)(2,1)S(1)} %gather_fusion.2, pred[22]{0:T(512)(128)(4,1)S(1)} %get-tuple-element.30), kind=kOutput, calls=%fused_computation.24 | convolution fusion | flops 739639296 | bytes 11534358 | tf_op jit(solution)/shard_map/mab,mbf->maf/dot_general | solution.py:20
  252.0 6.5 %copy.31 = f32[22,256,256]{2,0,1:T(8,128)} copy(f32[22,256,256]{1,2,0:T(8,128)} %fusion.19) | data formatting | bytes 11534336 | tf_op jit(solution)/shard_map/mab,mbf->maf/dot_general | solution.py:20
  258.6 1.9 gather_fusion
  260.4 5.4 %fusion.13 = f32[22,256,256]{1,2,0:T(8,128)} fusion(bf16[1,4,22,256,256]{4,3,2,1,0:T(8,128)(2,1)} %bitcast.101, bf16[22,256,256]{2,1,0:T(8,128)(2,1)S(1)} %gather_fusion, pred[22]{0:T(512)(128)(4,1)S(1)} %get-tuple-element.26), kind=kOutput, calls=%fused_computation.22 | convolution fusion | flops 739639296 | bytes 11534358 | tf_op jit(solution)/shard_map/mab,mbf->maf/dot_general | solution.py:20
  265.9 6.6 %copy.27 = f32[22,256,256]{2,0,1:T(8,128)} copy(f32[22,256,256]{1,2,0:T(8,128)} %fusion.13) | data formatting | bytes 11534336 | tf_op jit(solution)/shard_map/mab,mbf->maf/dot_general | solution.py:20
  272.4 1.9 gather_fusion.1
  274.3 5.4 %fusion.16 = f32[22,256,256]{1,2,0:T(8,128)} fusion(bf16[1,4,22,256,256]{4,3,2,1,0:T(8,128)(2,1)} %bitcast.102, bf16[22,256,256]{2,1,0:T(8,128)(2,1)S(1)} %gather_fusion.1, pred[22]{0:T(512)(128)(4,1)S(1)} %get-tuple-element.28), kind=kOutput, calls=%fused_computation.23 | convolution fusion | flops 739639296 | bytes 11534358 | tf_op jit(solution)/shard_map/mab,mbf->maf/dot_general | solution.py:20
  279.6 6.7 %copy.29 = f32[22,256,256]{2,0,1:T(8,128)} copy(f32[22,256,256]{1,2,0:T(8,128)} %fusion.16) | data formatting | bytes 11534336 | tf_op jit(solution)/shard_map/mab,mbf->maf/dot_general | solution.py:20
  286.3 1.9 gather_fusion.3
  288.2 5.4 %fusion.22 = f32[22,256,256]{1,2,0:T(8,128)} fusion(bf16[1,4,22,256,256]{4,3,2,1,0:T(8,128)(2,1)} %bitcast.103, bf16[22,256,256]{2,1,0:T(8,128)(2,1)S(1)} %gather_fusion.3, pred[22]{0:T(512)(128)(4,1)S(1)} %get-tuple-element.10), kind=kOutput, calls=%fused_computation.25 | convolution fusion | flops 739639296 | bytes 11534358 | tf_op jit(solution)/shard_map/mab,mbf->maf/dot_general | solution.py:20
  293.5 6.5 %copy.33 = f32[22,256,256]{2,0,1:T(8,128)} copy(f32[22,256,256]{1,2,0:T(8,128)} %fusion.22) | data formatting | bytes 11534336 | tf_op jit(solution)/shard_map/mab,mbf->maf/dot_general | solution.py:20
  300.1 5.6 %fusion.34 = f32[6,256,256]{2,0,1:T(8,128)S(1)} fusion(f32[22,256,256]{2,0,1:T(8,128)} %copy.31, f32[22]{0:T(128)S(1)} %compare_convert_fusion.1, s32[22]{0:T(128)S(1)} %get-tuple-element.23), kind=kOutput, calls=%fused_computation.46 | convolution fusion | flops 103809288 | bytes 7340208 | tf_op jit(solution)/shard_map/mk,maf->kaf/dot_general | solution.py:25
  305.7 5.8 %fusion.38 = f32[6,256,256]{2,0,1:T(8,128)S(1)} fusion(f32[22,256,256]{2,0,1:T(8,128)} %copy.27, f32[22]{0:T(128)S(1)} %compare_convert_fusion.3, s32[22]{0:T(128)S(1)} %get-tuple-element.25), kind=kOutput, calls=%fused_computation.50 | convolution fusion | flops 103809288 | bytes 7340208 | tf_op jit(solution)/shard_map/mk,maf->kaf/dot_general | solution.py:25
  311.5 3.1 fusion.36
  314.6 3.2 add_add_fusion
  317.9 1.6 copy.34
  319.6 33.4 %all-reduce.4.cloned.1.call-done = f32[1536,256]{1,0:T(8,128)} async-done(((f32[1536,256]{1,0:T(8,128)}), f32[1536,256]{1,0:T(8,128)}) %all-reduce.4.cloned.1.call-update) | async-done | bytes 1572880 | tf_op jit(solution)/shard_map/psum | solution.py:55
  352.9 2.7 fusion.12
  (25 shorter events, 0.1 us)
Async XLA Ops:
  6.5 346.4 %copy-start = (bf16[256,256]{1,0:T(8,128)(2,1)S(1)}, bf16[256,256]{1,0:T(8,128)(2,1)}, u32[]{:S(2)}) copy-start(bf16[256,256]{1,0:T(8,128)(2,1)} %param.10) | copy-start | bytes 393220
  6.5 238.2 %all-reduce.6.cloned.1.call-start = ((), (), s32[]{:S(2)}) async-start(), calls=%async_computation.2 | async-start | bytes 6291456 | tf_op jit(solution)/shard_map/psum | solution.py:9
  10.5 342.5 %all-reduce.4.cloned.1.call-start = ((), (), s32[]{:S(2)}) async-start(), calls=%async_computation.1 | async-start | bytes 3145728 | tf_op jit(solution)/shard_map/psum | solution.py:55
  28.2 5.1 %copy-start.3 = (s32[1,8]{1,0:T(1,128)S(1)}, s32[1,8]{1,0:T(1,128)}, u32[]{:S(2)}) copy-start(s32[1,8]{1,0:T(1,128)} %param.13) | copy-start | bytes 100
  28.2 8.4 %copy-start.2 = (s32[1,8,22]{2,1,0:T(8,128)S(1)}, s32[1,8,22]{2,1,0:T(8,128)}, u32[]{:S(2)}) copy-start(s32[1,8,22]{2,1,0:T(8,128)} %param.12) | copy-start | bytes 2116
  300.1 11.4 %slice-start = ((s8[6291456]{0:T(1024)(128)(4,1)}), s8[4194304]{0:T(1024)(128)(4,1)S(1)}, s32[]{:S(2)}) async-start(s8[6291456]{0:T(1024)(128)(4,1)} %bitcast.104), calls=%async_computation.3 | async-start | bytes 8388608
  305.6 5.8 %slice-start.1 = ((s8[6291456]{0:T(1024)(128)(4,1)}), s8[2097152]{0:T(1024)(128)(4,1)S(1)}, s32[]{:S(2)}) async-start(s8[6291456]{0:T(1024)(128)(4,1)} %bitcast.104), calls=%async_computation.4 | async-start | bytes 4194304
  305.7 9.0 %slice-start.2 = ((s8[6291456]{0:T(1024)(128)(4,1)}), s8[4194304]{0:T(1024)(128)(4,1)S(1)}, s32[]{:S(2)}) async-start(s8[6291456]{0:T(1024)(128)(4,1)} %bitcast.106), calls=%async_computation.5 | async-start | bytes 8388608
  311.5 3.2 slice-start.3
  317.9 35.0 %copy-start.1 = (bf16[1536,256]{1,0:T(8,128)(2,1)S(1)}, bf16[1536,256]{1,0:T(8,128)(2,1)}, u32[]{:S(2)}) copy-start(bf16[1536,256]{1,0:T(8,128)(2,1)} %param.8) | copy-start | bytes 2359300
Sparse Core Ops, SparseCore 0:
  13.1 231.6 all-reduce.5
  319.7 33.2 all-reduce.3
where the time goes:
time: 364 us; the launch traced here: 363 us
  waiting for transfers between devices  242 us (66%)
  matrix products  42 us (12%)
  local copies, waits for them, and re-layouts  41.2 us (11%)
  blocking collectives  17.7 us (5%)
  between operations  13.6 us (4%)
  other arithmetic  6.5 us (2%)
    psum x1, waiting for transfers between devices, from_root(): return lax.psum(jnp.where(mine, x, jnp.zeros_like(x)), axis)  208 us
    psum x1, waiting for transfers between devices, on_device(): summed = lax.psum(flat, 'rep')  33.4 us
    dot_general x4, local copies, waits for them, and re-layouts, add_block(): jnp.einsum('mab,mbf->maf', tiles, pieces, preferred_element_type=jnp.floa...  26.3 us
    dot_general x4, matrix products, add_block(): jnp.einsum('mab,mbf->maf', tiles, pieces, preferred_element_type=jnp.floa...  21.5 us
    dot_general x4, matrix products, add_block(): jnp.einsum('mk,maf->kaf', target, product, precision=lax.Precision.HIGHEST)  17.7 us
    all_to_all x1, blocking collectives, on_device(): lax.all_to_all(tile_values, 'rep', split_axis=1, concat_axis=2, tiled=True)  17.7 us
    gather x4, local copies, waits for them, and re-layouts, add_block(): pieces = jnp.take(stacked, places % side, axis=0)  7.45 us
  transfers between devices with their start and end apart: 2, of which 2 were waited for; matrix products, arithmetic and copies ran while one was open for 2% of the time, Pallas kernels for 0%

commit v1 on v0

v1 whole, which is shorter than its diff:
```python
import functools
import itertools

import jax
import jax.numpy as jnp
import numpy as np
from jax import lax
from jax.experimental import pallas as pl
from jax.experimental.pallas import tpu as pltpu
from jax.sharding import PartitionSpec as P

NZ, NX, NY, CORES = 8, 4, 4, 2
COLORS = 4
AXES = ("rows", "rep")
CHIPS = list(itertools.product(range(NZ), range(NX), range(NY)))
FIRST_HEIGHTS = (0, 2, 5, 7)


def flat(z, x, y, core):
    return ((z % NZ * NX + x % NX) * NY + y % NY) * CORES + core


def color_of(z, x, y):
    return (z + 2 * x - y) % COLORS


def place_of(color, height, x):
    return (height + color) % NZ, x % NX, (height + 2 * x) % NY


def plan():
    scatter = [[] for _ in range(3)]
    spread = [[] for _ in range(3)]
    gather = [[] for _ in range(7)]
    trade = [[] for _ in range(3)]
    for color, core in itertools.product(range(COLORS), range(CORES)):
        at = lambda height, x: flat(*place_of(color, height, x), core)
        for base in (0, 4):
            for i in range(1, 4):
                scatter[i - 1].append((at(base, 0), at(base, i)))
            for x in range(NX):
                for i, height in enumerate(FIRST_HEIGHTS[1:]):
                    spread[i].append((at(base, x), at(base + height, x)))
        for height, x in itertools.product(range(NZ), range(NX)):
            for i in range(1, 8):
                other = height ^ (i // 4)
                gather[i - 1].append((at(other, x + i % 4), at(height, x)))
    for z, x, y in CHIPS:
        for core in range(CORES):
            s = 1 if core == 0 else -1
            for i, (dz, dx, dy) in enumerate(((1, 0, 0), (0, 1, 0), (0, 0, 1))):
                trade[i].append((flat(z, x, y, core), flat(z + s * dz, x + s * dx, y + s * dy, core)))
    return scatter, spread, gather, trade


def facts():
    rows = []
    for z, x, y in CHIPS:
        color = color_of(z, x, y)
        height = (z - color) % NZ
        slot = lambda h, i: (0 if h % NZ in FIRST_HEIGHTS else 4) + i % NX
        for core in range(CORES):
            s = 1 if core == 0 else -1
            row = [int(x == 0 and y == 0)]
            row += [slot(height ^ (i // 4), x + i % 4) for i in range(8)]
            row += [color, (color - s) % COLORS, (color - 2 * s) % COLORS, (color + s) % COLORS]
            rows.append(row)
    return np.array(rows, np.int32)


def assemble_kernel(slots, *refs):
    *pieces, out = refs
    size = pieces[0].shape[0]
    for i, piece in enumerate(pieces):
        out[pl.ds(pl.multiple_of(slots[i] * size, size), size), :] = piece[...]


def multiply_kernel(first, last, which, table, own, peer, payload, *refs):
    if last:
        inverse, features, *refs = refs
    if first:
        out, *refs = refs
        acc = out
    elif last:
        before, out, *refs = refs
        acc = refs.pop(0)
    else:
        before, out, *refs = refs
        acc = out
    buffer, sems = refs
    blocks = own.shape[0]
    half = own.shape[1]
    tile = own.shape[2]
    height = payload.shape[0] // 2
    copies = []
    for i in range(2):
        block = which[0] + i * COLORS
        for j, source in enumerate((own, peer)):
            copy = pltpu.make_async_copy(source.at[block], buffer.at[i, j], sems.at[i, j])
            copy.start()
            copies.append((i, j, block, copy))
    acc[...] = jnp.zeros_like(acc) if first else before[...]
    for i, j, block, copy in copies:
        copy.wait()
        for k in range(half):
            entry = (block * 2 + j) * half + k
            row = pl.multiple_of(table[entry], tile)
            column = pl.multiple_of(table[2 * blocks * half + entry] + i * height, tile)
            acc[pl.ds(row, tile), :] += jnp.dot(
                buffer[i, j, k], payload[pl.ds(column, tile), :], preferred_element_type=jnp.float32
            )
    if last:
        total = acc[pl.ds(0, height), :]
        out[...] = (total * inverse[...] + features[...].astype(jnp.float32)).astype(out.dtype)


def multiply(which, table, own, peer, payload, before=None, inverse=None, features=None):
    first, last = before is None, inverse is not None
    blocks, half, tile, _ = own.shape
    height, width = payload.shape[0] // 2, payload.shape[1]
    acc = jax.ShapeDtypeStruct((height + tile, width), jnp.float32)
    vmem = pl.BlockSpec(memory_space=pltpu.VMEM)
    smem = pl.BlockSpec(memory_space=pltpu.SMEM)
    hbm = pl.BlockSpec(memory_space=pl.ANY)
    args = [which, table, own, peer, payload]
    specs = [smem, smem, hbm, hbm, vmem]
    if last:
        args += [inverse, features]
        specs += [vmem, vmem]
    alias = {}
    if not first:
        args.append(before)
        specs.append(vmem)
        if not last:
            alias = {len(args) - 1: 0}
    scratch = [pltpu.VMEM(acc.shape, acc.dtype)] if last else []
    scratch += [pltpu.VMEM((2, 2, half, tile, tile), own.dtype), pltpu.SemaphoreType.DMA((2, 2))]
    return pl.pallas_call(
        functools.partial(multiply_kernel, first, last),
        out_shape=jax.ShapeDtypeStruct((height, width), payload.dtype) if last else acc,
        in_specs=specs,
        out_specs=vmem,
        scratch_shapes=scratch,
        input_output_aliases=alias,
        compiler_params=pltpu.CompilerParams(vmem_limit_bytes=24 * 2**20),
        cost_estimate=pl.CostEstimate(
            flops=4 * half * 2 * tile * tile * 256, bytes_accessed=4 * half * tile * tile * 2, transcendentals=0
        ),
    )(*args)


def finish_kernel(mine, other, mine_weight, other_weight, out):
    here = jnp.dot(mine[...], mine_weight[...], preferred_element_type=jnp.float32)
    there = jnp.dot(other[...], other_weight[...], preferred_element_type=jnp.float32)
    out[...] = jnp.maximum(here + there, 0.0).astype(out.dtype)


def on_device(features, degrees, weight, tile_values, tile_pos, live):
    scatter, spread, gather, trade = plan()
    swap = [(i, i ^ 1) for i in range(len(CHIPS) * CORES)]
    send = lambda x, pairs: lax.ppermute(x, AXES, pairs)
    height, full = features.shape
    width = full // CORES
    blocks, half, tile = tile_values.shape[1:4]
    side = height // tile
    core = lax.axis_index("rep")
    me = lax.axis_index("rows") * CORES + core
    fact = lax.dynamic_index_in_dim(jnp.asarray(facts()), me, 0, keepdims=False)

    own = tile_values[0]
    peer = send(own, swap)

    inverse = lax.rsqrt(degrees.astype(jnp.float32))
    mine = lax.dynamic_slice_in_dim(features, core * width, width, 1)
    scaled = (mine.astype(jnp.float32) * inverse[:, None]).astype(jnp.bfloat16)

    quarter = scaled.reshape(4, height // 4, width)
    piece = jnp.where(fact[0] == 1, quarter[0], jnp.zeros_like(quarter[0]))
    for got in [send(quarter[i + 1], pairs) for i, pairs in enumerate(scatter)]:
        piece = piece + got
    kept = piece
    for got in [send(kept, pairs) for pairs in spread]:
        piece = piece + got
    pieces = [piece] + [send(piece, pairs) for pairs in gather]
    vmem = pl.BlockSpec(memory_space=pltpu.VMEM)
    smem = pl.BlockSpec(memory_space=pltpu.SMEM)
    payload = pl.pallas_call(
        assemble_kernel,
        out_shape=jax.ShapeDtypeStruct((8 * height // 4, width), scaled.dtype),
        in_specs=[smem] + [vmem] * 8,
        out_specs=vmem,
    )(fact[1:9], *pieces)
    arrived = [payload] + [send(payload, pairs) for pairs in trade]

    used = jnp.arange(half * CORES)[None, :] < live[0][:, None]
    row = jnp.where(used, tile_pos[0] // side, side) * tile
    column = tile_pos[0] % side * tile
    both = jnp.stack([row, column]).reshape(2, blocks, CORES, half)
    table = jnp.where(core == 0, both, both[:, :, ::-1]).reshape(-1)
    spread_inverse = jnp.broadcast_to(inverse[:, None], (height, width))

    acc = multiply(fact[9:10], table, own, peer, arrived[0])
    for i in (1, 2):
        acc = multiply(fact[9 + i : 10 + i], table, own, peer, arrived[i], acc)
    combined = multiply(fact[12:13], table, own, peer, arrived[3], acc, spread_inverse, mine)

    other = send(combined, swap)
    mine_weight = lax.dynamic_slice_in_dim(weight, core * width, width, 0)
    other_weight = lax.dynamic_slice_in_dim(weight, (1 - core) * width, width, 0)
    return pl.pallas_call(
        finish_kernel,
        out_shape=jax.ShapeDtypeStruct((height, full), jnp.bfloat16),
        in_specs=[vmem] * 4,
        out_specs=vmem,
    )(combined, other, mine_weight, other_weight)


def solution(mesh):
    placed = (
        P("rows", None),
        P("rows"),
        P(),
        P("rows", None, "rep", None, None),
        P("rows", None, None),
        P("rows", None),
    )
    return jax.shard_map(on_device, mesh=mesh, in_specs=placed, out_specs=P("rows", None), check_vma=False)
```

time: 364 us -> 92.1 us (0.25)
  waiting for transfers between devices: 242 us -> 16.7 us
  matrix products: 42 us -> 0 us
  starting transfers between devices: 0.04 us -> 37.4 us
  local copies, waits for them, and re-layouts: 41.2 us -> 10.1 us
  Pallas kernels: 0 us -> 23.7 us
  blocking collectives: 17.7 us -> 0 us
  between operations: 13.6 us -> 0.94 us
  other arithmetic: 6.5 us -> 2.78 us
    psum x2 -> x0, waiting for transfers between devices: 241 us -> none  [the longest x1 208 us: from_root(): return lax.psum(jnp.where(mine, x, jnp.zeros_like(x)), axis)]
    dot_general x9 -> x0, matrix products: 42 us -> none  [the longest x4 21.5 us: add_block(): jnp.einsum('mab,mbf->maf', tiles, pieces, preferred_element_type=jnp.floa...]
    ppermute x0 -> x18, starting transfers between devices: none -> 37.4 us  [on_device(): send = lambda x, pairs: lax.ppermute(x, AXES, pairs)]
    dot_general x4 -> x0, local copies, waits for them, and re-layouts: 26.3 us -> none  [add_block(): jnp.einsum('mab,mbf->maf', tiles, pieces, preferred_element_type=jnp.floa...]
    pallas_call x0 -> x6, Pallas kernels: none -> 23.7 us  [the longest x4 19 us: multiply(): pl.pallas_call(functools.partial(multiply_kernel, first, last), out_shape...]
    all_to_all x1 -> x0, blocking collectives: 17.7 us -> none  [on_device(): lax.all_to_all(tile_values, 'rep', split_axis=1, concat_axis=2, tiled=True)]
    ppermute x0 -> x18, waiting for transfers between devices: none -> 16.7 us  [on_device(): send = lambda x, pairs: lax.ppermute(x, AXES, pairs)]
    gather x4 -> x0, local copies, waits for them, and re-layouts: 7.45 us -> none  [add_block(): pieces = jnp.take(stacked, places % side, axis=0)]
  transfers between devices with their start and end apart: 2 -> 18, of which waited for: 2 -> 7; matrix products, arithmetic and copies ran while one was open for 2% -> 6% of each run, Pallas kernels for 0% -> 18%
where the time goes in v1:
time: 92.1 us; the launch traced here: 91.5 us
  starting transfers between devices  37.4 us (41%)
  Pallas kernels  23.7 us (26%)
  waiting for transfers between devices  16.7 us (18%)
  local copies, waits for them, and re-layouts  10.1 us (11%)
  other arithmetic  2.78 us (3%)
  between operations  0.94 us (1%)
    ppermute x18, starting transfers between devices, on_device(): send = lambda x, pairs: lax.ppermute(x, AXES, pairs)  37.4 us
    pallas_call x4, Pallas kernels, multiply(): pl.pallas_call(functools.partial(multiply_kernel, first, last), out_shape...  19 us
    ppermute x18, waiting for transfers between devices, on_device(): send = lambda x, pairs: lax.ppermute(x, AXES, pairs)  16.7 us
    unnamed x29, local copies, waits for them, and re-layouts  6.84 us
    pallas_call x1, Pallas kernels, on_device(): pl.pallas_call(finish_kernel, out_shape=jax.ShapeDtypeStruct((height, ful...  2.55 us
    pallas_call x1, Pallas kernels, on_device(): pl.pallas_call(assemble_kernel, out_shape=jax.ShapeDtypeStruct((8 * heigh...  2.16 us
  transfers between devices with their start and end apart: 18, of which 7 were waited for; matrix products, arithmetic and copies ran while one was open for 6% of the time, Pallas kernels for 18%

profile of v1, /device:TPU:1, one launch (start us, length us, event | category | flops | bytes accessed | tf_op | source)
XLA Modules:
  0.0 91.5 jit_solution(13338537712682967543)
XLA Ops:
  0.0 3.2 %collective-permute-start = (bf16[8,11,256,256]{3,2,1,0:T(8,128)(2,1)}, bf16[8,11,256,256]{3,2,1,0:T(8,128)(2,1)}, u32[]{:S(2)}, u32[]{:S(2)}) collective-permute-start(bf16[8,11,256,256]{3,2,1,0:T(8,128)(2,1)} %bitcast.12), channel_id=1, source_target_pairs={{0,1},{1,0},{2,3},{3,2},{4,5},{5,4},{6,7},{7,6},{8,9},{9,8},{10,11... | collective-permute-start | bytes 34603016 | tf_op jit(solution)/shard_map/ppermute | solution.py:161
  3.2 0.7 convert_rsqrt_fusion
  3.9 1.3 %multiply_convert_fusion = (bf16[1536,128]{1,0:T(8,128)(2,1)S(1)}, bf16[1536,128]{1,0:T(8,128)(2,1)S(1)}) fusion(f32[1536]{0:T(1024)S(1)} %convert_rsqrt_fusion, bf16[1536,256]{1,0:T(8,128)(2,1)} %param.7, s32[]{:T(128)S(6)} %select_n.53), kind=kLoop, calls=%fused_computation | loop fusion | flops 589824 | bytes 1185796 | tf_op jit(solution)/shard_map/convert_element_type | solution.py:175
  5.2 4.0 %collective-permute-start.1 = (bf16[384,128]{1,0:T(8,128)(2,1)S(1)}, bf16[384,128]{1,0:T(8,128)(2,1)S(1)}, u32[]{:S(2)}, u32[]{:S(2)}) collective-permute-start(bf16[384,128]{1,0:T(8,128)(2,1)S(1)} %get-tuple-element.7), channel_id=1, source_target_pairs={{0,12},{128,140},{1,13},{129,141},{32,44},{160,172},{33,45},{161,1... | collective-permute-start | bytes 294920 | tf_op jit(solution)/shard_map/ppermute | solution.py:161
  9.3 1.3 %collective-permute-start.2 = (bf16[384,128]{1,0:T(8,128)(2,1)S(1)}, bf16[384,128]{1,0:T(8,128)(2,1)S(1)}, u32[]{:S(2)}, u32[]{:S(2)}) collective-permute-start(bf16[384,128]{1,0:T(8,128)(2,1)S(1)} %get-tuple-element.9), channel_id=1, source_target_pairs={{0,16},{128,144},{1,17},{129,145},{32,48},{160,176},{33,49},{161,1... | collective-permute-start | bytes 294920 | tf_op jit(solution)/shard_map/ppermute | solution.py:161
  10.6 1.3 %collective-permute-start.3 = (bf16[384,128]{1,0:T(8,128)(2,1)S(1)}, bf16[384,128]{1,0:T(8,128)(2,1)S(1)}, u32[]{:S(2)}, u32[]{:S(2)}) collective-permute-start(bf16[384,128]{1,0:T(8,128)(2,1)S(1)} %get-tuple-element.8), channel_id=1, source_target_pairs={{0,28},{128,156},{1,29},{129,157},{32,60},{160,188},{33,61},{161,1... | collective-permute-start | bytes 294920 | tf_op jit(solution)/shard_map/ppermute | solution.py:161
  11.9 0.7 constant_dynamic-slice_fusion.3
  14.1 1.3 %collective-permute-start.4 = (bf16[384,128]{1,0:T(8,128)(2,1)S(1)}, bf16[384,128]{1,0:T(8,128)(2,1)S(1)}, u32[]{:S(2)}, u32[]{:S(2)}) collective-permute-start(bf16[384,128]{1,0:T(8,128)(2,1)S(1)} %fusion.2), channel_id=1, source_target_pairs={{0,68},{12,72},{16,84},{28,88},{128,196},{140,200},{144,212},{156,... | collective-permute-start | bytes 294920 | tf_op jit(solution)/shard_map/ppermute | solution.py:161
  15.4 2.3 %collective-permute-start.5 = (bf16[384,128]{1,0:T(8,128)(2,1)S(1)}, bf16[384,128]{1,0:T(8,128)(2,1)S(1)}, u32[]{:S(2)}, u32[]{:S(2)}) collective-permute-start(bf16[384,128]{1,0:T(8,128)(2,1)S(1)} %fusion.2), channel_id=1, source_target_pairs={{0,162},{12,174},{16,178},{28,190},{128,34},{140,46},{144,50},{156... | collective-permute-start | bytes 294920 | tf_op jit(solution)/shard_map/ppermute | solution.py:161
  17.7 1.3 %collective-permute-start.6 = (bf16[384,128]{1,0:T(8,128)(2,1)S(1)}, bf16[384,128]{1,0:T(8,128)(2,1)S(1)}, u32[]{:S(2)}, u32[]{:S(2)}) collective-permute-start(bf16[384,128]{1,0:T(8,128)(2,1)S(1)} %fusion.2), channel_id=1, source_target_pairs={{0,230},{12,234},{16,246},{28,250},{128,102},{140,106},{144,118},{... | collective-permute-start | bytes 294920 | tf_op jit(solution)/shard_map/ppermute | solution.py:161
  19.0 3.1 %collective-permute-done.5 = bf16[384,128]{1,0:T(8,128)(2,1)S(1)} collective-permute-done((bf16[384,128]{1,0:T(8,128)(2,1)S(1)}, bf16[384,128]{1,0:T(8,128)(2,1)S(1)}, u32[]{:S(2)}, u32[]{:S(2)}) %collective-permute-start.5) | collective-permute-done | bytes 98336 | tf_op jit(solution)/shard_map/ppermute | solution.py:161
  22.1 3.7 %collective-permute-done.6 = bf16[384,128]{1,0:T(8,128)(2,1)S(1)} collective-permute-done((bf16[384,128]{1,0:T(8,128)(2,1)S(1)}, bf16[384,128]{1,0:T(8,128)(2,1)S(1)}, u32[]{:S(2)}, u32[]{:S(2)}) %collective-permute-start.6) | collective-permute-done | bytes 98336 | tf_op jit(solution)/shard_map/ppermute | solution.py:161
  25.9 4.1 %collective-permute-start.10 = (bf16[384,128]{1,0:T(8,128)(2,1)S(1)}, bf16[384,128]{1,0:T(8,128)(2,1)S(1)}, u32[]{:S(2)}, u32[]{:S(2)}) collective-permute-start(bf16[384,128]{1,0:T(8,128)(2,1)S(1)} %add_add_fusion.refs_0_), channel_id=1, source_target_pairs={{34,0},{46,12},{50,16},{62,28},{0,34},{12,46},{16,50},{28,62},{102... | collective-permute-start | bytes 294920 | tf_op jit(solution)/shard_map/ppermute | solution.py:161
  30.0 3.7 %collective-permute-start.11 = (bf16[384,128]{1,0:T(8,128)(2,1)S(1)}, bf16[384,128]{1,0:T(8,128)(2,1)S(1)}, u32[]{:S(2)}, u32[]{:S(2)}) collective-permute-start(bf16[384,128]{1,0:T(8,128)(2,1)S(1)} %add_add_fusion.refs_0_), channel_id=1, source_target_pairs={{46,0},{50,12},{62,16},{34,28},{12,34},{16,46},{28,50},{0,62},{106... | collective-permute-start | bytes 294920 | tf_op jit(solution)/shard_map/ppermute | solution.py:161
  33.7 2.5 %collective-permute-start.13 = (bf16[384,128]{1,0:T(8,128)(2,1)S(1)}, bf16[384,128]{1,0:T(8,128)(2,1)S(1)}, u32[]{:S(2)}, u32[]{:S(2)}) collective-permute-start(bf16[384,128]{1,0:T(8,128)(2,1)S(1)} %add_add_fusion.refs_0_), channel_id=1, source_target_pairs={{62,0},{34,12},{46,16},{50,28},{28,34},{0,46},{12,50},{16,62},{122... | collective-permute-start | bytes 294920 | tf_op jit(solution)/shard_map/ppermute | solution.py:161
  36.2 3.0 %collective-permute-start.7 = (bf16[384,128]{1,0:T(8,128)(2,1)S(1)}, bf16[384,128]{1,0:T(8,128)(2,1)S(1)}, u32[]{:S(2)}, u32[]{:S(2)}) collective-permute-start(bf16[384,128]{1,0:T(8,128)(2,1)S(1)} %add_add_fusion.refs_0_), channel_id=1, source_target_pairs={{12,0},{16,12},{28,16},{0,28},{46,34},{50,46},{62,50},{34,62},{72,... | collective-permute-start | bytes 294920 | tf_op jit(solution)/shard_map/ppermute | solution.py:161
  39.2 2.2 %collective-permute-start.8 = (bf16[384,128]{1,0:T(8,128)(2,1)S(1)}, bf16[384,128]{1,0:T(8,128)(2,1)S(1)}, u32[]{:S(2)}, u32[]{:S(2)}) collective-permute-start(bf16[384,128]{1,0:T(8,128)(2,1)S(1)} %add_add_fusion.refs_0_), channel_id=1, source_target_pairs={{16,0},{28,12},{0,16},{12,28},{50,34},{62,46},{34,50},{46,62},{84,... | collective-permute-start | bytes 294920 | tf_op jit(solution)/shard_map/ppermute | solution.py:161
  42.9 3.3 %collective-permute-done.8.refs_2_ = bf16[384,128]{1,0:T(8,128)(2,1)S(1)} collective-permute-done((bf16[384,128]{1,0:T(8,128)(2,1)S(1)}, bf16[384,128]{1,0:T(8,128)(2,1)S(1)}, u32[]{:S(2)}, u32[]{:S(2)}) %collective-permute-start.8) | collective-permute-done | bytes 98336 | tf_op jit(solution)/shard_map/ppermute | solution.py:161
  46.2 5.2 %collective-permute-done.9.refs_3_ = bf16[384,128]{1,0:T(8,128)(2,1)S(1)} collective-permute-done((bf16[384,128]{1,0:T(8,128)(2,1)S(1)}, bf16[384,128]{1,0:T(8,128)(2,1)S(1)}, u32[]{:S(2)}, u32[]{:S(2)}) %collective-permute-start.9) | collective-permute-done | bytes 98336 | tf_op jit(solution)/shard_map/ppermute | solution.py:161
  52.1 2.2 %shard_map.76.payload = bf16[3072,128]{1,0:T(8,128)(2,1)} custom-call(s32[8]{0:T(128)} %slice_bitcast_fusion.slots, bf16[384,128]{1,0:T(8,128)(2,1)} %copy-done.4, bf16[384,128]{1,0:T(8,128)(2,1)} %copy-done.11, bf16[384,128]{1,0:T(8,128)(2,1)} %copy-done.12, bf16[384,128]{1,0:T(8,128)(2,1)} %copy-done.13, bf16[384,128]{1,0:T(8,128)(2,1)} %copy-done.7, ...), custom_call_target="tpu_custom_call" | custom-call | tf_op jit(solution)/shard_map/pallas_call | solution.py:187
  54.2 1.3 %collective-permute-start.16 = (bf16[3072,128]{1,0:T(8,128)(2,1)}, bf16[3072,128]{1,0:T(8,128)(2,1)S(1)}, u32[]{:S(2)}, u32[]{:S(2)}) collective-permute-start(bf16[3072,128]{1,0:T(8,128)(2,1)} %shard_map.76.payload), channel_id=1, source_target_pairs={{0,32},{1,225},{2,34},{3,227},{4,36},{5,229},{6,38},{7,231},{8,40}... | collective-permute-start | bytes 2359304 | tf_op jit(solution)/shard_map/ppermute | solution.py:161
  55.5 0.8 fusion.5
  56.4 1.5 %collective-permute-start.14 = (bf16[3072,128]{1,0:T(8,128)(2,1)}, bf16[3072,128]{1,0:T(8,128)(2,1)S(1)}, u32[]{:S(2)}, u32[]{:S(2)}) collective-permute-start(bf16[3072,128]{1,0:T(8,128)(2,1)} %shard_map.76.payload), channel_id=1, source_target_pairs={{0,2},{1,7},{2,4},{3,1},{4,6},{5,3},{6,0},{7,5},{8,10},{9,15},{10,... | collective-permute-start | bytes 2359304 | tf_op jit(solution)/shard_map/ppermute | solution.py:161
  58.1 4.3 %copy-done = bf16[1,8,11,256,256]{4,3,2,1,0:T(8,128)(2,1)S(1)} copy-done((bf16[1,8,11,256,256]{4,3,2,1,0:T(8,128)(2,1)S(1)}, bf16[1,8,11,256,256]{4,3,2,1,0:T(8,128)(2,1)}, u32[]{:S(2)}) %copy-start) | copy-done | bytes 11534360
  62.4 1.1 %copy-done.2 = bf16[3072,128]{1,0:T(8,128)(2,1)S(1)} copy-done((bf16[3072,128]{1,0:T(8,128)(2,1)S(1)}, bf16[3072,128]{1,0:T(8,128)(2,1)}, u32[]{:S(2)}) %copy-start.2) | copy-done | bytes 786456
  63.5 5.1 %shard_map.77.refs_0_ = f32[1792,128]{1,0:T(8,128)S(1)} custom-call(s32[1]{0:T(128)} %bitcast.7.which, s32[352]{0:T(512)S(1)} %reshape.60.table, bf16[8,11,256,256]{3,2,1,0:T(8,128)(2,1)S(1)} %bitcast.13, bf16[8,11,256,256]{3,2,1,0:T(8,128)(2,1)} %collective-permute-done.peer, bf16[3072,128]{1,0:T(8,128)(2,1)S(1)} %copy-done.2), custom_call_target="tpu_custom_call" | custom-call | flops 1476395008 | bytes 5767168 | tf_op jit(solution)/shard_map/pallas_call | solution.py:138
  68.7 4.5 %shard_map.78.refs_0_ = f32[1792,128]{1,0:T(8,128)S(1)} custom-call(s32[1]{0:T(128)} %bitcast.6.which, s32[352]{0:T(512)S(1)} %reshape.60.table, bf16[8,11,256,256]{3,2,1,0:T(8,128)(2,1)S(1)} %bitcast.14, bf16[8,11,256,256]{3,2,1,0:T(8,128)(2,1)} %collective-permute-done.peer, ...), custom_call_target="tpu_custom_call", output_to_operand_aliasing={{}: (5, {})} | custom-call | flops 1476395008 | bytes 5767168 | tf_op jit(solution)/shard_map/pallas_call | solution.py:138
  73.2 4.6 %shard_map.79.refs_2_ = f32[1792,128]{1,0:T(8,128)S(1)} custom-call(s32[1]{0:T(128)} %bitcast.5.which, s32[352]{0:T(512)S(1)} %reshape.60.table, bf16[8,11,256,256]{3,2,1,0:T(8,128)(2,1)S(1)} %bitcast.15, bf16[8,11,256,256]{3,2,1,0:T(8,128)(2,1)} %collective-permute-done.peer, ...), custom_call_target="tpu_custom_call", output_to_operand_aliasing={{}: (5, {})} | custom-call | flops 1476395008 | bytes 5767168 | tf_op jit(solution)/shard_map/pallas_call | solution.py:138
  78.1 4.7 %shard_map.80.mine = bf16[1536,128]{1,0:T(8,128)(2,1)S(1)} custom-call(s32[1]{0:T(128)} %bitcast.which, s32[352]{0:T(512)S(1)} %reshape.60.table, bf16[8,11,256,256]{3,2,1,0:T(8,128)(2,1)S(1)} %bitcast.16, bf16[8,11,256,256]{3,2,1,0:T(8,128)(2,1)} %collective-permute-done.peer, bf16[3072,128]{1,0:T(8,128)(2,1)S(1)} %collective-permute-done.14.payload, ...), custom_call_target="tpu_custom_call" | custom-call | flops 1476395008 | bytes 5767168 | tf_op jit(solution)/shard_map/pallas_call | solution.py:138
  82.9 4.0 %collective-permute-start.17 = (bf16[1536,128]{1,0:T(8,128)(2,1)S(1)}, bf16[1536,128]{1,0:T(8,128)(2,1)S(1)}, u32[]{:S(2)}, u32[]{:S(2)}) collective-permute-start(bf16[1536,128]{1,0:T(8,128)(2,1)S(1)} %shard_map.80.mine), channel_id=1, source_target_pairs={{0,1},{1,0},{2,3},{3,2},{4,5},{5,4},{6,7},{7,6},{8,9},{9,8},{10,11... | collective-permute-start | bytes 1179656 | tf_op jit(solution)/shard_map/ppermute | solution.py:161
  88.2 0.7 copy-done.5
  88.9 2.5 %shard_map.81 = bf16[1536,256]{1,0:T(8,128)(2,1)} custom-call(bf16[1536,128]{1,0:T(8,128)(2,1)} %copy-done.3, bf16[1536,128]{1,0:T(8,128)(2,1)} %copy-done.5, bf16[128,256]{1,0:T(8,128)(2,1)} %get-tuple-element.11.mine_weight, bf16[128,256]{1,0:T(8,128)(2,1)} %get-tuple-element.10.other_weight), custom_call_target="tpu_custom_call" | custom-call | tf_op jit(solution)/shard_map/pallas_call | solution.py:210
  (56 shorter events, 5.1 us)
Async XLA Ops:
  0.0 58.1 %collective-permute-start = (bf16[8,11,256,256]{3,2,1,0:T(8,128)(2,1)}, bf16[8,11,256,256]{3,2,1,0:T(8,128)(2,1)}, u32[]{:S(2)}, u32[]{:S(2)}) collective-permute-start(bf16[8,11,256,256]{3,2,1,0:T(8,128)(2,1)} %bitcast.12), channel_id=1, source_target_pairs={{0,1},{1,0},{2,3},{3,2},{4,5},{5,4},{6,7},{7,6},{8,9},{9,8},{10,11... | collective-permute-start | bytes 34603016 | tf_op jit(solution)/shard_map/ppermute | solution.py:161
  5.2 8.7 %collective-permute-start.1 = (bf16[384,128]{1,0:T(8,128)(2,1)S(1)}, bf16[384,128]{1,0:T(8,128)(2,1)S(1)}, u32[]{:S(2)}, u32[]{:S(2)}) collective-permute-start(bf16[384,128]{1,0:T(8,128)(2,1)S(1)} %get-tuple-element.7), channel_id=1, source_target_pairs={{0,12},{128,140},{1,13},{129,141},{32,44},{160,172},{33,45},{161,1... | collective-permute-start | bytes 294920 | tf_op jit(solution)/shard_map/ppermute | solution.py:161
  9.3 4.6 %collective-permute-start.2 = (bf16[384,128]{1,0:T(8,128)(2,1)S(1)}, bf16[384,128]{1,0:T(8,128)(2,1)S(1)}, u32[]{:S(2)}, u32[]{:S(2)}) collective-permute-start(bf16[384,128]{1,0:T(8,128)(2,1)S(1)} %get-tuple-element.9), channel_id=1, source_target_pairs={{0,16},{128,144},{1,17},{129,145},{32,48},{160,176},{33,49},{161,1... | collective-permute-start | bytes 294920 | tf_op jit(solution)/shard_map/ppermute | solution.py:161
  10.6 3.5 %collective-permute-start.3 = (bf16[384,128]{1,0:T(8,128)(2,1)S(1)}, bf16[384,128]{1,0:T(8,128)(2,1)S(1)}, u32[]{:S(2)}, u32[]{:S(2)}) collective-permute-start(bf16[384,128]{1,0:T(8,128)(2,1)S(1)} %get-tuple-element.8), channel_id=1, source_target_pairs={{0,28},{128,156},{1,29},{129,157},{32,60},{160,188},{33,61},{161,1... | collective-permute-start | bytes 294920 | tf_op jit(solution)/shard_map/ppermute | solution.py:161
  14.1 4.9 %collective-permute-start.4 = (bf16[384,128]{1,0:T(8,128)(2,1)S(1)}, bf16[384,128]{1,0:T(8,128)(2,1)S(1)}, u32[]{:S(2)}, u32[]{:S(2)}) collective-permute-start(bf16[384,128]{1,0:T(8,128)(2,1)S(1)} %fusion.2), channel_id=1, source_target_pairs={{0,68},{12,72},{16,84},{28,88},{128,196},{140,200},{144,212},{156,... | collective-permute-start | bytes 294920 | tf_op jit(solution)/shard_map/ppermute | solution.py:161
  15.4 6.7 %collective-permute-start.5 = (bf16[384,128]{1,0:T(8,128)(2,1)S(1)}, bf16[384,128]{1,0:T(8,128)(2,1)S(1)}, u32[]{:S(2)}, u32[]{:S(2)}) collective-permute-start(bf16[384,128]{1,0:T(8,128)(2,1)S(1)} %fusion.2), channel_id=1, source_target_pairs={{0,162},{12,174},{16,178},{28,190},{128,34},{140,46},{144,50},{156... | collective-permute-start | bytes 294920 | tf_op jit(solution)/shard_map/ppermute | solution.py:161
  17.7 8.1 %collective-permute-start.6 = (bf16[384,128]{1,0:T(8,128)(2,1)S(1)}, bf16[384,128]{1,0:T(8,128)(2,1)S(1)}, u32[]{:S(2)}, u32[]{:S(2)}) collective-permute-start(bf16[384,128]{1,0:T(8,128)(2,1)S(1)} %fusion.2), channel_id=1, source_target_pairs={{0,230},{12,234},{16,246},{28,250},{128,102},{140,106},{144,118},{... | collective-permute-start | bytes 294920 | tf_op jit(solution)/shard_map/ppermute | solution.py:161
  25.8 25.5 %copy-start.4 = (bf16[384,128]{1,0:T(8,128)(2,1)}, bf16[384,128]{1,0:T(8,128)(2,1)S(1)}, u32[]{:S(2)}) copy-start(bf16[384,128]{1,0:T(8,128)(2,1)S(1)} %add_add_fusion.refs_0_) | copy-start | bytes 294916
  25.9 10.4 %collective-permute-start.10 = (bf16[384,128]{1,0:T(8,128)(2,1)S(1)}, bf16[384,128]{1,0:T(8,128)(2,1)S(1)}, u32[]{:S(2)}, u32[]{:S(2)}) collective-permute-start(bf16[384,128]{1,0:T(8,128)(2,1)S(1)} %add_add_fusion.refs_0_), channel_id=1, source_target_pairs={{34,0},{46,12},{50,16},{62,28},{0,34},{12,46},{16,50},{28,62},{102... | collective-permute-start | bytes 294920 | tf_op jit(solution)/shard_map/ppermute | solution.py:161
  30.0 9.2 %collective-permute-start.11 = (bf16[384,128]{1,0:T(8,128)(2,1)S(1)}, bf16[384,128]{1,0:T(8,128)(2,1)S(1)}, u32[]{:S(2)}, u32[]{:S(2)}) collective-permute-start(bf16[384,128]{1,0:T(8,128)(2,1)S(1)} %add_add_fusion.refs_0_), channel_id=1, source_target_pairs={{46,0},{50,12},{62,16},{34,28},{12,34},{16,46},{28,50},{0,62},{106... | collective-permute-start | bytes 294920 | tf_op jit(solution)/shard_map/ppermute | solution.py:161
  33.7 7.8 %collective-permute-start.12 = (bf16[384,128]{1,0:T(8,128)(2,1)S(1)}, bf16[384,128]{1,0:T(8,128)(2,1)S(1)}, u32[]{:S(2)}, u32[]{:S(2)}) collective-permute-start(bf16[384,128]{1,0:T(8,128)(2,1)S(1)} %add_add_fusion.refs_0_), channel_id=1, source_target_pairs={{50,0},{62,12},{34,16},{46,28},{16,34},{28,46},{0,50},{12,62},{118... | collective-permute-start | bytes 294920 | tf_op jit(solution)/shard_map/ppermute | solution.py:161
  33.7 9.2 %collective-permute-start.13 = (bf16[384,128]{1,0:T(8,128)(2,1)S(1)}, bf16[384,128]{1,0:T(8,128)(2,1)S(1)}, u32[]{:S(2)}, u32[]{:S(2)}) collective-permute-start(bf16[384,128]{1,0:T(8,128)(2,1)S(1)} %add_add_fusion.refs_0_), channel_id=1, source_target_pairs={{62,0},{34,12},{46,16},{50,28},{28,34},{0,46},{12,50},{16,62},{122... | collective-permute-start | bytes 294920 | tf_op jit(solution)/shard_map/ppermute | solution.py:161
  36.2 15.1 %copy-start.7 = (bf16[384,128]{1,0:T(8,128)(2,1)}, bf16[384,128]{1,0:T(8,128)(2,1)S(1)}, u32[]{:S(2)}) copy-start(bf16[384,128]{1,0:T(8,128)(2,1)S(1)} %collective-permute-done.10.refs_4_) | copy-start | bytes 294916
  36.2 6.7 %collective-permute-start.7 = (bf16[384,128]{1,0:T(8,128)(2,1)S(1)}, bf16[384,128]{1,0:T(8,128)(2,1)S(1)}, u32[]{:S(2)}, u32[]{:S(2)}) collective-permute-start(bf16[384,128]{1,0:T(8,128)(2,1)S(1)} %add_add_fusion.refs_0_), channel_id=1, source_target_pairs={{12,0},{16,12},{28,16},{0,28},{46,34},{50,46},{62,50},{34,62},{72,... | collective-permute-start | bytes 294920 | tf_op jit(solution)/shard_map/ppermute | solution.py:161
  39.2 12.1 %copy-start.8 = (bf16[384,128]{1,0:T(8,128)(2,1)}, bf16[384,128]{1,0:T(8,128)(2,1)S(1)}, u32[]{:S(2)}) copy-start(bf16[384,128]{1,0:T(8,128)(2,1)S(1)} %collective-permute-done.11.refs_5_) | copy-start | bytes 294916
  39.2 7.0 %collective-permute-start.8 = (bf16[384,128]{1,0:T(8,128)(2,1)S(1)}, bf16[384,128]{1,0:T(8,128)(2,1)S(1)}, u32[]{:S(2)}, u32[]{:S(2)}) collective-permute-start(bf16[384,128]{1,0:T(8,128)(2,1)S(1)} %add_add_fusion.refs_0_), channel_id=1, source_target_pairs={{16,0},{28,12},{0,16},{12,28},{50,34},{62,46},{34,50},{46,62},{84,... | collective-permute-start | bytes 294920 | tf_op jit(solution)/shard_map/ppermute | solution.py:161
  41.4 10.0 %copy-start.9 = (bf16[384,128]{1,0:T(8,128)(2,1)}, bf16[384,128]{1,0:T(8,128)(2,1)S(1)}, u32[]{:S(2)}) copy-start(bf16[384,128]{1,0:T(8,128)(2,1)S(1)} %collective-permute-done.12.refs_6_) | copy-start | bytes 294916
  41.4 10.0 %collective-permute-start.9 = (bf16[384,128]{1,0:T(8,128)(2,1)S(1)}, bf16[384,128]{1,0:T(8,128)(2,1)S(1)}, u32[]{:S(2)}, u32[]{:S(2)}) collective-permute-start(bf16[384,128]{1,0:T(8,128)(2,1)S(1)} %add_add_fusion.refs_0_), channel_id=1, source_target_pairs={{28,0},{0,12},{12,16},{16,28},{62,34},{34,46},{46,50},{50,62},{88,... | collective-permute-start | bytes 294920 | tf_op jit(solution)/shard_map/ppermute | solution.py:161
  42.9 8.5 %copy-start.10 = (bf16[384,128]{1,0:T(8,128)(2,1)}, bf16[384,128]{1,0:T(8,128)(2,1)S(1)}, u32[]{:S(2)}) copy-start(bf16[384,128]{1,0:T(8,128)(2,1)S(1)} %collective-permute-done.13.refs_7_) | copy-start | bytes 294916
  42.9 8.5 %copy-start.11 = (bf16[384,128]{1,0:T(8,128)(2,1)}, bf16[384,128]{1,0:T(8,128)(2,1)S(1)}, u32[]{:S(2)}) copy-start(bf16[384,128]{1,0:T(8,128)(2,1)S(1)} %collective-permute-done.7.refs_1_) | copy-start | bytes 294916
  46.2 5.2 %copy-start.12 = (bf16[384,128]{1,0:T(8,128)(2,1)}, bf16[384,128]{1,0:T(8,128)(2,1)S(1)}, u32[]{:S(2)}) copy-start(bf16[384,128]{1,0:T(8,128)(2,1)S(1)} %collective-permute-done.8.refs_2_) | copy-start | bytes 294916
  51.4 0.7 copy-start.13
  54.2 14.5 %collective-permute-start.16 = (bf16[3072,128]{1,0:T(8,128)(2,1)}, bf16[3072,128]{1,0:T(8,128)(2,1)S(1)}, u32[]{:S(2)}, u32[]{:S(2)}) collective-permute-start(bf16[3072,128]{1,0:T(8,128)(2,1)} %shard_map.76.payload), channel_id=1, source_target_pairs={{0,32},{1,225},{2,34},{3,227},{4,36},{5,229},{6,38},{7,231},{8,40}... | collective-permute-start | bytes 2359304 | tf_op jit(solution)/shard_map/ppermute | solution.py:161
  55.5 17.7 %collective-permute-start.15 = (bf16[3072,128]{1,0:T(8,128)(2,1)}, bf16[3072,128]{1,0:T(8,128)(2,1)S(1)}, u32[]{:S(2)}, u32[]{:S(2)}) collective-permute-start(bf16[3072,128]{1,0:T(8,128)(2,1)} %shard_map.76.payload), channel_id=1, source_target_pairs={{0,8},{1,25},{2,10},{3,27},{4,12},{5,29},{6,14},{7,31},{8,16},{9,1... | collective-permute-start | bytes 2359304 | tf_op jit(solution)/shard_map/ppermute | solution.py:161
  56.4 21.5 %collective-permute-start.14 = (bf16[3072,128]{1,0:T(8,128)(2,1)}, bf16[3072,128]{1,0:T(8,128)(2,1)S(1)}, u32[]{:S(2)}, u32[]{:S(2)}) collective-permute-start(bf16[3072,128]{1,0:T(8,128)(2,1)} %shard_map.76.payload), channel_id=1, source_target_pairs={{0,2},{1,7},{2,4},{3,1},{4,6},{5,3},{6,0},{7,5},{8,10},{9,15},{10,... | collective-permute-start | bytes 2359304 | tf_op jit(solution)/shard_map/ppermute | solution.py:161
  58.1 4.3 %copy-start = (bf16[1,8,11,256,256]{4,3,2,1,0:T(8,128)(2,1)S(1)}, bf16[1,8,11,256,256]{4,3,2,1,0:T(8,128)(2,1)}, u32[]{:S(2)}) copy-start(bf16[1,8,11,256,256]{4,3,2,1,0:T(8,128)(2,1)} %param.10) | copy-start | bytes 34603012
  62.4 1.1 %copy-start.2 = (bf16[3072,128]{1,0:T(8,128)(2,1)S(1)}, bf16[3072,128]{1,0:T(8,128)(2,1)}, u32[]{:S(2)}) copy-start(bf16[3072,128]{1,0:T(8,128)(2,1)} %shard_map.76.payload) | copy-start | bytes 2359300
  63.5 5.1 %copy-start.1 = (bf16[1,8,11,256,256]{4,3,2,1,0:T(8,128)(2,1)S(1)}, bf16[1,8,11,256,256]{4,3,2,1,0:T(8,128)(2,1)}, u32[]{:S(2)}) copy-start(bf16[1,8,11,256,256]{4,3,2,1,0:T(8,128)(2,1)} %param.10) | copy-start | bytes 34603012
  78.1 8.7 %copy-start.6 = (bf16[256,256]{1,0:T(8,128)(2,1)S(1)}, bf16[256,256]{1,0:T(8,128)(2,1)}, u32[]{:S(2)}) copy-start(bf16[256,256]{1,0:T(8,128)(2,1)} %param.9) | copy-start | bytes 393220
  82.8 5.3 %copy-start.3 = (bf16[1536,128]{1,0:T(8,128)(2,1)}, bf16[1536,128]{1,0:T(8,128)(2,1)S(1)}, u32[]{:S(2)}) copy-start(bf16[1536,128]{1,0:T(8,128)(2,1)S(1)} %shard_map.80.mine) | copy-start | bytes 1179652
  82.9 5.3 %collective-permute-start.17 = (bf16[1536,128]{1,0:T(8,128)(2,1)S(1)}, bf16[1536,128]{1,0:T(8,128)(2,1)S(1)}, u32[]{:S(2)}, u32[]{:S(2)}) collective-permute-start(bf16[1536,128]{1,0:T(8,128)(2,1)S(1)} %shard_map.80.mine), channel_id=1, source_target_pairs={{0,1},{1,0},{2,3},{3,2},{4,5},{5,4},{6,7},{7,6},{8,9},{9,8},{10,11... | collective-permute-start | bytes 1179656 | tf_op jit(solution)/shard_map/ppermute | solution.py:161
  88.2 0.7 copy-start.5

commit v2 on v0

v2 whole, which is shorter than its diff:
```python
import functools
import itertools

import jax
import jax.numpy as jnp
import numpy as np
from jax import lax
from jax.experimental import pallas as pl
from jax.experimental.pallas import tpu as pltpu
from jax.sharding import PartitionSpec as P

NZ, NX, NY, CORES = 8, 4, 4, 2
AXES = ("rows", "rep")
CHIPS = list(itertools.product(range(NZ), range(NX), range(NY)))
COLORS = 4
FIRST_PIECE = ((0, 0), (0, 3), (2, 0), (2, 3), (5, 0), (5, 3), (7, 0), (7, 3))
SECOND_PIECE = ((1, 1), (0, 2), (2, 1), (2, 2), (4, 1), (5, 2), (7, 1), (7, 2))
SEEDS = ((7, 0), (0, 2), (1, 1))
CHILDREN = {
    (0, 0): ((2, 3), (7, 3), (0, 3)),
    (7, 0): ((5, 3), (5, 0), (2, 0)),
    (0, 2): ((7, 2), (2, 1), (5, 2)),
    (1, 1): ((7, 1), (4, 1), (2, 2)),
}


def flat(z, x, y, core):
    return ((z % NZ * NX + x % NX) * NY + y % NY) * CORES + core


def color_of(z, x, y, core):
    return (z + 2 * x - y if core == 0 else z + 2 * y - x) % COLORS


def chip_at(color, height, across, core):
    other = height % NZ + 2 * across
    return ((color + height) % NZ, across, other) if core == 0 else ((color + height) % NZ, other, across)


def slot_of(height, across):
    for base in (0, 4):
        place = ((height - base) % NZ, across)
        for piece, places in enumerate((FIRST_PIECE, SECOND_PIECE)):
            if place in places:
                return base // 2 + piece


def plan():
    scatter, spread, gather, trade = ([[] for _ in range(3)] for _ in range(4))
    for color, core in itertools.product(range(COLORS), range(CORES)):
        at = lambda height, across: flat(*chip_at(color, height, across, core), core)
        for base in (0, 4):
            for i, (height, across) in enumerate(SEEDS):
                scatter[i].append((at(base, 0), at(base + height, across)))
            for (height, across), places in CHILDREN.items():
                for i, (h, a) in enumerate(places):
                    spread[i].append((at(base + height, across), at(base + h, a)))
        for height, across in itertools.product(range(NZ), range(NX)):
            for i in range(1, 4):
                gather[i - 1].append((at(height ^ (i & 1), across ^ (i >> 1)), at(height, across)))
    for z, x, y in CHIPS:
        for core, s in ((0, 1), (1, -1)):
            for i, (dz, dx, dy) in enumerate(((1, 0, 0), (0, 1, 0), (0, 0, 1))):
                trade[i].append((flat(z, x, y, core), flat(z + s * dz, x + s * dx, y + s * dy, core)))
    return scatter, spread, gather, trade


def facts():
    rows = []
    for z, x, y in CHIPS:
        for core, s in ((0, 1), (1, -1)):
            color = color_of(z, x, y, core)
            height, across = (z - color) % NZ, (x, y)[core]
            row = [int(x == 0 and y == 0)]
            row += [slot_of(height ^ (i & 1), across ^ (i >> 1)) for i in range(4)]
            sent = [color_of(z - s, x, y, core), color_of(z, x - s, y, core), color_of(z, x, y - s, core)]
            row += [color, color + COLORS] + sent + [c + COLORS for c in sent]
            rows.append(row)
    return np.array(rows, np.int32)


VMEM = pl.BlockSpec(memory_space=pltpu.VMEM)
SMEM = pl.BlockSpec(memory_space=pltpu.SMEM)
HBM = pl.BlockSpec(memory_space=pltpu.HBM)


def assemble_kernel(slots, *refs):
    *pieces, first, second = refs
    size = pieces[0].shape[0]
    for i, piece in enumerate(pieces):
        place = pl.ds(pl.multiple_of(slots[i] % 2 * size, size), size)

        @pl.when(slots[i] < 2)
        def _():
            first[place, :] = piece[...]

        @pl.when(slots[i] >= 2)
        def _():
            second[place, :] = piece[...]


def prepare_kernel(order, table, own, peer, *refs):
    *mats, done, sems = refs
    blocks, half, tile = own.shape[:3]
    slots = CORES * half

    def place(j, k, act):
        entry = order[j] * slots + k
        row, column = table[entry], table[blocks * slots + entry]

        @pl.when(row >= 0)
        def _():
            target = mats[j].at[pl.ds(pl.multiple_of(row, tile), tile), pl.ds(pl.multiple_of(column, tile), tile)]
            act(pltpu.make_async_copy((own if k < half else peer).at[order[j], k % half], target, sems.at[j]))

    for j in range(blocks):
        mats[j][...] = jnp.zeros(mats[j].shape, mats[j].dtype)
        for k in range(slots):
            place(j, k, lambda copy: copy.start())
    for j in range(blocks):
        for k in range(slots):
            place(j, k, lambda copy: copy.wait())
    done[...] = jnp.zeros_like(done)


def multiply_kernel(first, last, mat, source, *refs):
    product = jnp.dot(mat[...], source[...], preferred_element_type=jnp.float32)
    if not first:
        before, *refs = refs
        product = before[...] + product
    if last:
        inverse, features, out = refs
        out[...] = (product * inverse[...] + features[...].astype(jnp.float32)).astype(out.dtype)
    else:
        refs[0][...] = product


def multiply(mat, source, before=None, extra=()):
    first, last = before is None, bool(extra)
    args = [mat, source] + ([] if first else [before]) + list(extra)
    return pl.pallas_call(
        functools.partial(multiply_kernel, first, last),
        out_shape=jax.ShapeDtypeStruct(source.shape, source.dtype if last else jnp.float32),
        in_specs=[VMEM] * len(args),
        out_specs=VMEM,
        input_output_aliases={} if first or last else {2: 0},
        compiler_params=pltpu.CompilerParams(vmem_limit_bytes=6 * 2**20),
        cost_estimate=pl.CostEstimate(
            flops=4 * mat.size * source.shape[1], bytes_accessed=mat.size * 2, transcendentals=0
        ),
    )(*args)


def finish_kernel(mine, other, mine_weight, other_weight, out):
    here = jnp.dot(mine[...], mine_weight[...], preferred_element_type=jnp.float32)
    there = jnp.dot(other[...], other_weight[...], preferred_element_type=jnp.float32)
    out[...] = jnp.maximum(here + there, 0.0).astype(out.dtype)


def on_device(features, degrees, weight, tile_values, tile_pos, live):
    scatter, spread, gather, trade = plan()
    swap = [(i, i ^ 1) for i in range(len(CHIPS) * CORES)]
    send = lambda x, pairs: lax.ppermute(x, AXES, pairs)
    height, full = features.shape
    width = full // CORES
    blocks, half, tile = tile_values.shape[1:4]
    side = height // tile
    core = lax.axis_index("rep")
    me = lax.axis_index("rows") * CORES + core
    fact = lax.dynamic_index_in_dim(jnp.asarray(facts()), me, 0, keepdims=False)
    order = fact[5:]

    own = tile_values[0]
    peer = send(own, swap)

    inverse = lax.rsqrt(degrees.astype(jnp.float32))
    mine = lax.dynamic_slice_in_dim(features, core * width, width, 1)
    scaled = (mine.astype(jnp.float32) * inverse[:, None]).astype(jnp.bfloat16)

    used = jnp.arange(half * CORES)[None, :] < live[0][:, None]
    row = jnp.where(used, tile_pos[0] // side * tile, -1)
    column = tile_pos[0] % side * tile
    both = jnp.stack([row, column]).reshape(2, blocks, CORES, half)
    table = jnp.where(core == 0, both, both[:, :, ::-1]).reshape(-1)

    cut = scaled.reshape(2, height // 2, width)
    piece = jnp.where(fact[0] == 1, cut[0], jnp.zeros_like(cut[0]))
    for got in [send(cut[min(i, 1)], pairs) for i, pairs in enumerate(scatter)]:
        piece = piece + got
    kept = piece
    table, kept = lax.optimization_barrier((table, kept))
    matrix = jax.ShapeDtypeStruct((height, height), own.dtype)
    *mats, done = pl.pallas_call(
        prepare_kernel,
        out_shape=[matrix] * blocks + [jax.ShapeDtypeStruct((16, width), own.dtype)],
        in_specs=[SMEM, SMEM, HBM, HBM],
        out_specs=[VMEM] * (blocks + 1),
        scratch_shapes=[pltpu.SemaphoreType.DMA((blocks,))],
        compiler_params=pltpu.CompilerParams(vmem_limit_bytes=42 * 2**20),
        cost_estimate=pl.CostEstimate(flops=0, bytes_accessed=4 * own.size * 2, transcendentals=0),
    )(order, table, own, peer)
    for got in [send(kept, pairs) for pairs in spread]:
        piece = piece + got
    piece = piece + done[:1]
    pieces = [piece] + [send(piece, pairs) for pairs in gather]
    half_block = jax.ShapeDtypeStruct((height, width), scaled.dtype)
    first, second = pl.pallas_call(
        assemble_kernel,
        out_shape=(half_block, half_block),
        in_specs=[SMEM] + [VMEM] * 4,
        out_specs=(VMEM, VMEM),
        compiler_params=pltpu.CompilerParams(vmem_limit_bytes=4 * 2**20),
    )(fact[1:5], *pieces)
    arrived = [send(block, pairs) for block in (first, second) for pairs in trade]

    spread_inverse = jnp.broadcast_to(inverse[:, None], (height, width))
    total = None
    for i, source in enumerate([first, second] + arrived):
        total = multiply(mats[i], source, total, (spread_inverse, mine) if i == blocks - 1 else ())
    combined = total

    other = send(combined, swap)
    mine_weight = lax.dynamic_slice_in_dim(weight, core * width, width, 0)
    other_weight = lax.dynamic_slice_in_dim(weight, (1 - core) * width, width, 0)
    return pl.pallas_call(
        finish_kernel,
        out_shape=jax.ShapeDtypeStruct((height, full), jnp.bfloat16),
        in_specs=[VMEM] * 4,
        out_specs=VMEM,
        compiler_params=pltpu.CompilerParams(vmem_limit_bytes=6 * 2**20),
    )(combined, other, mine_weight, other_weight)


def solution(mesh):
    placed = (
        P("rows", None),
        P("rows"),
        P(),
        P("rows", None, "rep", None, None),
        P("rows", None, None),
        P("rows", None),
    )
    return jax.shard_map(on_device, mesh=mesh, in_specs=placed, out_specs=P("rows", None), check_vma=False)
```

time: 364 us -> 81 us (0.22)
  waiting for transfers between devices: 242 us -> 13.2 us
  matrix products: 42 us -> 0 us
  local copies, waits for them, and re-layouts: 41.2 us -> 1.52 us
  starting transfers between devices: 0.04 us -> 36.2 us
  Pallas kernels: 0 us -> 27.5 us
  blocking collectives: 17.7 us -> 0 us
  between operations: 13.6 us -> 0.52 us
  other arithmetic: 6.5 us -> 2.82 us
    psum x2 -> x0, waiting for transfers between devices: 241 us -> none  [the longest x1 208 us: from_root(): return lax.psum(jnp.where(mine, x, jnp.zeros_like(x)), axis)]
    dot_general x9 -> x0, matrix products: 42 us -> none  [the longest x4 21.5 us: add_block(): jnp.einsum('mab,mbf->maf', tiles, pieces, preferred_element_type=jnp.floa...]
    ppermute x0 -> x17, starting transfers between devices: none -> 36.2 us  [on_device(): send = lambda x, pairs: lax.ppermute(x, AXES, pairs)]
    pallas_call x0 -> x11, Pallas kernels: none -> 27.5 us  [the longest x1 14.1 us: on_device(): pl.pallas_call(prepare_kernel, out_shape=[matrix] * blocks + [jax.ShapeDt...]
    dot_general x4 -> x0, local copies, waits for them, and re-layouts: 26.3 us -> none  [add_block(): jnp.einsum('mab,mbf->maf', tiles, pieces, preferred_element_type=jnp.floa...]
    all_to_all x1 -> x0, blocking collectives: 17.7 us -> none  [on_device(): lax.all_to_all(tile_values, 'rep', split_axis=1, concat_axis=2, tiled=True)]
    ppermute x0 -> x17, waiting for transfers between devices: none -> 13.2 us  [on_device(): send = lambda x, pairs: lax.ppermute(x, AXES, pairs)]
    gather x4 -> x0, local copies, waits for them, and re-layouts: 7.45 us -> none  [add_block(): pieces = jnp.take(stacked, places % side, axis=0)]
  transfers between devices with their start and end apart: 2 -> 17, of which waited for: 2 -> 4; matrix products, arithmetic and copies ran while one was open for 2% -> 5% of each run, Pallas kernels for 0% -> 29%
where the time goes in v2:
time: 81 us; the launch traced here: 81.8 us
  starting transfers between devices  36.2 us (45%)
  Pallas kernels  27.5 us (34%)
  waiting for transfers between devices  13.2 us (16%)
  other arithmetic  2.82 us (3%)
  local copies, waits for them, and re-layouts  1.52 us (2%)
    ppermute x17, starting transfers between devices, on_device(): send = lambda x, pairs: lax.ppermute(x, AXES, pairs)  36.2 us
    pallas_call x1, Pallas kernels, on_device(): pl.pallas_call(prepare_kernel, out_shape=[matrix] * blocks + [jax.ShapeDt...  14.1 us
    ppermute x17, waiting for transfers between devices, on_device(): send = lambda x, pairs: lax.ppermute(x, AXES, pairs)  13.2 us
    pallas_call x8, Pallas kernels, multiply(): pl.pallas_call(functools.partial(multiply_kernel, first, last), out_shape...  11.3 us
  transfers between devices with their start and end apart: 17, of which 4 were waited for; matrix products, arithmetic and copies ran while one was open for 5% of the time, Pallas kernels for 29%

profile of v2, /device:TPU:1, one launch (start us, length us, event | category | flops | bytes accessed | tf_op | source)
XLA Modules:
  0.0 81.8 jit_solution(5063294284498982970)
XLA Ops:
  0.0 3.2 %collective-permute-start.3 = (bf16[8,11,256,256]{3,2,1,0:T(8,128)(2,1)}, bf16[8,11,256,256]{3,2,1,0:T(8,128)(2,1)}, u32[]{:S(2)}, u32[]{:S(2)}) collective-permute-start(bf16[8,11,256,256]{3,2,1,0:T(8,128)(2,1)} %bitcast.25), channel_id=1, source_target_pairs={{0,1},{1,0},{2,3},{3,2},{4,5},{5,4},{6,7},{7,6},{8,9},{9,8},{10,11... | collective-permute-start | bytes 34603016 | tf_op jit(solution)/shard_map/ppermute | solution.py:163
  3.2 0.7 convert_rsqrt_fusion
  3.9 1.3 %multiply_convert_fusion = (bf16[1536,128]{1,0:T(8,128)(2,1)S(1)}, bf16[1536,128]{1,0:T(8,128)(2,1)S(1)}) fusion(f32[1536]{0:T(1024)S(1)} %convert_rsqrt_fusion, bf16[1536,256]{1,0:T(8,128)(2,1)} %param.7, s32[]{:T(128)S(6)} %select_n.53), kind=kLoop, calls=%fused_computation | loop fusion | flops 589824 | bytes 1185796 | tf_op jit(solution)/shard_map/convert_element_type | solution.py:178
  5.2 3.1 %collective-permute-start.1 = (bf16[768,128]{1,0:T(8,128)(2,1)S(1)}, bf16[768,128]{1,0:T(8,128)(2,1)S(1)}, u32[]{:S(2)}, u32[]{:S(2)}) collective-permute-start(bf16[768,128]{1,0:T(8,128)(2,1)S(1)} %get-tuple-element.34), channel_id=1, source_target_pairs={{0,16},{128,144},{1,5},{129,133},{32,48},{160,176},{33,37},{161,16... | collective-permute-start | bytes 589832 | tf_op jit(solution)/shard_map/ppermute | solution.py:163
  8.4 2.6 %collective-permute-start.2 = (bf16[768,128]{1,0:T(8,128)(2,1)S(1)}, bf16[768,128]{1,0:T(8,128)(2,1)S(1)}, u32[]{:S(2)}, u32[]{:S(2)}) collective-permute-start(bf16[768,128]{1,0:T(8,128)(2,1)S(1)} %get-tuple-element.34), channel_id=1, source_target_pairs={{0,46},{128,174},{1,59},{129,187},{32,78},{160,206},{33,91},{161,2... | collective-permute-start | bytes 589832 | tf_op jit(solution)/shard_map/ppermute | solution.py:163
  11.0 3.6 %collective-permute-start = (bf16[768,128]{1,0:T(8,128)(2,1)S(1)}, bf16[768,128]{1,0:T(8,128)(2,1)S(1)}, u32[]{:S(2)}, u32[]{:S(2)}) collective-permute-start(bf16[768,128]{1,0:T(8,128)(2,1)S(1)} %get-tuple-element.33), channel_id=1, source_target_pairs={{0,230},{128,102},{1,249},{129,121},{32,6},{160,134},{33,25},{161,... | collective-permute-start | bytes 589832 | tf_op jit(solution)/shard_map/ppermute | solution.py:163
  14.6 0.8 fusion.2
  15.7 0.7 constant_dynamic-slice_fusion.3
  16.5 2.1 %collective-permute-done = bf16[768,128]{1,0:T(8,128)(2,1)S(1)} collective-permute-done((bf16[768,128]{1,0:T(8,128)(2,1)S(1)}, bf16[768,128]{1,0:T(8,128)(2,1)S(1)}, u32[]{:S(2)}, u32[]{:S(2)}) %collective-permute-start) | collective-permute-done | bytes 196640 | tf_op jit(solution)/shard_map/ppermute | solution.py:163
  18.6 1.3 %collective-permute-start.4 = (bf16[768,128]{1,0:T(8,128)(2,1)S(1)}, bf16[768,128]{1,0:T(8,128)(2,1)S(1)}, u32[]{:S(2)}, u32[]{:S(2)}) collective-permute-start(bf16[768,128]{1,0:T(8,128)(2,1)S(1)} %add_add_fusion.1), channel_id=1, source_target_pairs={{0,88},{230,190},{16,246},{46,234},{128,216},{102,62},{144,118},{1... | collective-permute-start | bytes 589832 | tf_op jit(solution)/shard_map/ppermute | solution.py:163
  19.9 1.3 %collective-permute-start.5 = (bf16[768,128]{1,0:T(8,128)(2,1)S(1)}, bf16[768,128]{1,0:T(8,128)(2,1)S(1)}, u32[]{:S(2)}, u32[]{:S(2)}) collective-permute-start(bf16[768,128]{1,0:T(8,128)(2,1)S(1)} %add_add_fusion.1), channel_id=1, source_target_pairs={{0,250},{230,162},{16,72},{46,140},{128,122},{102,34},{144,200},{1... | collective-permute-start | bytes 589832 | tf_op jit(solution)/shard_map/ppermute | solution.py:163
  21.2 1.3 %collective-permute-start.6 = (bf16[768,128]{1,0:T(8,128)(2,1)S(1)}, bf16[768,128]{1,0:T(8,128)(2,1)S(1)}, u32[]{:S(2)}, u32[]{:S(2)}) collective-permute-start(bf16[768,128]{1,0:T(8,128)(2,1)S(1)} %add_add_fusion.1), channel_id=1, source_target_pairs={{0,28},{230,68},{16,178},{46,84},{128,156},{102,196},{144,50},{174... | collective-permute-start | bytes 589832 | tf_op jit(solution)/shard_map/ppermute | solution.py:163
  22.6 14.1 %shard_map.76 = (bf16[1536,1536]{1,0:T(8,128)(2,1)S(1)}, bf16[1536,1536]{1,0:T(8,128)(2,1)S(1)}, bf16[1536,1536]{1,0:T(8,128)(2,1)}, bf16[1536,1536]{1,0:T(8,128...) custom-call(s32[8]{0:T(128)S(1)} %slice_bitcast_fusion.2.order, ...), custom_call_target="tpu_custom_call" | custom-call | bytes 46137344 | tf_op jit(solution)/shard_map/pallas_call | solution.py:193
  36.9 7.1 %collective-permute-start.8 = (bf16[768,128]{1,0:T(8,128)(2,1)S(1)}, bf16[768,128]{1,0:T(8,128)(2,1)S(1)}, u32[]{:S(2)}, u32[]{:S(2)}) collective-permute-start(bf16[768,128]{1,0:T(8,128)(2,1)S(1)} %add_add_fusion.refs_0_), channel_id=1, source_target_pairs={{12,0},{0,12},{28,16},{16,28},{46,34},{34,46},{62,50},{50,62},{72,... | collective-permute-start | bytes 589832 | tf_op jit(solution)/shard_map/ppermute | solution.py:163
  44.0 4.0 %collective-permute-done.8.refs_2_ = bf16[768,128]{1,0:T(8,128)(2,1)S(1)} collective-permute-done((bf16[768,128]{1,0:T(8,128)(2,1)S(1)}, bf16[768,128]{1,0:T(8,128)(2,1)S(1)}, u32[]{:S(2)}, u32[]{:S(2)}) %collective-permute-start.8) | collective-permute-done | bytes 196640 | tf_op jit(solution)/shard_map/ppermute | solution.py:163
  48.0 5.8 %collective-permute-done.9.refs_3_ = bf16[768,128]{1,0:T(8,128)(2,1)S(1)} collective-permute-done((bf16[768,128]{1,0:T(8,128)(2,1)S(1)}, bf16[768,128]{1,0:T(8,128)(2,1)S(1)}, u32[]{:S(2)}, u32[]{:S(2)}) %collective-permute-start.9) | collective-permute-done | bytes 196640 | tf_op jit(solution)/shard_map/ppermute | solution.py:163
  53.8 0.7 shard_map.77
  54.4 4.1 %collective-permute-start.15 = (bf16[1536,128]{1,0:T(8,128)(2,1)S(1)}, bf16[1536,128]{1,0:T(8,128)(2,1)S(1)}, u32[]{:S(2)}, u32[]{:S(2)}) collective-permute-start(bf16[1536,128]{1,0:T(8,128)(2,1)S(1)} %get-tuple-element.26.source), channel_id=1, source_target_pairs={{0,32},{1,225},{2,34},{3,227},{4,36},{5,229},{6,38},{7,231},{8,40}... | collective-permute-start | bytes 1179656 | tf_op jit(solution)/shard_map/ppermute | solution.py:163
  58.6 1.6 %collective-permute-start.14 = (bf16[1536,128]{1,0:T(8,128)(2,1)S(1)}, bf16[1536,128]{1,0:T(8,128)(2,1)S(1)}, u32[]{:S(2)}, u32[]{:S(2)}) collective-permute-start(bf16[1536,128]{1,0:T(8,128)(2,1)S(1)} %get-tuple-element.26.source), channel_id=1, source_target_pairs={{0,8},{1,25},{2,10},{3,27},{4,12},{5,29},{6,14},{7,31},{8,16},{9,1... | collective-permute-start | bytes 1179656 | tf_op jit(solution)/shard_map/ppermute | solution.py:163
  60.2 1.0 %collective-permute-start.13 = (bf16[1536,128]{1,0:T(8,128)(2,1)S(1)}, bf16[1536,128]{1,0:T(8,128)(2,1)S(1)}, u32[]{:S(2)}, u32[]{:S(2)}) collective-permute-start(bf16[1536,128]{1,0:T(8,128)(2,1)S(1)} %get-tuple-element.26.source), channel_id=1, source_target_pairs={{0,2},{1,7},{2,4},{3,1},{4,6},{5,3},{6,0},{7,5},{8,10},{9,15},{10,... | collective-permute-start | bytes 1179656 | tf_op jit(solution)/shard_map/ppermute | solution.py:163
  61.7 1.4 %shard_map.78.refs_0_ = f32[1536,128]{1,0:T(8,128)S(1)} custom-call(bf16[1536,1536]{1,0:T(8,128)(2,1)S(1)} %get-tuple-element.30.mat, bf16[1536,128]{1,0:T(8,128)(2,1)S(1)} %get-tuple-element.26.source), custom_call_target="tpu_custom_call" | custom-call | flops 1207959552 | bytes 4718592 | tf_op jit(solution)/shard_map/pallas_call | solution.py:141
  63.1 1.4 %shard_map.79.refs_0_ = f32[1536,128]{1,0:T(8,128)S(1)} custom-call(bf16[1536,1536]{1,0:T(8,128)(2,1)S(1)} %get-tuple-element.29.mat, bf16[1536,128]{1,0:T(8,128)(2,1)S(1)} %get-tuple-element.22.source, f32[1536,128]{1,0:T(8,128)S(1)} %shard_map.78.refs_0_), custom_call_target="tpu_custom_call", output_to_operand_aliasing={{}: (2, {})} | custom-call | flops 1207959552 | bytes 4718592 | tf_op jit(solution)/shard_map/pallas_call | solution.py:141
  64.6 2.5 %collective-permute-start.10 = (bf16[1536,128]{1,0:T(8,128)(2,1)S(1)}, bf16[1536,128]{1,0:T(8,128)(2,1)S(1)}, u32[]{:S(2)}, u32[]{:S(2)}) collective-permute-start(bf16[1536,128]{1,0:T(8,128)(2,1)S(1)} %get-tuple-element.22.source), channel_id=1, source_target_pairs={{0,2},{1,7},{2,4},{3,1},{4,6},{5,3},{6,0},{7,5},{8,10},{9,15},{10,... | collective-permute-start | bytes 1179656 | tf_op jit(solution)/shard_map/ppermute | solution.py:163
  67.1 1.4 %shard_map.80.refs_0_ = f32[1536,128]{1,0:T(8,128)S(1)} custom-call(bf16[1536,1536]{1,0:T(8,128)(2,1)S(1)} %bitcast.24, bf16[1536,128]{1,0:T(8,128)(2,1)S(1)} %collective-permute-done.15.source, f32[1536,128]{1,0:T(8,128)S(1)} %shard_map.79.refs_0_), custom_call_target="tpu_custom_call", output_to_operand_aliasing={{}: (2, {})} | custom-call | flops 1207959552 | bytes 4718592 | tf_op jit(solution)/shard_map/pallas_call | solution.py:141
  68.6 1.4 %shard_map.81.refs_0_ = f32[1536,128]{1,0:T(8,128)S(1)} custom-call(bf16[1536,1536]{1,0:T(8,128)(2,1)S(1)} %bitcast.22, bf16[1536,128]{1,0:T(8,128)(2,1)S(1)} %collective-permute-done.14.source, f32[1536,128]{1,0:T(8,128)S(1)} %shard_map.80.refs_0_), custom_call_target="tpu_custom_call", output_to_operand_aliasing={{}: (2, {})} | custom-call | flops 1207959552 | bytes 4718592 | tf_op jit(solution)/shard_map/pallas_call | solution.py:141
  70.1 1.4 %shard_map.82.refs_0_ = f32[1536,128]{1,0:T(8,128)S(1)} custom-call(bf16[1536,1536]{1,0:T(8,128)(2,1)S(1)} %bitcast.20, bf16[1536,128]{1,0:T(8,128)(2,1)S(1)} %collective-permute-done.13.source, f32[1536,128]{1,0:T(8,128)S(1)} %shard_map.81.refs_0_), custom_call_target="tpu_custom_call", output_to_operand_aliasing={{}: (2, {})} | custom-call | flops 1207959552 | bytes 4718592 | tf_op jit(solution)/shard_map/pallas_call | solution.py:141
  71.5 1.4 %shard_map.83.refs_0_ = f32[1536,128]{1,0:T(8,128)S(1)} custom-call(bf16[1536,1536]{1,0:T(8,128)(2,1)S(1)} %bitcast.18, bf16[1536,128]{1,0:T(8,128)(2,1)S(1)} %collective-permute-done.12.source, f32[1536,128]{1,0:T(8,128)S(1)} %shard_map.82.refs_0_), custom_call_target="tpu_custom_call", output_to_operand_aliasing={{}: (2, {})} | custom-call | flops 1207959552 | bytes 4718592 | tf_op jit(solution)/shard_map/pallas_call | solution.py:141
  73.0 1.4 %shard_map.84.refs_0_ = f32[1536,128]{1,0:T(8,128)S(1)} custom-call(bf16[1536,1536]{1,0:T(8,128)(2,1)S(1)} %bitcast.16, bf16[1536,128]{1,0:T(8,128)(2,1)S(1)} %collective-permute-done.11.source, f32[1536,128]{1,0:T(8,128)S(1)} %shard_map.83.refs_0_), custom_call_target="tpu_custom_call", output_to_operand_aliasing={{}: (2, {})} | custom-call | flops 1207959552 | bytes 4718592 | tf_op jit(solution)/shard_map/pallas_call | solution.py:141
  74.8 1.4 %shard_map.85.mine = bf16[1536,128]{1,0:T(8,128)(2,1)S(1)} custom-call(bf16[1536,1536]{1,0:T(8,128)(2,1)S(1)} %bitcast.14, bf16[1536,128]{1,0:T(8,128)(2,1)S(1)} %collective-permute-done.10.source, f32[1536,128]{1,0:T(8,128)S(1)} %shard_map.84.refs_0_, f32[1536,128]{1,0:T(8,128)S(1)} %mul.30.refs_1_, bf16[1536,128]{1,0:T(8,128)(2,1)S(1)} %get-tuple-element.32.refs_2_), custom_call_target="tpu_custom_call" | custom-call | flops 1207959552 | bytes 4718592 | tf_op jit(solution)/shard_map/pallas_call | solution.py:141
  76.2 2.9 %collective-permute-start.16 = (bf16[1536,128]{1,0:T(8,128)(2,1)S(1)}, bf16[1536,128]{1,0:T(8,128)(2,1)S(1)}, u32[]{:S(2)}, u32[]{:S(2)}) collective-permute-start(bf16[1536,128]{1,0:T(8,128)(2,1)S(1)} %shard_map.85.mine), channel_id=1, source_target_pairs={{0,1},{1,0},{2,3},{3,2},{4,5},{5,4},{6,7},{7,6},{8,9},{9,8},{10,11... | collective-permute-start | bytes 1179656 | tf_op jit(solution)/shard_map/ppermute | solution.py:163
  79.1 1.3 %collective-permute-done.16.other = bf16[1536,128]{1,0:T(8,128)(2,1)S(1)} collective-permute-done((bf16[1536,128]{1,0:T(8,128)(2,1)S(1)}, bf16[1536,128]{1,0:T(8,128)(2,1)S(1)}, u32[]{:S(2)}, u32[]{:S(2)}) %collective-permute-start.16) | collective-permute-done | bytes 393248 | tf_op jit(solution)/shard_map/ppermute | solution.py:163
  80.4 1.4 %shard_map.86 = bf16[1536,256]{1,0:T(8,128)(2,1)} custom-call(bf16[1536,128]{1,0:T(8,128)(2,1)S(1)} %shard_map.85.mine, bf16[1536,128]{1,0:T(8,128)(2,1)S(1)} %collective-permute-done.16.other, bf16[128,256]{1,0:T(8,128)(2,1)S(1)} %get-tuple-element.36.mine_weight, bf16[128,256]{1,0:T(8,128)(2,1)S(1)} %get-tuple-element.35.other_weight), custom_call_target="tpu_custom_call" | custom-call | tf_op jit(solution)/shard_map/pallas_call | solution.py:225
  (64 shorter events, 1.5 us)
Async XLA Ops:
  0.0 22.6 %collective-permute-start.3 = (bf16[8,11,256,256]{3,2,1,0:T(8,128)(2,1)}, bf16[8,11,256,256]{3,2,1,0:T(8,128)(2,1)}, u32[]{:S(2)}, u32[]{:S(2)}) collective-permute-start(bf16[8,11,256,256]{3,2,1,0:T(8,128)(2,1)} %bitcast.25), channel_id=1, source_target_pairs={{0,1},{1,0},{2,3},{3,2},{4,5},{5,4},{6,7},{7,6},{8,9},{9,8},{10,11... | collective-permute-start | bytes 34603016 | tf_op jit(solution)/shard_map/ppermute | solution.py:163
  5.2 11.3 %collective-permute-start.1 = (bf16[768,128]{1,0:T(8,128)(2,1)S(1)}, bf16[768,128]{1,0:T(8,128)(2,1)S(1)}, u32[]{:S(2)}, u32[]{:S(2)}) collective-permute-start(bf16[768,128]{1,0:T(8,128)(2,1)S(1)} %get-tuple-element.34), channel_id=1, source_target_pairs={{0,16},{128,144},{1,5},{129,133},{32,48},{160,176},{33,37},{161,16... | collective-permute-start | bytes 589832 | tf_op jit(solution)/shard_map/ppermute | solution.py:163
  8.4 8.2 %collective-permute-start.2 = (bf16[768,128]{1,0:T(8,128)(2,1)S(1)}, bf16[768,128]{1,0:T(8,128)(2,1)S(1)}, u32[]{:S(2)}, u32[]{:S(2)}) collective-permute-start(bf16[768,128]{1,0:T(8,128)(2,1)S(1)} %get-tuple-element.34), channel_id=1, source_target_pairs={{0,46},{128,174},{1,59},{129,187},{32,78},{160,206},{33,91},{161,2... | collective-permute-start | bytes 589832 | tf_op jit(solution)/shard_map/ppermute | solution.py:163
  11.0 7.6 %collective-permute-start = (bf16[768,128]{1,0:T(8,128)(2,1)S(1)}, bf16[768,128]{1,0:T(8,128)(2,1)S(1)}, u32[]{:S(2)}, u32[]{:S(2)}) collective-permute-start(bf16[768,128]{1,0:T(8,128)(2,1)S(1)} %get-tuple-element.33), channel_id=1, source_target_pairs={{0,230},{128,102},{1,249},{129,121},{32,6},{160,134},{33,25},{161,... | collective-permute-start | bytes 589832 | tf_op jit(solution)/shard_map/ppermute | solution.py:163
  18.6 18.1 %collective-permute-start.4 = (bf16[768,128]{1,0:T(8,128)(2,1)S(1)}, bf16[768,128]{1,0:T(8,128)(2,1)S(1)}, u32[]{:S(2)}, u32[]{:S(2)}) collective-permute-start(bf16[768,128]{1,0:T(8,128)(2,1)S(1)} %add_add_fusion.1), channel_id=1, source_target_pairs={{0,88},{230,190},{16,246},{46,234},{128,216},{102,62},{144,118},{1... | collective-permute-start | bytes 589832 | tf_op jit(solution)/shard_map/ppermute | solution.py:163
  19.9 16.8 %collective-permute-start.5 = (bf16[768,128]{1,0:T(8,128)(2,1)S(1)}, bf16[768,128]{1,0:T(8,128)(2,1)S(1)}, u32[]{:S(2)}, u32[]{:S(2)}) collective-permute-start(bf16[768,128]{1,0:T(8,128)(2,1)S(1)} %add_add_fusion.1), channel_id=1, source_target_pairs={{0,250},{230,162},{16,72},{46,140},{128,122},{102,34},{144,200},{1... | collective-permute-start | bytes 589832 | tf_op jit(solution)/shard_map/ppermute | solution.py:163
  21.2 15.5 %collective-permute-start.6 = (bf16[768,128]{1,0:T(8,128)(2,1)S(1)}, bf16[768,128]{1,0:T(8,128)(2,1)S(1)}, u32[]{:S(2)}, u32[]{:S(2)}) collective-permute-start(bf16[768,128]{1,0:T(8,128)(2,1)S(1)} %add_add_fusion.1), channel_id=1, source_target_pairs={{0,28},{230,68},{16,178},{46,84},{128,156},{102,196},{144,50},{174... | collective-permute-start | bytes 589832 | tf_op jit(solution)/shard_map/ppermute | solution.py:163
  36.8 7.2 %collective-permute-start.7 = (bf16[768,128]{1,0:T(8,128)(2,1)S(1)}, bf16[768,128]{1,0:T(8,128)(2,1)S(1)}, u32[]{:S(2)}, u32[]{:S(2)}) collective-permute-start(bf16[768,128]{1,0:T(8,128)(2,1)S(1)} %add_add_fusion.refs_0_), channel_id=1, source_target_pairs={{34,0},{46,12},{50,16},{62,28},{0,34},{12,46},{16,50},{28,62},{102... | collective-permute-start | bytes 589832 | tf_op jit(solution)/shard_map/ppermute | solution.py:163
  36.9 11.1 %collective-permute-start.8 = (bf16[768,128]{1,0:T(8,128)(2,1)S(1)}, bf16[768,128]{1,0:T(8,128)(2,1)S(1)}, u32[]{:S(2)}, u32[]{:S(2)}) collective-permute-start(bf16[768,128]{1,0:T(8,128)(2,1)S(1)} %add_add_fusion.refs_0_), channel_id=1, source_target_pairs={{12,0},{0,12},{28,16},{16,28},{46,34},{34,46},{62,50},{50,62},{72,... | collective-permute-start | bytes 589832 | tf_op jit(solution)/shard_map/ppermute | solution.py:163
  43.9 9.9 %collective-permute-start.9 = (bf16[768,128]{1,0:T(8,128)(2,1)S(1)}, bf16[768,128]{1,0:T(8,128)(2,1)S(1)}, u32[]{:S(2)}, u32[]{:S(2)}) collective-permute-start(bf16[768,128]{1,0:T(8,128)(2,1)S(1)} %add_add_fusion.refs_0_), channel_id=1, source_target_pairs={{46,0},{34,12},{62,16},{50,28},{12,34},{0,46},{28,50},{16,62},{106... | collective-permute-start | bytes 589832 | tf_op jit(solution)/shard_map/ppermute | solution.py:163
  53.8 13.3 %slice-start.10 = ((s8[4718592]{0:T(1024)(128)(4,1)}), s8[4194304]{0:T(1024)(128)(4,1)S(1)}, s32[]{:S(2)}) async-start(s8[4718592]{0:T(1024)(128)(4,1)} %bitcast.23), calls=%async_computation.10 | async-start | bytes 8388608
  54.4 10.1 %collective-permute-start.15 = (bf16[1536,128]{1,0:T(8,128)(2,1)S(1)}, bf16[1536,128]{1,0:T(8,128)(2,1)S(1)}, u32[]{:S(2)}, u32[]{:S(2)}) collective-permute-start(bf16[1536,128]{1,0:T(8,128)(2,1)S(1)} %get-tuple-element.26.source), channel_id=1, source_target_pairs={{0,32},{1,225},{2,34},{3,227},{4,36},{5,229},{6,38},{7,231},{8,40}... | collective-permute-start | bytes 1179656 | tf_op jit(solution)/shard_map/ppermute | solution.py:163
  58.6 9.9 %collective-permute-start.14 = (bf16[1536,128]{1,0:T(8,128)(2,1)S(1)}, bf16[1536,128]{1,0:T(8,128)(2,1)S(1)}, u32[]{:S(2)}, u32[]{:S(2)}) collective-permute-start(bf16[1536,128]{1,0:T(8,128)(2,1)S(1)} %get-tuple-element.26.source), channel_id=1, source_target_pairs={{0,8},{1,25},{2,10},{3,27},{4,12},{5,29},{6,14},{7,31},{8,16},{9,1... | collective-permute-start | bytes 1179656 | tf_op jit(solution)/shard_map/ppermute | solution.py:163
  60.2 9.8 %collective-permute-start.13 = (bf16[1536,128]{1,0:T(8,128)(2,1)S(1)}, bf16[1536,128]{1,0:T(8,128)(2,1)S(1)}, u32[]{:S(2)}, u32[]{:S(2)}) collective-permute-start(bf16[1536,128]{1,0:T(8,128)(2,1)S(1)} %get-tuple-element.26.source), channel_id=1, source_target_pairs={{0,2},{1,7},{2,4},{3,1},{4,6},{5,3},{6,0},{7,5},{8,10},{9,15},{10,... | collective-permute-start | bytes 1179656 | tf_op jit(solution)/shard_map/ppermute | solution.py:163
  61.3 10.2 %collective-permute-start.12 = (bf16[1536,128]{1,0:T(8,128)(2,1)S(1)}, bf16[1536,128]{1,0:T(8,128)(2,1)S(1)}, u32[]{:S(2)}, u32[]{:S(2)}) collective-permute-start(bf16[1536,128]{1,0:T(8,128)(2,1)S(1)} %get-tuple-element.22.source), channel_id=1, source_target_pairs={{0,32},{1,225},{2,34},{3,227},{4,36},{5,229},{6,38},{7,231},{8,40}... | collective-permute-start | bytes 1179656 | tf_op jit(solution)/shard_map/ppermute | solution.py:163
  61.7 11.3 %collective-permute-start.11 = (bf16[1536,128]{1,0:T(8,128)(2,1)S(1)}, bf16[1536,128]{1,0:T(8,128)(2,1)S(1)}, u32[]{:S(2)}, u32[]{:S(2)}) collective-permute-start(bf16[1536,128]{1,0:T(8,128)(2,1)S(1)} %get-tuple-element.22.source), channel_id=1, source_target_pairs={{0,8},{1,25},{2,10},{3,27},{4,12},{5,29},{6,14},{7,31},{8,16},{9,1... | collective-permute-start | bytes 1179656 | tf_op jit(solution)/shard_map/ppermute | solution.py:163
  61.7 5.4 %slice-start.11 = ((s8[4718592]{0:T(1024)(128)(4,1)}), s8[524288]{0:T(1024)(128)(4,1)S(1)}, s32[]{:S(2)}) async-start(s8[4718592]{0:T(1024)(128)(4,1)} %bitcast.23), calls=%async_computation.11 | async-start | bytes 1048576
  61.7 6.8 %slice-start.8 = ((s8[4718592]{0:T(1024)(128)(4,1)}), s8[4194304]{0:T(1024)(128)(4,1)S(1)}, s32[]{:S(2)}) async-start(s8[4718592]{0:T(1024)(128)(4,1)} %bitcast.21), calls=%async_computation.8 | async-start | bytes 8388608
  63.1 5.4 %slice-start.9 = ((s8[4718592]{0:T(1024)(128)(4,1)}), s8[524288]{0:T(1024)(128)(4,1)S(1)}, s32[]{:S(2)}) async-start(s8[4718592]{0:T(1024)(128)(4,1)} %bitcast.21), calls=%async_computation.9 | async-start | bytes 1048576
  63.1 6.9 %slice-start.6 = ((s8[4718592]{0:T(1024)(128)(4,1)}), s8[4194304]{0:T(1024)(128)(4,1)S(1)}, s32[]{:S(2)}) async-start(s8[4718592]{0:T(1024)(128)(4,1)} %bitcast.19), calls=%async_computation.6 | async-start | bytes 8388608
  64.6 9.9 %collective-permute-start.10 = (bf16[1536,128]{1,0:T(8,128)(2,1)S(1)}, bf16[1536,128]{1,0:T(8,128)(2,1)S(1)}, u32[]{:S(2)}, u32[]{:S(2)}) collective-permute-start(bf16[1536,128]{1,0:T(8,128)(2,1)S(1)} %get-tuple-element.22.source), channel_id=1, source_target_pairs={{0,2},{1,7},{2,4},{3,1},{4,6},{5,3},{6,0},{7,5},{8,10},{9,15},{10,... | collective-permute-start | bytes 1179656 | tf_op jit(solution)/shard_map/ppermute | solution.py:163
  67.1 3.0 %slice-start.7 = ((s8[4718592]{0:T(1024)(128)(4,1)}), s8[524288]{0:T(1024)(128)(4,1)S(1)}, s32[]{:S(2)}) async-start(s8[4718592]{0:T(1024)(128)(4,1)} %bitcast.19), calls=%async_computation.7 | async-start | bytes 1048576
  67.1 4.4 %slice-start.4 = ((s8[4718592]{0:T(1024)(128)(4,1)}), s8[4194304]{0:T(1024)(128)(4,1)S(1)}, s32[]{:S(2)}) async-start(s8[4718592]{0:T(1024)(128)(4,1)} %bitcast.17), calls=%async_computation.4 | async-start | bytes 8388608
  68.6 3.0 %slice-start.5 = ((s8[4718592]{0:T(1024)(128)(4,1)}), s8[524288]{0:T(1024)(128)(4,1)S(1)}, s32[]{:S(2)}) async-start(s8[4718592]{0:T(1024)(128)(4,1)} %bitcast.17), calls=%async_computation.5 | async-start | bytes 1048576
  68.6 4.4 %slice-start.2 = ((s8[4718592]{0:T(1024)(128)(4,1)}), s8[4194304]{0:T(1024)(128)(4,1)S(1)}, s32[]{:S(2)}) async-start(s8[4718592]{0:T(1024)(128)(4,1)} %bitcast.15), calls=%async_computation.2 | async-start | bytes 8388608
  70.0 2.9 %slice-start.3 = ((s8[4718592]{0:T(1024)(128)(4,1)}), s8[524288]{0:T(1024)(128)(4,1)S(1)}, s32[]{:S(2)}) async-start(s8[4718592]{0:T(1024)(128)(4,1)} %bitcast.15), calls=%async_computation.3 | async-start | bytes 1048576
  70.1 4.7 %slice-start = ((s8[4718592]{0:T(1024)(128)(4,1)}), s8[4194304]{0:T(1024)(128)(4,1)S(1)}, s32[]{:S(2)}) async-start(s8[4718592]{0:T(1024)(128)(4,1)} %bitcast.13), calls=%async_computation | async-start | bytes 8388608
  71.5 3.2 %slice-start.1 = ((s8[4718592]{0:T(1024)(128)(4,1)}), s8[524288]{0:T(1024)(128)(4,1)S(1)}, s32[]{:S(2)}) async-start(s8[4718592]{0:T(1024)(128)(4,1)} %bitcast.13), calls=%async_computation.1 | async-start | bytes 1048576
  74.4 4.6 %copy-start = (bf16[256,256]{1,0:T(8,128)(2,1)S(1)}, bf16[256,256]{1,0:T(8,128)(2,1)}, u32[]{:S(2)}) copy-start(bf16[256,256]{1,0:T(8,128)(2,1)} %param.9) | copy-start | bytes 393220
  76.2 4.2 %collective-permute-start.16 = (bf16[1536,128]{1,0:T(8,128)(2,1)S(1)}, bf16[1536,128]{1,0:T(8,128)(2,1)S(1)}, u32[]{:S(2)}, u32[]{:S(2)}) collective-permute-start(bf16[1536,128]{1,0:T(8,128)(2,1)S(1)} %shard_map.85.mine), channel_id=1, source_target_pairs={{0,1},{1,0},{2,3},{3,2},{4,5},{5,4},{6,7},{7,6},{8,9},{9,8},{10,11... | collective-permute-start | bytes 1179656 | tf_op jit(solution)/shard_map/ppermute | solution.py:163

commit v3 on v2

v3 whole, which is shorter than its diff:
```python
import functools
import itertools

import jax
import jax.numpy as jnp
import numpy as np
from jax import lax
from jax.experimental import pallas as pl
from jax.experimental.pallas import tpu as pltpu
from jax.sharding import PartitionSpec as P

NZ, NX, NY, CORES = 8, 4, 4, 2
AXES = ("rows", "rep")
CHIPS = list(itertools.product(range(NZ), range(NX), range(NY)))
COLORS = 4
PIECES = 4
SIGNS = ((1, 1), (1, -1), (-1, 1), (-1, -1))
HOLDERS = (
    ((0, 0), (2, 1), (0, 3), (6, 1), (1, 3), (3, 0), (6, 3), (4, 3)),
    ((0, 2), (3, 2), (5, 2), (1, 1), (0, 1), (4, 1), (5, 1), (2, 2)),
    ((7, 3), (5, 0), (7, 1), (6, 2), (2, 3), (2, 0), (4, 2), (4, 0)),
    ((7, 0), (7, 2), (6, 0), (5, 3), (1, 0), (3, 1), (3, 3), (1, 2)),
)
GROUP_SHIFT = 1
PARTNERS = 1


def flat(z, x, y, core):
    return ((z % NZ * NX + x % NX) * NY + y % NY) * CORES + core


def color_of(z, x, y, core):
    return (z + 2 * x - y if core == 0 else z + 2 * y - x) % COLORS


def chip_at(color, height, across, core):
    up, side = SIGNS[color]
    height, across = up * height % NZ, side * across % NX
    z, other = color + COLORS * core + height, height + 2 * across
    return (z, across, other) if core == 0 else (z, other, across)


def partner(height, across, i):
    if i & 1:
        height = (height - GROUP_SHIFT ^ 1) + GROUP_SHIFT
    return height % NZ, across ^ (PARTNERS if i & 2 else 0)


def plan():
    scatter = [[] for _ in range(PIECES)]
    spread, gather, trade = ([[] for _ in range(3)] for _ in range(3))
    for color, core in itertools.product(range(COLORS), range(CORES)):
        at = lambda place, on=core: flat(*chip_at(color, *place, core), on)
        owner = (0, 0)
        for piece, places in enumerate(HOLDERS):
            if places[0] != owner:
                scatter[piece].append((at(owner), at(places[0])))
                scatter[piece].append((at(owner, 1 - core), at(places[4])))
            else:
                scatter[piece].append((at(owner), at(places[4])))
            for holder in (0, 4):
                for i in range(3):
                    spread[i].append((at(places[holder]), at(places[holder + 1 + i])))
        for place in itertools.product(range(NZ), range(NX)):
            for i in range(1, 4):
                gather[i - 1].append((at(partner(*place, i)), at(place)))
    for z, x, y in CHIPS:
        for core, s in ((0, 1), (1, -1)):
            for i, (dz, dx, dy) in enumerate(((1, 0, 0), (0, 1, 0), (0, 0, 1))):
                trade[i].append((flat(z, x, y, core), flat(z + s * dz, x + s * dx, y + s * dy, core)))
    return scatter, spread, gather, trade


def facts():
    rows = []
    for z, x, y in CHIPS:
        for core, s in ((0, 1), (1, -1)):
            color = color_of(z, x, y, core)
            up, side = SIGNS[color]
            place = up * (z - color - COLORS * core) % NZ, side * (x, y)[core] % NX
            row = [int(place == (0, 0))]
            for i in range(4):
                row.append(next(p for p, places in enumerate(HOLDERS) if partner(*place, i) in places))
            sent = [color_of(z - s, x, y, core), color_of(z, x - s, y, core), color_of(z, x, y - s, core)]
            row += [c + COLORS * core for c in [color] + sent]
            rows.append(row)
    return np.array(rows, np.int32)


VMEM = pl.BlockSpec(memory_space=pltpu.VMEM)
SMEM = pl.BlockSpec(memory_space=pltpu.SMEM)
HBM = pl.BlockSpec(memory_space=pltpu.HBM)


def inverse_columns(degrees):
    groups, lanes = degrees.shape
    padded = jnp.concatenate([degrees[...], jnp.ones((-groups % 8, lanes), degrees.dtype)], axis=0)
    return lax.rsqrt(padded.astype(jnp.float32)).T


def scale_kernel(blocks, features, degrees, *refs):
    *outs, held, held_degrees, sems = refs

    @pl.when(lax.axis_index("rows") % (lax.axis_size("rows") // blocks) == 0)
    def _():
        copies = [
            pltpu.make_async_copy(degrees, held_degrees, sems.at[0]),
            pltpu.make_async_copy(features, held, sems.at[1]),
        ]
        for copy in copies:
            copy.start()
        copies[0].wait()
        inverse = inverse_columns(held_degrees)
        copies[1].wait()
        groups, size = degrees.shape
        for i in range(groups):
            out, place = outs[i * len(outs) // groups], i % (groups // len(outs)) * size
            here = held[pl.ds(i * size, size), :].astype(jnp.float32)
            out[pl.ds(place, size), :] = (here * inverse[:, i : i + 1]).astype(out.dtype)


def assemble_kernel(slots, *refs):
    *pieces, out = refs
    size = pieces[0].shape[0]
    for i, piece in enumerate(pieces):
        out[pl.ds(pl.multiple_of(slots[i] * size, size), size), :] = piece[...]


def prepare_kernel(order, table, own, peer, *refs):
    *mats, sems = refs
    blocks, half, tile = own.shape[:3]
    slots = CORES * half
    places = [(j, k) for j in range(len(mats)) for k in range(slots)]

    def place(j, k, act):
        entry = order[j] * slots + k
        row, column = table[entry], table[blocks * slots + entry]

        @pl.when(row >= 0)
        def _():
            target = mats[j].at[pl.ds(pl.multiple_of(row, tile), tile), pl.ds(pl.multiple_of(column, tile), tile)]
            act(pltpu.make_async_copy((own if k < half else peer).at[order[j], k % half], target, sems.at[j]))

    for j, k in places:
        if k == 0:
            mats[j][...] = jnp.zeros(mats[j].shape, mats[j].dtype)
        place(j, k, lambda copy: copy.start())
    for j, k in places:
        place(j, k, lambda copy: copy.wait())


def multiply_kernel(mat, source, *refs):
    *before, out = refs
    product = jnp.dot(mat[...], source[...], preferred_element_type=jnp.float32)
    out[...] = before[0][...] + product if before else product


def multiply_part_kernel(start, mat, source, before, out):
    rows = pl.ds(start, out.shape[0])
    out[...] = before[rows, :] + jnp.dot(mat[rows, :], source[...], preferred_element_type=jnp.float32)


def multiply(mat, source, before=None, part=None):
    args = [mat, source] + ([] if before is None else [before])
    height, width = source.shape
    if part is None:
        kernel, alias = multiply_kernel, ({} if before is None else {2: 0})
    else:
        height //= 2
        kernel, alias = functools.partial(multiply_part_kernel, part * height), {}
    return pl.pallas_call(
        kernel,
        out_shape=jax.ShapeDtypeStruct((height, width), jnp.float32),
        in_specs=[VMEM] * len(args),
        out_specs=VMEM,
        input_output_aliases=alias,
        compiler_params=pltpu.CompilerParams(vmem_limit_bytes=10 * 2**20),
        cost_estimate=pl.CostEstimate(
            flops=2 * height * mat.shape[1] * width, bytes_accessed=mat.size * 2, transcendentals=0
        ),
    )(*args)


def finish_kernel(start, mine, other, degrees, features, weight, *refs):
    *_, out, done, sem = refs
    rows = pl.ds(start, mine.shape[0])
    inverse = inverse_columns(degrees)
    size = degrees.shape[1]
    for i in range(mine.shape[0] // size):
        here = pl.ds(i * size, size)
        column = start // size + i
        total = (mine[here, :] + other[here, :]) * inverse[:, column : column + 1]
        combined = total + features[pl.ds(start + i * size, size), :].astype(jnp.float32)
        result = jnp.dot(combined.astype(jnp.bfloat16), weight[...], preferred_element_type=jnp.float32)
        done[here, :] = jnp.maximum(result, 0.0).astype(done.dtype)
    copy = pltpu.make_async_copy(done, out.at[rows], sem)
    copy.start()
    copy.wait()


def finish(part, mine, other, degrees, features, weight, before=None):
    args = [mine, other, degrees, features, weight] + ([] if before is None else [before])
    return pl.pallas_call(
        functools.partial(finish_kernel, part * mine.shape[0]),
        out_shape=jax.ShapeDtypeStruct(features.shape, jnp.bfloat16),
        in_specs=[VMEM] * 5 + [HBM] * (len(args) - 5),
        out_specs=HBM,
        scratch_shapes=[pltpu.VMEM(mine.shape, jnp.bfloat16), pltpu.SemaphoreType.DMA],
        input_output_aliases={} if before is None else {5: 0},
        compiler_params=pltpu.CompilerParams(vmem_limit_bytes=12 * 2**20),
        cost_estimate=pl.CostEstimate(
            flops=2 * mine.size * weight.shape[1], bytes_accessed=mine.size * 12, transcendentals=0
        ),
    )(*args)


def on_device(features, degrees, weight, tile_values, tile_pos, live):
    scatter, spread, gather, trade = plan()
    swap = [(i, i ^ 1) for i in range(len(CHIPS) * CORES)]
    send = lambda x, pairs: lax.ppermute(x, AXES, pairs)
    height, width = features.shape
    blocks, half, tile = tile_values.shape[1:4]
    side = height // tile
    core = lax.axis_index("rep")
    me = lax.axis_index("rows") * CORES + core
    fact = lax.dynamic_index_in_dim(jnp.asarray(facts()), me, 0, keepdims=False)
    order = fact[5:]

    own = tile_values[0]
    peer = send(own, swap)
    own = pltpu.with_memory_space_constraint(own, pltpu.HBM)

    degrees = degrees.reshape(-1, 128)
    in_hbm = lambda x: pltpu.with_memory_space_constraint(x, pltpu.HBM)
    cut = pl.pallas_call(
        functools.partial(scale_kernel, blocks),
        out_shape=[jax.ShapeDtypeStruct((height // PIECES, width), jnp.bfloat16)] * PIECES,
        in_specs=[HBM, HBM],
        out_specs=[VMEM] * PIECES,
        scratch_shapes=[
            pltpu.VMEM(features.shape, features.dtype),
            pltpu.VMEM(degrees.shape, degrees.dtype),
            pltpu.SemaphoreType.DMA((2,)),
        ],
        compiler_params=pltpu.CompilerParams(vmem_limit_bytes=4 * 2**20),
    )(in_hbm(features), in_hbm(degrees))

    used = jnp.arange(half * CORES)[None, :] < live[0][:, None]
    row = jnp.where(used, tile_pos[0] // side * tile, -1)
    column = tile_pos[0] % side * tile
    both = jnp.stack([row, column]).reshape(2, blocks, CORES, half)
    table = jnp.where(core == 0, both, both[:, :, ::-1]).reshape(-1)

    piece = jnp.where(fact[0] == 1, cut[0], jnp.zeros_like(cut[0]))
    for got in [send(cut[i], pairs) for i, pairs in enumerate(scatter)]:
        piece = piece + got
    kept = piece
    for got in [send(kept, pairs) for pairs in spread]:
        piece = piece + got
    pieces = [piece] + [send(piece, pairs) for pairs in gather]
    source = pl.pallas_call(
        assemble_kernel,
        out_shape=jax.ShapeDtypeStruct((height, width), features.dtype),
        in_specs=[SMEM] + [VMEM] * 4,
        out_specs=VMEM,
        compiler_params=pltpu.CompilerParams(vmem_limit_bytes=4 * 2**20),
    )(fact[1:5], *pieces)
    order, source = lax.optimization_barrier((order, source))
    traded = [send(source, pairs) for pairs in trade]
    matrix = jax.ShapeDtypeStruct((height, height), own.dtype)
    mats = pl.pallas_call(
        prepare_kernel,
        out_shape=[matrix] * COLORS,
        in_specs=[SMEM, SMEM, HBM, HBM],
        out_specs=[VMEM] * COLORS,
        scratch_shapes=[pltpu.SemaphoreType.DMA((COLORS,))],
        compiler_params=pltpu.CompilerParams(vmem_limit_bytes=24 * 2**20),
        cost_estimate=pl.CostEstimate(flops=0, bytes_accessed=own.size * 4, transcendentals=0),
    )(order, table, own, peer)
    total = None
    for mat, block in zip(mats[:-1], [source] + traded[:-1]):
        total = multiply(mat, block, total)
    parts = [multiply(mats[-1], traded[-1], total, part) for part in range(2)]
    others = [send(part, swap) for part in parts]
    result = finish(0, parts[0], others[0], degrees, features, weight)
    return finish(1, parts[1], others[1], degrees, features, weight, result)


def solution(mesh):
    placed = (
        P("rows", None),
        P("rows"),
        P(),
        P("rows", None, "rep", None, None),
        P("rows", None, None),
        P("rows", None),
    )
    return jax.shard_map(on_device, mesh=mesh, in_specs=placed, out_specs=P("rows", None), check_vma=False)
```

time: 81 us -> 69.6 us (0.86); the launches traced: 81.8 us -> 68.7 us
  Pallas kernels: 27.5 us -> 16.6 us
  waiting for transfers between devices: 13.2 us -> 22.9 us
  starting transfers between devices: 36.2 us -> 26.9 us
  other arithmetic: 2.82 us -> 0.85 us
    pallas_call x11 -> x10, Pallas kernels: 27.5 us -> 16.6 us  [the longest x1 6.19 us: on_device(): pl.pallas_call(prepare_kernel, out_shape=[matrix] * COLORS, in_specs=[SME...]
    ppermute x17 -> x16, waiting for transfers between devices: 13.2 us -> 22.9 us  [on_device(): send = lambda x, pairs: lax.ppermute(x, AXES, pairs)]
    ppermute x17 -> x16, starting transfers between devices: 36.2 us -> 26.9 us  [on_device(): send = lambda x, pairs: lax.ppermute(x, AXES, pairs)]
    convert_element_type x1 -> x0, other arithmetic: 1.27 us -> none  [on_device(): scaled = (mine.astype(jnp.float32) * inverse[:, None]).astype(jnp.bfloat16)]
  transfers between devices with their start and end apart: 17 -> 16, of which waited for: 4 -> 6; matrix products, arithmetic and copies ran while one was open for 5% -> 3% of each run, Pallas kernels for 29% -> 21%
where the time goes in v3:
time: 69.6 us; the launch traced here: 68.7 us
  starting transfers between devices  26.9 us (39%)
  waiting for transfers between devices  22.9 us (33%)
  Pallas kernels  16.6 us (24%)
  local copies, waits for them, and re-layouts  1.11 us (2%)
  other arithmetic  0.85 us (1%)
    ppermute x16, starting transfers between devices, on_device(): send = lambda x, pairs: lax.ppermute(x, AXES, pairs)  26.9 us
    ppermute x16, waiting for transfers between devices, on_device(): send = lambda x, pairs: lax.ppermute(x, AXES, pairs)  22.9 us
    pallas_call x1, Pallas kernels, on_device(): pl.pallas_call(prepare_kernel, out_shape=[matrix] * COLORS, in_specs=[SME...  6.19 us
    pallas_call x5, Pallas kernels, multiply(): pl.pallas_call(kernel, out_shape=jax.ShapeDtypeStruct((height, width), jn...  5.88 us
    pallas_call x2, Pallas kernels, finish(): pl.pallas_call(functools.partial(finish_kernel, part * mine.shape[0]), ou...  2.45 us
    pallas_call x1, Pallas kernels, on_device(): pl.pallas_call(functools.partial(scale_kernel, blocks), out_shape=[jax.Sh...  1.45 us
  transfers between devices with their start and end apart: 16, of which 6 were waited for; matrix products, arithmetic and copies ran while one was open for 3% of the time, Pallas kernels for 21%

profile of v3, /device:TPU:1, one launch (start us, length us, event | category | flops | bytes accessed | tf_op | source)
XLA Modules:
  0.0 68.7 jit_solution(1007808161382142072)
XLA Ops:
  0.0 3.2 %collective-permute-start.10 = (bf16[8,11,256,256]{3,2,1,0:T(8,128)(2,1)}, bf16[8,11,256,256]{3,2,1,0:T(8,128)(2,1)}, u32[]{:S(2)}, u32[]{:S(2)}) collective-permute-start(bf16[8,11,256,256]{3,2,1,0:T(8,128)(2,1)} %bitcast.15), channel_id=1, source_target_pairs={{0,1},{1,0},{2,3},{3,2},{4,5},{5,4},{6,7},{7,6},{8,9},{9,8},{10,11... | collective-permute-start | bytes 34603016 | tf_op jit(solution)/shard_map/ppermute | solution.py:220
  3.2 1.5 %shard_map.76 = (bf16[384,256]{1,0:T(8,128)(2,1)S(1)}, bf16[384,256]{1,0:T(8,128)(2,1)S(1)}, bf16[384,256]{1,0:T(8,128)(2,1)S(1)}, bf16[384,256]{1,0:T(8,128)(2,1)S(1)}) custom-call(bf16[1536,256]{1,0:T(8,128)(2,1)} %features.5, s32[12,128]{1,0:T(8,128)} %bitcast.12), custom_call_target="tpu_custom_call" | custom-call | tf_op jit(solution)/shard_map/pallas_call | solution.py:235
  4.7 0.7 collective-permute-start
  5.4 2.5 %collective-permute-start.1 = (bf16[384,256]{1,0:T(8,128)(2,1)S(1)}, bf16[384,256]{1,0:T(8,128)(2,1)S(1)}, u32[]{:S(2)}, u32[]{:S(2)}) collective-permute-start(bf16[384,256]{1,0:T(8,128)(2,1)S(1)} %get-tuple-element.16), channel_id=1, source_target_pairs={{0,16},{1,12},{129,133},{128,147},{32,48},{33,60},{161,165},{160,1... | collective-permute-start | bytes 589832 | tf_op jit(solution)/shard_map/ppermute | solution.py:220
  7.9 2.0 %collective-permute-start.2 = (bf16[384,256]{1,0:T(8,128)(2,1)S(1)}, bf16[384,256]{1,0:T(8,128)(2,1)S(1)}, u32[]{:S(2)}, u32[]{:S(2)}) collective-permute-start(bf16[384,256]{1,0:T(8,128)(2,1)S(1)} %get-tuple-element.17), channel_id=1, source_target_pairs={{0,250},{1,88},{129,111},{128,199},{32,10},{33,104},{161,139},{160... | collective-permute-start | bytes 589832 | tf_op jit(solution)/shard_map/ppermute | solution.py:220
  9.9 1.3 %collective-permute-start.3 = (bf16[384,256]{1,0:T(8,128)(2,1)S(1)}, bf16[384,256]{1,0:T(8,128)(2,1)S(1)}, u32[]{:S(2)}, u32[]{:S(2)}) collective-permute-start(bf16[384,256]{1,0:T(8,128)(2,1)S(1)} %get-tuple-element.18), channel_id=1, source_target_pairs={{0,230},{1,34},{129,121},{128,169},{32,6},{33,66},{161,153},{160,2... | collective-permute-start | bytes 589832 | tf_op jit(solution)/shard_map/ppermute | solution.py:220
  11.2 0.7 %constant_dynamic-slice_fusion = s32[1,9]{1,0:T(1,128)S(1)} fusion(s32[256,9]{1,0:T(8,128)} %constant.45.clone, s32[]{:T(128)S(6)} %select_n.39), kind=kLoop, calls=%fused_computation.16 | loop fusion | bytes 76 | tf_op jit(solution)/shard_map/jit(dynamic_index_in_dim)/dynamic_slice | solution.py:226
  12.0 2.3 %collective-permute-done.2 = bf16[384,256]{1,0:T(8,128)(2,1)S(1)} collective-permute-done((bf16[384,256]{1,0:T(8,128)(2,1)S(1)}, bf16[384,256]{1,0:T(8,128)(2,1)S(1)}, u32[]{:S(2)}, u32[]{:S(2)}) %collective-permute-start.2) | collective-permute-done | bytes 196640 | tf_op jit(solution)/shard_map/ppermute | solution.py:220
  14.3 2.4 %collective-permute-done.3 = bf16[384,256]{1,0:T(8,128)(2,1)S(1)} collective-permute-done((bf16[384,256]{1,0:T(8,128)(2,1)S(1)}, bf16[384,256]{1,0:T(8,128)(2,1)S(1)}, u32[]{:S(2)}, u32[]{:S(2)}) %collective-permute-start.3) | collective-permute-done | bytes 196640 | tf_op jit(solution)/shard_map/ppermute | solution.py:220
  16.7 0.7 collective-permute-start.4
  17.4 0.7 collective-permute-start.5
  18.1 1.3 %collective-permute-start.6 = (bf16[384,256]{1,0:T(8,128)(2,1)S(1)}, bf16[384,256]{1,0:T(8,128)(2,1)S(1)}, u32[]{:S(2)}, u32[]{:S(2)}) collective-permute-start(bf16[384,256]{1,0:T(8,128)(2,1)S(1)} %add_add_fusion.1), channel_id=1, source_target_pairs={{0,200},{62,156},{16,46},{12,84},{250,212},{88,128},{230,190},{34,... | collective-permute-start | bytes 589832 | tf_op jit(solution)/shard_map/ppermute | solution.py:220
  19.4 11.8 %collective-permute-done.6 = bf16[384,256]{1,0:T(8,128)(2,1)S(1)} collective-permute-done((bf16[384,256]{1,0:T(8,128)(2,1)S(1)}, bf16[384,256]{1,0:T(8,128)(2,1)S(1)}, u32[]{:S(2)}, u32[]{:S(2)}) %collective-permute-start.6) | collective-permute-done | bytes 196640 | tf_op jit(solution)/shard_map/ppermute | solution.py:220
  31.3 0.7 %collective-permute-start.8 = (bf16[384,256]{1,0:T(8,128)(2,1)S(1)}, bf16[384,256]{1,0:T(8,128)(2,1)S(1)}, u32[]{:S(2)}, u32[]{:S(2)}) collective-permute-start(bf16[384,256]{1,0:T(8,128)(2,1)S(1)} %add_add_fusion.refs_0_), channel_id=1, source_target_pairs={{12,0},{0,12},{28,16},{16,28},{46,34},{34,46},{62,50},{50,62},{72,... | collective-permute-start | bytes 589832 | tf_op jit(solution)/shard_map/ppermute | solution.py:220
  32.1 5.5 %collective-permute-start.9 = (bf16[384,256]{1,0:T(8,128)(2,1)S(1)}, bf16[384,256]{1,0:T(8,128)(2,1)S(1)}, u32[]{:S(2)}, u32[]{:S(2)}) collective-permute-start(bf16[384,256]{1,0:T(8,128)(2,1)S(1)} %add_add_fusion.refs_0_), channel_id=1, source_target_pairs={{234,0},{230,12},{250,16},{246,28},{72,34},{68,46},{88,50},{84,62}... | collective-permute-start | bytes 589832 | tf_op jit(solution)/shard_map/ppermute | solution.py:220
  37.6 2.6 %collective-permute-done.7.refs_1_ = bf16[384,256]{1,0:T(8,128)(2,1)S(1)} collective-permute-done((bf16[384,256]{1,0:T(8,128)(2,1)S(1)}, bf16[384,256]{1,0:T(8,128)(2,1)S(1)}, u32[]{:S(2)}, u32[]{:S(2)}) %collective-permute-start.7) | collective-permute-done | bytes 196640 | tf_op jit(solution)/shard_map/ppermute | solution.py:220
  40.2 3.0 %collective-permute-done.9.refs_3_ = bf16[384,256]{1,0:T(8,128)(2,1)S(1)} collective-permute-done((bf16[384,256]{1,0:T(8,128)(2,1)S(1)}, bf16[384,256]{1,0:T(8,128)(2,1)S(1)}, u32[]{:S(2)}, u32[]{:S(2)}) %collective-permute-start.9) | collective-permute-done | bytes 196640 | tf_op jit(solution)/shard_map/ppermute | solution.py:220
  43.2 0.6 shard_map.77.source
  43.8 1.9 %collective-permute-start.13 = (bf16[1536,256]{1,0:T(8,128)(2,1)S(1)}, bf16[1536,256]{1,0:T(8,128)(2,1)S(1)}, u32[]{:S(2)}, u32[]{:S(2)}) collective-permute-start(bf16[1536,256]{1,0:T(8,128)(2,1)S(1)} %shard_map.77.source), channel_id=1, source_target_pairs={{0,32},{1,225},{2,34},{3,227},{4,36},{5,229},{6,38},{7,231},{8,40}... | collective-permute-start | bytes 2359304 | tf_op jit(solution)/shard_map/ppermute | solution.py:220
  45.7 3.3 %collective-permute-start.12 = (bf16[1536,256]{1,0:T(8,128)(2,1)S(1)}, bf16[1536,256]{1,0:T(8,128)(2,1)S(1)}, u32[]{:S(2)}, u32[]{:S(2)}) collective-permute-start(bf16[1536,256]{1,0:T(8,128)(2,1)S(1)} %shard_map.77.source), channel_id=1, source_target_pairs={{0,8},{1,25},{2,10},{3,27},{4,12},{5,29},{6,14},{7,31},{8,16},{9,1... | collective-permute-start | bytes 2359304 | tf_op jit(solution)/shard_map/ppermute | solution.py:220
  49.0 0.8 %fusion.2 = (s32[1,8,22]{2,1,0:T(8,128)S(1)}, s32[1,8,22]{2,1,0:T(8,128)S(1)}) fusion(s32[1,8,22]{2,1,0:T(8,128)} %param.11, s32[8]{0:T(128)} %bitcast.21), kind=kLoop, calls=%fused_computation.9 | loop fusion | flops 2816 | bytes 2144 | tf_op jit(solution)/shard_map/mul | solution.py:250
  50.0 2.3 %collective-permute-start.11 = (bf16[1536,256]{1,0:T(8,128)(2,1)S(1)}, bf16[1536,256]{1,0:T(8,128)(2,1)S(1)}, u32[]{:S(2)}, u32[]{:S(2)}) collective-permute-start(bf16[1536,256]{1,0:T(8,128)(2,1)S(1)} %shard_map.77.source), channel_id=1, source_target_pairs={{0,2},{1,7},{2,4},{3,1},{4,6},{5,3},{6,0},{7,5},{8,10},{9,15},{10,... | collective-permute-start | bytes 2359304 | tf_op jit(solution)/shard_map/ppermute | solution.py:220
  52.4 6.2 %shard_map.78 = (bf16[1536,1536]{1,0:T(8,128)(2,1)S(1)}, bf16[1536,1536]{1,0:T(8,128)(2,1)S(1)}, bf16[1536,1536]{1,0:T(8,128)(2,1)S(1)}, bf16[1536,1536]{1,0:T(8,128)(2,1)S(1)}) custom-call(s32[4]{0:T(128)S(1)} %get-tuple-element.19.order, s32[352]{0:T(512)S(1)} %reshape.51.table, bf16[8,11,256,256]{3,2,1,0:T(8,128)(2,1)} %bitcast.16, ...), custom_call_target="tpu_custom_call" | custom-call | bytes 23068672 | tf_op jit(solution)/shard_map/pallas_call | solution.py:271
  58.6 1.4 %shard_map.79.refs_0_ = f32[1536,256]{1,0:T(8,128)S(1)} custom-call(bf16[1536,1536]{1,0:T(8,128)(2,1)S(1)} %get-tuple-element.24.mat, bf16[1536,256]{1,0:T(8,128)(2,1)S(1)} %shard_map.77.source), custom_call_target="tpu_custom_call" | custom-call | flops 1207959552 | bytes 4718592 | tf_op jit(solution)/shard_map/pallas_call | solution.py:171
  60.0 1.5 %shard_map.80.refs_0_ = f32[1536,256]{1,0:T(8,128)S(1)} custom-call(bf16[1536,1536]{1,0:T(8,128)(2,1)S(1)} %get-tuple-element.23.mat, bf16[1536,256]{1,0:T(8,128)(2,1)S(1)} %collective-permute-done.13.source, f32[1536,256]{1,0:T(8,128)S(1)} %shard_map.79.refs_0_), custom_call_target="tpu_custom_call", output_to_operand_aliasing={{}: (2, {})} | custom-call | flops 1207959552 | bytes 4718592 | tf_op jit(solution)/shard_map/pallas_call | solution.py:171
  61.5 1.5 %shard_map.81.before = f32[1536,256]{1,0:T(8,128)S(1)} custom-call(bf16[1536,1536]{1,0:T(8,128)(2,1)S(1)} %get-tuple-element.22.mat, bf16[1536,256]{1,0:T(8,128)(2,1)S(1)} %collective-permute-done.12.source, f32[1536,256]{1,0:T(8,128)S(1)} %shard_map.80.refs_0_), custom_call_target="tpu_custom_call", output_to_operand_aliasing={{}: (2, {})} | custom-call | flops 1207959552 | bytes 4718592 | tf_op jit(solution)/shard_map/pallas_call | solution.py:171
  63.0 0.8 %shard_map.83.mine = f32[768,256]{1,0:T(8,128)S(1)} custom-call(bf16[1536,1536]{1,0:T(8,128)(2,1)S(1)} %get-tuple-element.20.mat, bf16[1536,256]{1,0:T(8,128)(2,1)S(1)} %collective-permute-done.11.source, f32[1536,256]{1,0:T(8,128)S(1)} %shard_map.81.before), custom_call_target="tpu_custom_call" | custom-call | flops 603979776 | bytes 4718592 | tf_op jit(solution)/shard_map/pallas_call | solution.py:171
  63.9 0.8 %shard_map.82.mine = f32[768,256]{1,0:T(8,128)S(1)} custom-call(bf16[1536,1536]{1,0:T(8,128)(2,1)S(1)} %get-tuple-element.20.mat, bf16[1536,256]{1,0:T(8,128)(2,1)S(1)} %collective-permute-done.11.source, f32[1536,256]{1,0:T(8,128)S(1)} %shard_map.81.before), custom_call_target="tpu_custom_call" | custom-call | flops 603979776 | bytes 4718592 | tf_op jit(solution)/shard_map/pallas_call | solution.py:171
  64.7 0.6 collective-permute-start.14
  65.3 0.9 %collective-permute-done.15.other = f32[768,256]{1,0:T(8,128)S(1)} collective-permute-done((f32[768,256]{1,0:T(8,128)S(1)}, f32[768,256]{1,0:T(8,128)S(1)}, u32[]{:S(2)}, u32[]{:S(2)}) %collective-permute-start.15) | collective-permute-done | bytes 786464 | tf_op jit(solution)/shard_map/ppermute | solution.py:220
  66.2 1.2 %shard_map.84.refs_0_ = bf16[1536,256]{1,0:T(8,128)(2,1)} custom-call(f32[768,256]{1,0:T(8,128)S(1)} %shard_map.83.mine, f32[768,256]{1,0:T(8,128)S(1)} %collective-permute-done.15.other, s32[12,128]{1,0:T(8,128)S(1)} %bitcast.13, bf16[1536,256]{1,0:T(8,128)(2,1)S(1)} %copy-done, bf16[256,256]{1,0:T(8,128)(2,1)S(1)} %copy-done.1), custom_call_target="tpu_custom_call" | custom-call | flops 100663296 | bytes 2359296 | tf_op jit(solution)/shard_map/pallas_call | solution.py:203
  67.5 1.2 %shard_map.85 = bf16[1536,256]{1,0:T(8,128)(2,1)} custom-call(f32[768,256]{1,0:T(8,128)S(1)} %shard_map.82.mine, f32[768,256]{1,0:T(8,128)S(1)} %collective-permute-done.14.other, s32[12,128]{1,0:T(8,128)S(1)} %bitcast.14, bf16[1536,256]{1,0:T(8,128)(2,1)S(1)} %copy-done, bf16[256,256]{1,0:T(8,128)(2,1)S(1)} %copy-done.1, ...), custom_call_target="tpu_custom_call", output_to_operand_aliasing={{}: (5, {})} | custom-call | flops 100663296 | bytes 2359296 | tf_op jit(solution)/shard_map/pallas_call | solution.py:203
  (28 shorter events, 0.7 us)
Async XLA Ops:
  0.0 52.4 %collective-permute-start.10 = (bf16[8,11,256,256]{3,2,1,0:T(8,128)(2,1)}, bf16[8,11,256,256]{3,2,1,0:T(8,128)(2,1)}, u32[]{:S(2)}, u32[]{:S(2)}) collective-permute-start(bf16[8,11,256,256]{3,2,1,0:T(8,128)(2,1)} %bitcast.15), channel_id=1, source_target_pairs={{0,1},{1,0},{2,3},{3,2},{4,5},{5,4},{6,7},{7,6},{8,9},{9,8},{10,11... | collective-permute-start | bytes 34603016 | tf_op jit(solution)/shard_map/ppermute | solution.py:220
  4.7 7.3 %collective-permute-start = (bf16[384,256]{1,0:T(8,128)(2,1)S(1)}, bf16[384,256]{1,0:T(8,128)(2,1)S(1)}, u32[]{:S(2)}, u32[]{:S(2)}) collective-permute-start(bf16[384,256]{1,0:T(8,128)(2,1)S(1)} %get-tuple-element.15), channel_id=1, source_target_pairs={{0,62},{129,191},{32,78},{161,219},{64,58},{193,175},{96,74},{225,... | collective-permute-start | bytes 589832 | tf_op jit(solution)/shard_map/ppermute | solution.py:220
  5.4 6.6 %collective-permute-start.1 = (bf16[384,256]{1,0:T(8,128)(2,1)S(1)}, bf16[384,256]{1,0:T(8,128)(2,1)S(1)}, u32[]{:S(2)}, u32[]{:S(2)}) collective-permute-start(bf16[384,256]{1,0:T(8,128)(2,1)S(1)} %get-tuple-element.16), channel_id=1, source_target_pairs={{0,16},{1,12},{129,133},{128,147},{32,48},{33,60},{161,165},{160,1... | collective-permute-start | bytes 589832 | tf_op jit(solution)/shard_map/ppermute | solution.py:220
  7.9 6.4 %collective-permute-start.2 = (bf16[384,256]{1,0:T(8,128)(2,1)S(1)}, bf16[384,256]{1,0:T(8,128)(2,1)S(1)}, u32[]{:S(2)}, u32[]{:S(2)}) collective-permute-start(bf16[384,256]{1,0:T(8,128)(2,1)S(1)} %get-tuple-element.17), channel_id=1, source_target_pairs={{0,250},{1,88},{129,111},{128,199},{32,10},{33,104},{161,139},{160... | collective-permute-start | bytes 589832 | tf_op jit(solution)/shard_map/ppermute | solution.py:220
  9.9 6.8 %collective-permute-start.3 = (bf16[384,256]{1,0:T(8,128)(2,1)S(1)}, bf16[384,256]{1,0:T(8,128)(2,1)S(1)}, u32[]{:S(2)}, u32[]{:S(2)}) collective-permute-start(bf16[384,256]{1,0:T(8,128)(2,1)S(1)} %get-tuple-element.18), channel_id=1, source_target_pairs={{0,230},{1,34},{129,121},{128,169},{32,6},{33,66},{161,153},{160,2... | collective-permute-start | bytes 589832 | tf_op jit(solution)/shard_map/ppermute | solution.py:220
  16.7 2.7 %collective-permute-start.4 = (bf16[384,256]{1,0:T(8,128)(2,1)S(1)}, bf16[384,256]{1,0:T(8,128)(2,1)S(1)}, u32[]{:S(2)}, u32[]{:S(2)}) collective-permute-start(bf16[384,256]{1,0:T(8,128)(2,1)S(1)} %add_add_fusion.1), channel_id=1, source_target_pairs={{0,72},{62,102},{16,118},{12,140},{250,162},{88,68},{230,246},{34,... | collective-permute-start | bytes 589832 | tf_op jit(solution)/shard_map/ppermute | solution.py:220
  17.4 2.0 %collective-permute-start.5 = (bf16[384,256]{1,0:T(8,128)(2,1)S(1)}, bf16[384,256]{1,0:T(8,128)(2,1)S(1)}, u32[]{:S(2)}, u32[]{:S(2)}) collective-permute-start(bf16[384,256]{1,0:T(8,128)(2,1)S(1)} %add_add_fusion.1), channel_id=1, source_target_pairs={{0,28},{62,216},{16,178},{12,174},{250,234},{88,144},{230,196},{34... | collective-permute-start | bytes 589832 | tf_op jit(solution)/shard_map/ppermute | solution.py:220
  18.1 13.1 %collective-permute-start.6 = (bf16[384,256]{1,0:T(8,128)(2,1)S(1)}, bf16[384,256]{1,0:T(8,128)(2,1)S(1)}, u32[]{:S(2)}, u32[]{:S(2)}) collective-permute-start(bf16[384,256]{1,0:T(8,128)(2,1)S(1)} %add_add_fusion.1), channel_id=1, source_target_pairs={{0,200},{62,156},{16,46},{12,84},{250,212},{88,128},{230,190},{34,... | collective-permute-start | bytes 589832 | tf_op jit(solution)/shard_map/ppermute | solution.py:220
  31.2 9.0 %collective-permute-start.7 = (bf16[384,256]{1,0:T(8,128)(2,1)S(1)}, bf16[384,256]{1,0:T(8,128)(2,1)S(1)}, u32[]{:S(2)}, u32[]{:S(2)}) collective-permute-start(bf16[384,256]{1,0:T(8,128)(2,1)S(1)} %add_add_fusion.refs_0_), channel_id=1, source_target_pairs={{230,0},{234,12},{246,16},{250,28},{68,34},{72,46},{84,50},{88,62}... | collective-permute-start | bytes 589832 | tf_op jit(solution)/shard_map/ppermute | solution.py:220
  31.3 8.9 %collective-permute-start.8 = (bf16[384,256]{1,0:T(8,128)(2,1)S(1)}, bf16[384,256]{1,0:T(8,128)(2,1)S(1)}, u32[]{:S(2)}, u32[]{:S(2)}) collective-permute-start(bf16[384,256]{1,0:T(8,128)(2,1)S(1)} %add_add_fusion.refs_0_), channel_id=1, source_target_pairs={{12,0},{0,12},{28,16},{16,28},{46,34},{34,46},{62,50},{50,62},{72,... | collective-permute-start | bytes 589832 | tf_op jit(solution)/shard_map/ppermute | solution.py:220
  32.1 11.1 %collective-permute-start.9 = (bf16[384,256]{1,0:T(8,128)(2,1)S(1)}, bf16[384,256]{1,0:T(8,128)(2,1)S(1)}, u32[]{:S(2)}, u32[]{:S(2)}) collective-permute-start(bf16[384,256]{1,0:T(8,128)(2,1)S(1)} %add_add_fusion.refs_0_), channel_id=1, source_target_pairs={{234,0},{230,12},{250,16},{246,28},{72,34},{68,46},{88,50},{84,62}... | collective-permute-start | bytes 589832 | tf_op jit(solution)/shard_map/ppermute | solution.py:220
  43.8 16.3 %collective-permute-start.13 = (bf16[1536,256]{1,0:T(8,128)(2,1)S(1)}, bf16[1536,256]{1,0:T(8,128)(2,1)S(1)}, u32[]{:S(2)}, u32[]{:S(2)}) collective-permute-start(bf16[1536,256]{1,0:T(8,128)(2,1)S(1)} %shard_map.77.source), channel_id=1, source_target_pairs={{0,32},{1,225},{2,34},{3,227},{4,36},{5,229},{6,38},{7,231},{8,40}... | collective-permute-start | bytes 2359304 | tf_op jit(solution)/shard_map/ppermute | solution.py:220
  45.7 15.8 %collective-permute-start.12 = (bf16[1536,256]{1,0:T(8,128)(2,1)S(1)}, bf16[1536,256]{1,0:T(8,128)(2,1)S(1)}, u32[]{:S(2)}, u32[]{:S(2)}) collective-permute-start(bf16[1536,256]{1,0:T(8,128)(2,1)S(1)} %shard_map.77.source), channel_id=1, source_target_pairs={{0,8},{1,25},{2,10},{3,27},{4,12},{5,29},{6,14},{7,31},{8,16},{9,1... | collective-permute-start | bytes 2359304 | tf_op jit(solution)/shard_map/ppermute | solution.py:220
  50.0 13.0 %collective-permute-start.11 = (bf16[1536,256]{1,0:T(8,128)(2,1)S(1)}, bf16[1536,256]{1,0:T(8,128)(2,1)S(1)}, u32[]{:S(2)}, u32[]{:S(2)}) collective-permute-start(bf16[1536,256]{1,0:T(8,128)(2,1)S(1)} %shard_map.77.source), channel_id=1, source_target_pairs={{0,2},{1,7},{2,4},{3,1},{4,6},{5,3},{6,0},{7,5},{8,10},{9,15},{10,... | collective-permute-start | bytes 2359304 | tf_op jit(solution)/shard_map/ppermute | solution.py:220
  63.8 2.4 %copy-start = (bf16[1536,256]{1,0:T(8,128)(2,1)S(1)}, bf16[1536,256]{1,0:T(8,128)(2,1)}, u32[]{:S(2)}) copy-start(bf16[1536,256]{1,0:T(8,128)(2,1)} %features.5) | copy-start | bytes 2359300
  63.8 2.4 %copy-start.1 = (bf16[256,256]{1,0:T(8,128)(2,1)S(1)}, bf16[256,256]{1,0:T(8,128)(2,1)}, u32[]{:S(2)}) copy-start(bf16[256,256]{1,0:T(8,128)(2,1)} %weight.3) | copy-start | bytes 393220
  63.8 2.4 %copy-start.2 = (s32[1536]{0:T(1024)S(1)}, s32[1536]{0:T(1024)}, u32[]{:S(2)}) copy-start(s32[1536]{0:T(1024)} %param.8) | copy-start | bytes 18436
  63.8 2.4 %collective-permute-start.15 = (f32[768,256]{1,0:T(8,128)S(1)}, f32[768,256]{1,0:T(8,128)S(1)}, u32[]{:S(2)}, u32[]{:S(2)}) collective-permute-start(f32[768,256]{1,0:T(8,128)S(1)} %shard_map.83.mine), channel_id=1, source_target_pairs={{0,1},{1,0},{2,3},{3,2},{4,5},{5,4},{6,7},{7,6},{8,9},{9,8},{10,11... | collective-permute-start | bytes 2359304 | tf_op jit(solution)/shard_map/ppermute | solution.py:220
  64.7 2.7 %collective-permute-start.14 = (f32[768,256]{1,0:T(8,128)S(1)}, f32[768,256]{1,0:T(8,128)S(1)}, u32[]{:S(2)}, u32[]{:S(2)}) collective-permute-start(f32[768,256]{1,0:T(8,128)S(1)} %shard_map.82.mine), channel_id=1, source_target_pairs={{0,1},{1,0},{2,3},{3,2},{4,5},{5,4},{6,7},{7,6},{8,9},{9,8},{10,11... | collective-permute-start | bytes 2359304 | tf_op jit(solution)/shard_map/ppermute | solution.py:220

commit v4 on v3

--- a/solution.py
+++ b/solution.py
@@ -181,32 +181,51 @@
     )(*args)
 
 
-def finish_kernel(start, mine, other, degrees, features, weight, *refs):
-    *_, out, done, sem = refs
-    rows = pl.ds(start, mine.shape[0])
+def finish_rows(i, start, mine, other, inverse, features, weight, done):
+    size = inverse.shape[0]
+    here = pl.ds(i * size, size)
+    column = start // size + i
+    total = (mine[here, :] + other[here, :]) * inverse[:, column : column + 1]
+    combined = total + features[pl.ds(start + i * size, size), :].astype(jnp.float32)
+    result = jnp.dot(combined.astype(jnp.bfloat16), weight[...], preferred_element_type=jnp.float32)
+    done[here, :] = jnp.maximum(result, 0.0).astype(done.dtype)
+
+
+def finish_first_kernel(mine, other, degrees, features, weight, done):
     inverse = inverse_columns(degrees)
-    size = degrees.shape[1]
-    for i in range(mine.shape[0] // size):
-        here = pl.ds(i * size, size)
-        column = start // size + i
-        total = (mine[here, :] + other[here, :]) * inverse[:, column : column + 1]
-        combined = total + features[pl.ds(start + i * size, size), :].astype(jnp.float32)
-        result = jnp.dot(combined.astype(jnp.bfloat16), weight[...], preferred_element_type=jnp.float32)
-        done[here, :] = jnp.maximum(result, 0.0).astype(done.dtype)
-    copy = pltpu.make_async_copy(done, out.at[rows], sem)
-    copy.start()
-    copy.wait()
-
-
-def finish(part, mine, other, degrees, features, weight, before=None):
-    args = [mine, other, degrees, features, weight] + ([] if before is None else [before])
+    for i in range(mine.shape[0] // inverse.shape[0]):
+        finish_rows(i, 0, mine, other, inverse, features, weight, done)
+
+
+def finish_second_kernel(mine, other, degrees, features, weight, first, out, done, sems):
+    half, size = mine.shape[0], degrees.shape[1]
+    copies = [pltpu.make_async_copy(first, out.at[pl.ds(0, half)], sems.at[half // size])]
+    copies[0].start()
+    inverse = inverse_columns(degrees)
+    for i in range(half // size):
+        finish_rows(i, half, mine, other, inverse, features, weight, done)
+        group = done.at[pl.ds(i * size, size)]
+        copies.append(pltpu.make_async_copy(group, out.at[pl.ds(half + i * size, size)], sems.at[i]))
+        copies[-1].start()
+    for copy in copies:
+        copy.wait()
+
+
+def finish(mine, other, degrees, features, weight, first=None):
+    half = jax.ShapeDtypeStruct(mine.shape, jnp.bfloat16)
+    last = first is not None
+    args = [mine, other, degrees, features, weight] + ([first] if last else [])
     return pl.pallas_call(
-        functools.partial(finish_kernel, part * mine.shape[0]),
-        out_shape=jax.ShapeDtypeStruct(features.shape, jnp.bfloat16),
-        in_specs=[VMEM] * 5 + [HBM] * (len(args) - 5),
-        out_specs=HBM,
-        scratch_shapes=[pltpu.VMEM(mine.shape, jnp.bfloat16), pltpu.SemaphoreType.DMA],
-        input_output_aliases={} if before is None else {5: 0},
+        finish_second_kernel if last else finish_first_kernel,
+        out_shape=jax.ShapeDtypeStruct(features.shape, jnp.bfloat16) if last else half,
+        in_specs=[VMEM] * len(args),
+        out_specs=HBM if last else VMEM,
+        scratch_shapes=[
+            pltpu.VMEM(half.shape, half.dtype),
+            pltpu.SemaphoreType.DMA((mine.shape[0] // degrees.shape[1] + 1,)),
+        ]
+        if last
+        else [],
         compiler_params=pltpu.CompilerParams(vmem_limit_bytes=12 * 2**20),
         cost_estimate=pl.CostEstimate(
             flops=2 * mine.size * weight.shape[1], bytes_accessed=mine.size * 12, transcendentals=0
@@ -254,7 +273,7 @@
     piece = jnp.where(fact[0] == 1, cut[0], jnp.zeros_like(cut[0]))
     for got in [send(cut[i], pairs) for i, pairs in enumerate(scatter)]:
         piece = piece + got
-    kept = piece
+    table, kept = lax.optimization_barrier((table, piece))
     for got in [send(kept, pairs) for pairs in spread]:
         piece = piece + got
     pieces = [piece] + [send(piece, pairs) for pairs in gather]
@@ -282,8 +301,8 @@
         total = multiply(mat, block, total)
     parts = [multiply(mats[-1], traded[-1], total, part) for part in range(2)]
     others = [send(part, swap) for part in parts]
-    result = finish(0, parts[0], others[0], degrees, features, weight)
-    return finish(1, parts[1], others[1], degrees, features, weight, result)
+    result = finish(parts[0], others[0], degrees, features, weight)
+    return finish(parts[1], others[1], degrees, features, weight, result)
 
 
 def solution(mesh):

time: 69.6 us -> 68.9 us (0.990)
  Pallas kernels: 16.6 us -> 13.7 us
  starting transfers between devices: 26.9 us -> 28.6 us
    pallas_call x1, Pallas kernels: 6.19 us -> 4.12 us  [on_device(): pl.pallas_call(prepare_kernel, out_shape=[matrix] * COLORS, in_specs=[SME...]
    ppermute x16, starting transfers between devices: 26.9 us -> 28.6 us  [on_device(): send = lambda x, pairs: lax.ppermute(x, AXES, pairs)]
    pallas_call x2, Pallas kernels: 2.45 us -> 1.66 us  [finish(): pl.pallas_call(finish_second_kernel if last else finish_first_kernel, out...]
  transfers between devices with their start and end apart: 16 -> 16, of which waited for: 6 -> 8; matrix products, arithmetic and copies ran while one was open for 3% -> 3% of each run, Pallas kernels for 21% -> 17%
where the time goes in v4:
time: 68.9 us; the launch traced here: 67.9 us
  starting transfers between devices  28.6 us (42%)
  waiting for transfers between devices  23.3 us (34%)
  Pallas kernels  13.7 us (20%)
  local copies, waits for them, and re-layouts  1.11 us (2%)
  other arithmetic  0.87 us (1%)
    ppermute x16, starting transfers between devices, on_device(): send = lambda x, pairs: lax.ppermute(x, AXES, pairs)  28.6 us
    ppermute x16, waiting for transfers between devices, on_device(): send = lambda x, pairs: lax.ppermute(x, AXES, pairs)  23.3 us
    pallas_call x5, Pallas kernels, multiply(): pl.pallas_call(kernel, out_shape=jax.ShapeDtypeStruct((height, width), jn...  5.87 us
    pallas_call x1, Pallas kernels, on_device(): pl.pallas_call(prepare_kernel, out_shape=[matrix] * COLORS, in_specs=[SME...  4.12 us
    pallas_call x2, Pallas kernels, finish(): pl.pallas_call(finish_second_kernel if last else finish_first_kernel, out...  1.66 us
    pallas_call x1, Pallas kernels, on_device(): pl.pallas_call(functools.partial(scale_kernel, blocks), out_shape=[jax.Sh...  1.45 us
  transfers between devices with their start and end apart: 16, of which 8 were waited for; matrix products, arithmetic and copies ran while one was open for 3% of the time, Pallas kernels for 17%

profile of v4, /device:TPU:1, one launch (start us, length us, event | category | flops | bytes accessed | tf_op | source)
XLA Modules:
  0.0 67.9 jit_solution(2677779921824506636)
XLA Ops:
  0.0 3.2 %collective-permute-start.10 = (bf16[8,11,256,256]{3,2,1,0:T(8,128)(2,1)}, bf16[8,11,256,256]{3,2,1,0:T(8,128)(2,1)}, u32[]{:S(2)}, u32[]{:S(2)}) collective-permute-start(bf16[8,11,256,256]{3,2,1,0:T(8,128)(2,1)} %bitcast.15), channel_id=1, source_target_pairs={{0,1},{1,0},{2,3},{3,2},{4,5},{5,4},{6,7},{7,6},{8,9},{9,8},{10,11... | collective-permute-start | bytes 34603016 | tf_op jit(solution)/shard_map/ppermute | solution.py:239
  3.2 1.5 %shard_map.76 = (bf16[384,256]{1,0:T(8,128)(2,1)S(1)}, bf16[384,256]{1,0:T(8,128)(2,1)S(1)}, bf16[384,256]{1,0:T(8,128)(2,1)S(1)}, bf16[384,256]{1,0:T(8,128)(2,1)S(1)}) custom-call(bf16[1536,256]{1,0:T(8,128)(2,1)} %features.5, s32[12,128]{1,0:T(8,128)} %bitcast.12), custom_call_target="tpu_custom_call" | custom-call | tf_op jit(solution)/shard_map/pallas_call | solution.py:254
  4.7 0.7 collective-permute-start
  5.4 2.5 %collective-permute-start.1 = (bf16[384,256]{1,0:T(8,128)(2,1)S(1)}, bf16[384,256]{1,0:T(8,128)(2,1)S(1)}, u32[]{:S(2)}, u32[]{:S(2)}) collective-permute-start(bf16[384,256]{1,0:T(8,128)(2,1)S(1)} %get-tuple-element.18), channel_id=1, source_target_pairs={{0,16},{1,12},{129,133},{128,147},{32,48},{33,60},{161,165},{160,1... | collective-permute-start | bytes 589832 | tf_op jit(solution)/shard_map/ppermute | solution.py:239
  7.9 2.0 %collective-permute-start.2 = (bf16[384,256]{1,0:T(8,128)(2,1)S(1)}, bf16[384,256]{1,0:T(8,128)(2,1)S(1)}, u32[]{:S(2)}, u32[]{:S(2)}) collective-permute-start(bf16[384,256]{1,0:T(8,128)(2,1)S(1)} %get-tuple-element.19), channel_id=1, source_target_pairs={{0,250},{1,88},{129,111},{128,199},{32,10},{33,104},{161,139},{160... | collective-permute-start | bytes 589832 | tf_op jit(solution)/shard_map/ppermute | solution.py:239
  9.9 1.3 %collective-permute-start.3 = (bf16[384,256]{1,0:T(8,128)(2,1)S(1)}, bf16[384,256]{1,0:T(8,128)(2,1)S(1)}, u32[]{:S(2)}, u32[]{:S(2)}) collective-permute-start(bf16[384,256]{1,0:T(8,128)(2,1)S(1)} %get-tuple-element.20), channel_id=1, source_target_pairs={{0,230},{1,34},{129,121},{128,169},{32,6},{33,66},{161,153},{160,2... | collective-permute-start | bytes 589832 | tf_op jit(solution)/shard_map/ppermute | solution.py:239
  11.2 0.8 %fusion.2 = (s32[1,8,22]{2,1,0:T(8,128)S(1)}, s32[1,8,22]{2,1,0:T(8,128)S(1)}) fusion(s32[1,8,22]{2,1,0:T(8,128)} %param.11, s32[8]{0:T(128)} %bitcast.21), kind=kLoop, calls=%fused_computation.9 | loop fusion | flops 2816 | bytes 2144 | tf_op jit(solution)/shard_map/mul | solution.py:269
  12.3 0.7 %constant_dynamic-slice_fusion = s32[1,9]{1,0:T(1,128)S(1)} fusion(s32[256,9]{1,0:T(8,128)} %constant.45.clone, s32[]{:T(128)S(6)} %select_n.39), kind=kLoop, calls=%fused_computation.16 | loop fusion | bytes 76 | tf_op jit(solution)/shard_map/jit(dynamic_index_in_dim)/dynamic_slice | solution.py:245
  13.1 1.2 %collective-permute-done.2 = bf16[384,256]{1,0:T(8,128)(2,1)S(1)} collective-permute-done((bf16[384,256]{1,0:T(8,128)(2,1)S(1)}, bf16[384,256]{1,0:T(8,128)(2,1)S(1)}, u32[]{:S(2)}, u32[]{:S(2)}) %collective-permute-start.2) | collective-permute-done | bytes 196640 | tf_op jit(solution)/shard_map/ppermute | solution.py:239
  14.3 2.4 %collective-permute-done.3 = bf16[384,256]{1,0:T(8,128)(2,1)S(1)} collective-permute-done((bf16[384,256]{1,0:T(8,128)(2,1)S(1)}, bf16[384,256]{1,0:T(8,128)(2,1)S(1)}, u32[]{:S(2)}, u32[]{:S(2)}) %collective-permute-start.3) | collective-permute-done | bytes 196640 | tf_op jit(solution)/shard_map/ppermute | solution.py:239
  16.8 0.7 collective-permute-start.4
  17.4 0.7 collective-permute-start.5
  18.1 1.3 %collective-permute-start.6 = (bf16[384,256]{1,0:T(8,128)(2,1)S(1)}, bf16[384,256]{1,0:T(8,128)(2,1)S(1)}, u32[]{:S(2)}, u32[]{:S(2)}) collective-permute-start(bf16[384,256]{1,0:T(8,128)(2,1)S(1)} %add_add_fusion.1), channel_id=1, source_target_pairs={{0,200},{62,156},{16,46},{12,84},{250,212},{88,128},{230,190},{34,... | collective-permute-start | bytes 589832 | tf_op jit(solution)/shard_map/ppermute | solution.py:239
  19.4 11.8 %collective-permute-done.6 = bf16[384,256]{1,0:T(8,128)(2,1)S(1)} collective-permute-done((bf16[384,256]{1,0:T(8,128)(2,1)S(1)}, bf16[384,256]{1,0:T(8,128)(2,1)S(1)}, u32[]{:S(2)}, u32[]{:S(2)}) %collective-permute-start.6) | collective-permute-done | bytes 196640 | tf_op jit(solution)/shard_map/ppermute | solution.py:239
  31.3 0.7 %collective-permute-start.8 = (bf16[384,256]{1,0:T(8,128)(2,1)S(1)}, bf16[384,256]{1,0:T(8,128)(2,1)S(1)}, u32[]{:S(2)}, u32[]{:S(2)}) collective-permute-start(bf16[384,256]{1,0:T(8,128)(2,1)S(1)} %add_add_fusion.refs_0_), channel_id=1, source_target_pairs={{12,0},{0,12},{28,16},{16,28},{46,34},{34,46},{62,50},{50,62},{72,... | collective-permute-start | bytes 589832 | tf_op jit(solution)/shard_map/ppermute | solution.py:239
  32.1 5.5 %collective-permute-start.9 = (bf16[384,256]{1,0:T(8,128)(2,1)S(1)}, bf16[384,256]{1,0:T(8,128)(2,1)S(1)}, u32[]{:S(2)}, u32[]{:S(2)}) collective-permute-start(bf16[384,256]{1,0:T(8,128)(2,1)S(1)} %add_add_fusion.refs_0_), channel_id=1, source_target_pairs={{234,0},{230,12},{250,16},{246,28},{72,34},{68,46},{88,50},{84,62}... | collective-permute-start | bytes 589832 | tf_op jit(solution)/shard_map/ppermute | solution.py:239
  37.7 2.6 %collective-permute-done.7.refs_1_ = bf16[384,256]{1,0:T(8,128)(2,1)S(1)} collective-permute-done((bf16[384,256]{1,0:T(8,128)(2,1)S(1)}, bf16[384,256]{1,0:T(8,128)(2,1)S(1)}, u32[]{:S(2)}, u32[]{:S(2)}) %collective-permute-start.7) | collective-permute-done | bytes 196640 | tf_op jit(solution)/shard_map/ppermute | solution.py:239
  40.2 3.0 %collective-permute-done.9.refs_3_ = bf16[384,256]{1,0:T(8,128)(2,1)S(1)} collective-permute-done((bf16[384,256]{1,0:T(8,128)(2,1)S(1)}, bf16[384,256]{1,0:T(8,128)(2,1)S(1)}, u32[]{:S(2)}, u32[]{:S(2)}) %collective-permute-start.9) | collective-permute-done | bytes 196640 | tf_op jit(solution)/shard_map/ppermute | solution.py:239
  43.8 1.9 %collective-permute-start.13 = (bf16[1536,256]{1,0:T(8,128)(2,1)S(1)}, bf16[1536,256]{1,0:T(8,128)(2,1)S(1)}, u32[]{:S(2)}, u32[]{:S(2)}) collective-permute-start(bf16[1536,256]{1,0:T(8,128)(2,1)S(1)} %shard_map.77.source), channel_id=1, source_target_pairs={{0,32},{1,225},{2,34},{3,227},{4,36},{5,229},{6,38},{7,231},{8,40}... | collective-permute-start | bytes 2359304 | tf_op jit(solution)/shard_map/ppermute | solution.py:239
  45.7 3.3 %collective-permute-start.12 = (bf16[1536,256]{1,0:T(8,128)(2,1)S(1)}, bf16[1536,256]{1,0:T(8,128)(2,1)S(1)}, u32[]{:S(2)}, u32[]{:S(2)}) collective-permute-start(bf16[1536,256]{1,0:T(8,128)(2,1)S(1)} %shard_map.77.source), channel_id=1, source_target_pairs={{0,8},{1,25},{2,10},{3,27},{4,12},{5,29},{6,14},{7,31},{8,16},{9,1... | collective-permute-start | bytes 2359304 | tf_op jit(solution)/shard_map/ppermute | solution.py:239
  49.1 2.3 %collective-permute-start.11 = (bf16[1536,256]{1,0:T(8,128)(2,1)S(1)}, bf16[1536,256]{1,0:T(8,128)(2,1)S(1)}, u32[]{:S(2)}, u32[]{:S(2)}) collective-permute-start(bf16[1536,256]{1,0:T(8,128)(2,1)S(1)} %shard_map.77.source), channel_id=1, source_target_pairs={{0,2},{1,7},{2,4},{3,1},{4,6},{5,3},{6,0},{7,5},{8,10},{9,15},{10,... | collective-permute-start | bytes 2359304 | tf_op jit(solution)/shard_map/ppermute | solution.py:239
  51.4 4.1 %shard_map.78 = (bf16[1536,1536]{1,0:T(8,128)(2,1)S(1)}, bf16[1536,1536]{1,0:T(8,128)(2,1)S(1)}, bf16[1536,1536]{1,0:T(8,128)(2,1)S(1)}, bf16[1536,1536]{1,0:T(8,128)(2,1)S(1)}) custom-call(s32[4]{0:T(128)S(1)} %get-tuple-element.22.order, s32[352]{0:T(512)S(1)} %reshape.51.table, bf16[8,11,256,256]{3,2,1,0:T(8,128)(2,1)} %bitcast.16, ...), custom_call_target="tpu_custom_call" | custom-call | bytes 23068672 | tf_op jit(solution)/shard_map/pallas_call | solution.py:290
  55.5 1.4 %shard_map.79.refs_0_ = f32[1536,256]{1,0:T(8,128)S(1)} custom-call(bf16[1536,1536]{1,0:T(8,128)(2,1)S(1)} %get-tuple-element.28.mat, bf16[1536,256]{1,0:T(8,128)(2,1)S(1)} %shard_map.77.source), custom_call_target="tpu_custom_call" | custom-call | flops 1207959552 | bytes 4718592 | tf_op jit(solution)/shard_map/pallas_call | solution.py:171
  56.9 0.6 collective-permute-done.13.source
  57.6 1.5 %shard_map.80.refs_0_ = f32[1536,256]{1,0:T(8,128)S(1)} custom-call(bf16[1536,1536]{1,0:T(8,128)(2,1)S(1)} %get-tuple-element.27.mat, bf16[1536,256]{1,0:T(8,128)(2,1)S(1)} %collective-permute-done.13.source, f32[1536,256]{1,0:T(8,128)S(1)} %shard_map.79.refs_0_), custom_call_target="tpu_custom_call", output_to_operand_aliasing={{}: (2, {})} | custom-call | flops 1207959552 | bytes 4718592 | tf_op jit(solution)/shard_map/pallas_call | solution.py:171
  59.0 1.5 %shard_map.81.before = f32[1536,256]{1,0:T(8,128)S(1)} custom-call(bf16[1536,1536]{1,0:T(8,128)(2,1)S(1)} %get-tuple-element.26.mat, bf16[1536,256]{1,0:T(8,128)(2,1)S(1)} %collective-permute-done.12.source, f32[1536,256]{1,0:T(8,128)S(1)} %shard_map.80.refs_0_), custom_call_target="tpu_custom_call", output_to_operand_aliasing={{}: (2, {})} | custom-call | flops 1207959552 | bytes 4718592 | tf_op jit(solution)/shard_map/pallas_call | solution.py:171
  60.5 0.8 %shard_map.83.mine = f32[768,256]{1,0:T(8,128)S(1)} custom-call(bf16[1536,1536]{1,0:T(8,128)(2,1)S(1)} %get-tuple-element.24.mat, bf16[1536,256]{1,0:T(8,128)(2,1)S(1)} %collective-permute-done.11.source, f32[1536,256]{1,0:T(8,128)S(1)} %shard_map.81.before), custom_call_target="tpu_custom_call" | custom-call | flops 603979776 | bytes 4718592 | tf_op jit(solution)/shard_map/pallas_call | solution.py:171
  61.3 2.2 %collective-permute-start.15 = (f32[768,256]{1,0:T(8,128)S(1)}, f32[768,256]{1,0:T(8,128)S(1)}, u32[]{:S(2)}, u32[]{:S(2)}) collective-permute-start(f32[768,256]{1,0:T(8,128)S(1)} %shard_map.83.mine), channel_id=1, source_target_pairs={{0,1},{1,0},{2,3},{3,2},{4,5},{5,4},{6,7},{7,6},{8,9},{9,8},{10,11... | collective-permute-start | bytes 2359304 | tf_op jit(solution)/shard_map/ppermute | solution.py:239
  63.5 0.8 %shard_map.82.mine = f32[768,256]{1,0:T(8,128)S(1)} custom-call(bf16[1536,1536]{1,0:T(8,128)(2,1)S(1)} %get-tuple-element.24.mat, bf16[1536,256]{1,0:T(8,128)(2,1)S(1)} %collective-permute-done.11.source, f32[1536,256]{1,0:T(8,128)S(1)} %shard_map.81.before), custom_call_target="tpu_custom_call" | custom-call | flops 603979776 | bytes 4718592 | tf_op jit(solution)/shard_map/pallas_call | solution.py:171
  64.4 1.0 %collective-permute-done.15.other = f32[768,256]{1,0:T(8,128)S(1)} collective-permute-done((f32[768,256]{1,0:T(8,128)S(1)}, f32[768,256]{1,0:T(8,128)S(1)}, u32[]{:S(2)}, u32[]{:S(2)}) %collective-permute-start.15) | collective-permute-done | bytes 786464 | tf_op jit(solution)/shard_map/ppermute | solution.py:239
  65.9 0.8 %collective-permute-done.14.other = f32[768,256]{1,0:T(8,128)S(1)} collective-permute-done((f32[768,256]{1,0:T(8,128)S(1)}, f32[768,256]{1,0:T(8,128)S(1)}, u32[]{:S(2)}, u32[]{:S(2)}) %collective-permute-start.14) | collective-permute-done | bytes 786464 | tf_op jit(solution)/shard_map/ppermute | solution.py:239
  66.7 1.2 %shard_map.85 = bf16[1536,256]{1,0:T(8,128)(2,1)} custom-call(f32[768,256]{1,0:T(8,128)S(1)} %shard_map.82.mine, f32[768,256]{1,0:T(8,128)S(1)} %collective-permute-done.14.other, s32[12,128]{1,0:T(8,128)S(1)} %bitcast.14, bf16[1536,256]{1,0:T(8,128)(2,1)S(1)} %copy-done, bf16[256,256]{1,0:T(8,128)(2,1)S(1)} %copy-done.1, bf16[768,256]{1,0:T(8,128)(2,1)S(1)} %shard_map.84.first), custom_call_target="tpu_custom_call" | custom-call | flops 100663296 | bytes 2359296 | tf_op jit(solution)/shard_map/pallas_call | solution.py:218
  (28 shorter events, 1.8 us)
Async XLA Ops:
  0.0 51.4 %collective-permute-start.10 = (bf16[8,11,256,256]{3,2,1,0:T(8,128)(2,1)}, bf16[8,11,256,256]{3,2,1,0:T(8,128)(2,1)}, u32[]{:S(2)}, u32[]{:S(2)}) collective-permute-start(bf16[8,11,256,256]{3,2,1,0:T(8,128)(2,1)} %bitcast.15), channel_id=1, source_target_pairs={{0,1},{1,0},{2,3},{3,2},{4,5},{5,4},{6,7},{7,6},{8,9},{9,8},{10,11... | collective-permute-start | bytes 34603016 | tf_op jit(solution)/shard_map/ppermute | solution.py:239
  4.7 8.4 %collective-permute-start = (bf16[384,256]{1,0:T(8,128)(2,1)S(1)}, bf16[384,256]{1,0:T(8,128)(2,1)S(1)}, u32[]{:S(2)}, u32[]{:S(2)}) collective-permute-start(bf16[384,256]{1,0:T(8,128)(2,1)S(1)} %get-tuple-element.17), channel_id=1, source_target_pairs={{0,62},{129,191},{32,78},{161,219},{64,58},{193,175},{96,74},{225,... | collective-permute-start | bytes 589832 | tf_op jit(solution)/shard_map/ppermute | solution.py:239
  5.4 7.7 %collective-permute-start.1 = (bf16[384,256]{1,0:T(8,128)(2,1)S(1)}, bf16[384,256]{1,0:T(8,128)(2,1)S(1)}, u32[]{:S(2)}, u32[]{:S(2)}) collective-permute-start(bf16[384,256]{1,0:T(8,128)(2,1)S(1)} %get-tuple-element.18), channel_id=1, source_target_pairs={{0,16},{1,12},{129,133},{128,147},{32,48},{33,60},{161,165},{160,1... | collective-permute-start | bytes 589832 | tf_op jit(solution)/shard_map/ppermute | solution.py:239
  7.9 6.4 %collective-permute-start.2 = (bf16[384,256]{1,0:T(8,128)(2,1)S(1)}, bf16[384,256]{1,0:T(8,128)(2,1)S(1)}, u32[]{:S(2)}, u32[]{:S(2)}) collective-permute-start(bf16[384,256]{1,0:T(8,128)(2,1)S(1)} %get-tuple-element.19), channel_id=1, source_target_pairs={{0,250},{1,88},{129,111},{128,199},{32,10},{33,104},{161,139},{160... | collective-permute-start | bytes 589832 | tf_op jit(solution)/shard_map/ppermute | solution.py:239
  9.9 6.8 %collective-permute-start.3 = (bf16[384,256]{1,0:T(8,128)(2,1)S(1)}, bf16[384,256]{1,0:T(8,128)(2,1)S(1)}, u32[]{:S(2)}, u32[]{:S(2)}) collective-permute-start(bf16[384,256]{1,0:T(8,128)(2,1)S(1)} %get-tuple-element.20), channel_id=1, source_target_pairs={{0,230},{1,34},{129,121},{128,169},{32,6},{33,66},{161,153},{160,2... | collective-permute-start | bytes 589832 | tf_op jit(solution)/shard_map/ppermute | solution.py:239
  16.8 2.7 %collective-permute-start.4 = (bf16[384,256]{1,0:T(8,128)(2,1)S(1)}, bf16[384,256]{1,0:T(8,128)(2,1)S(1)}, u32[]{:S(2)}, u32[]{:S(2)}) collective-permute-start(bf16[384,256]{1,0:T(8,128)(2,1)S(1)} %add_add_fusion.1), channel_id=1, source_target_pairs={{0,72},{62,102},{16,118},{12,140},{250,162},{88,68},{230,246},{34,... | collective-permute-start | bytes 589832 | tf_op jit(solution)/shard_map/ppermute | solution.py:239
  17.4 2.0 %collective-permute-start.5 = (bf16[384,256]{1,0:T(8,128)(2,1)S(1)}, bf16[384,256]{1,0:T(8,128)(2,1)S(1)}, u32[]{:S(2)}, u32[]{:S(2)}) collective-permute-start(bf16[384,256]{1,0:T(8,128)(2,1)S(1)} %add_add_fusion.1), channel_id=1, source_target_pairs={{0,28},{62,216},{16,178},{12,174},{250,234},{88,144},{230,196},{34... | collective-permute-start | bytes 589832 | tf_op jit(solution)/shard_map/ppermute | solution.py:239
  18.1 13.1 %collective-permute-start.6 = (bf16[384,256]{1,0:T(8,128)(2,1)S(1)}, bf16[384,256]{1,0:T(8,128)(2,1)S(1)}, u32[]{:S(2)}, u32[]{:S(2)}) collective-permute-start(bf16[384,256]{1,0:T(8,128)(2,1)S(1)} %add_add_fusion.1), channel_id=1, source_target_pairs={{0,200},{62,156},{16,46},{12,84},{250,212},{88,128},{230,190},{34,... | collective-permute-start | bytes 589832 | tf_op jit(solution)/shard_map/ppermute | solution.py:239
  31.2 9.0 %collective-permute-start.7 = (bf16[384,256]{1,0:T(8,128)(2,1)S(1)}, bf16[384,256]{1,0:T(8,128)(2,1)S(1)}, u32[]{:S(2)}, u32[]{:S(2)}) collective-permute-start(bf16[384,256]{1,0:T(8,128)(2,1)S(1)} %add_add_fusion.refs_0_), channel_id=1, source_target_pairs={{230,0},{234,12},{246,16},{250,28},{68,34},{72,46},{84,50},{88,62}... | collective-permute-start | bytes 589832 | tf_op jit(solution)/shard_map/ppermute | solution.py:239
  31.3 8.9 %collective-permute-start.8 = (bf16[384,256]{1,0:T(8,128)(2,1)S(1)}, bf16[384,256]{1,0:T(8,128)(2,1)S(1)}, u32[]{:S(2)}, u32[]{:S(2)}) collective-permute-start(bf16[384,256]{1,0:T(8,128)(2,1)S(1)} %add_add_fusion.refs_0_), channel_id=1, source_target_pairs={{12,0},{0,12},{28,16},{16,28},{46,34},{34,46},{62,50},{50,62},{72,... | collective-permute-start | bytes 589832 | tf_op jit(solution)/shard_map/ppermute | solution.py:239
  32.1 11.1 %collective-permute-start.9 = (bf16[384,256]{1,0:T(8,128)(2,1)S(1)}, bf16[384,256]{1,0:T(8,128)(2,1)S(1)}, u32[]{:S(2)}, u32[]{:S(2)}) collective-permute-start(bf16[384,256]{1,0:T(8,128)(2,1)S(1)} %add_add_fusion.refs_0_), channel_id=1, source_target_pairs={{234,0},{230,12},{250,16},{246,28},{72,34},{68,46},{88,50},{84,62}... | collective-permute-start | bytes 589832 | tf_op jit(solution)/shard_map/ppermute | solution.py:239
  43.8 13.8 %collective-permute-start.13 = (bf16[1536,256]{1,0:T(8,128)(2,1)S(1)}, bf16[1536,256]{1,0:T(8,128)(2,1)S(1)}, u32[]{:S(2)}, u32[]{:S(2)}) collective-permute-start(bf16[1536,256]{1,0:T(8,128)(2,1)S(1)} %shard_map.77.source), channel_id=1, source_target_pairs={{0,32},{1,225},{2,34},{3,227},{4,36},{5,229},{6,38},{7,231},{8,40}... | collective-permute-start | bytes 2359304 | tf_op jit(solution)/shard_map/ppermute | solution.py:239
  45.7 13.3 %collective-permute-start.12 = (bf16[1536,256]{1,0:T(8,128)(2,1)S(1)}, bf16[1536,256]{1,0:T(8,128)(2,1)S(1)}, u32[]{:S(2)}, u32[]{:S(2)}) collective-permute-start(bf16[1536,256]{1,0:T(8,128)(2,1)S(1)} %shard_map.77.source), channel_id=1, source_target_pairs={{0,8},{1,25},{2,10},{3,27},{4,12},{5,29},{6,14},{7,31},{8,16},{9,1... | collective-permute-start | bytes 2359304 | tf_op jit(solution)/shard_map/ppermute | solution.py:239
  49.1 11.5 %collective-permute-start.11 = (bf16[1536,256]{1,0:T(8,128)(2,1)S(1)}, bf16[1536,256]{1,0:T(8,128)(2,1)S(1)}, u32[]{:S(2)}, u32[]{:S(2)}) collective-permute-start(bf16[1536,256]{1,0:T(8,128)(2,1)S(1)} %shard_map.77.source), channel_id=1, source_target_pairs={{0,2},{1,7},{2,4},{3,1},{4,6},{5,3},{6,0},{7,5},{8,10},{9,15},{10,... | collective-permute-start | bytes 2359304 | tf_op jit(solution)/shard_map/ppermute | solution.py:239
  61.3 4.1 %copy-start = (bf16[1536,256]{1,0:T(8,128)(2,1)S(1)}, bf16[1536,256]{1,0:T(8,128)(2,1)}, u32[]{:S(2)}) copy-start(bf16[1536,256]{1,0:T(8,128)(2,1)} %features.5) | copy-start | bytes 2359300
  61.3 4.1 %copy-start.1 = (bf16[256,256]{1,0:T(8,128)(2,1)S(1)}, bf16[256,256]{1,0:T(8,128)(2,1)}, u32[]{:S(2)}) copy-start(bf16[256,256]{1,0:T(8,128)(2,1)} %weight.3) | copy-start | bytes 393220
  61.3 4.1 %copy-start.2 = (s32[1536]{0:T(1024)S(1)}, s32[1536]{0:T(1024)}, u32[]{:S(2)}) copy-start(s32[1536]{0:T(1024)} %param.8) | copy-start | bytes 18436
  61.3 4.1 %collective-permute-start.15 = (f32[768,256]{1,0:T(8,128)S(1)}, f32[768,256]{1,0:T(8,128)S(1)}, u32[]{:S(2)}, u32[]{:S(2)}) collective-permute-start(f32[768,256]{1,0:T(8,128)S(1)} %shard_map.83.mine), channel_id=1, source_target_pairs={{0,1},{1,0},{2,3},{3,2},{4,5},{5,4},{6,7},{7,6},{8,9},{9,8},{10,11... | collective-permute-start | bytes 2359304 | tf_op jit(solution)/shard_map/ppermute | solution.py:239
  64.3 2.4 %collective-permute-start.14 = (f32[768,256]{1,0:T(8,128)S(1)}, f32[768,256]{1,0:T(8,128)S(1)}, u32[]{:S(2)}, u32[]{:S(2)}) collective-permute-start(f32[768,256]{1,0:T(8,128)S(1)} %shard_map.82.mine), channel_id=1, source_target_pairs={{0,1},{1,0},{2,3},{3,2},{4,5},{5,4},{6,7},{7,6},{8,9},{9,8},{10,11... | collective-permute-start | bytes 2359304 | tf_op jit(solution)/shard_map/ppermute | solution.py:239

commit v5 on v4

--- a/solution.py
+++ b/solution.py
@@ -166,8 +166,9 @@
     if part is None:
         kernel, alias = multiply_kernel, ({} if before is None else {2: 0})
     else:
-        height //= 2
-        kernel, alias = functools.partial(multiply_part_kernel, part * height), {}
+        start = part * (height * 2 // 3)
+        height = height // 3 if part else height * 2 // 3
+        kernel, alias = functools.partial(multiply_part_kernel, start), {}
     return pl.pallas_call(
         kernel,
         out_shape=jax.ShapeDtypeStruct((height, width), jnp.float32),
@@ -198,14 +199,14 @@
 
 
 def finish_second_kernel(mine, other, degrees, features, weight, first, out, done, sems):
-    half, size = mine.shape[0], degrees.shape[1]
-    copies = [pltpu.make_async_copy(first, out.at[pl.ds(0, half)], sems.at[half // size])]
+    start, rows, size = first.shape[0], mine.shape[0], degrees.shape[1]
+    copies = [pltpu.make_async_copy(first, out.at[pl.ds(0, start)], sems.at[rows // size])]
     copies[0].start()
     inverse = inverse_columns(degrees)
-    for i in range(half // size):
-        finish_rows(i, half, mine, other, inverse, features, weight, done)
+    for i in range(rows // size):
+        finish_rows(i, start, mine, other, inverse, features, weight, done)
         group = done.at[pl.ds(i * size, size)]
-        copies.append(pltpu.make_async_copy(group, out.at[pl.ds(half + i * size, size)], sems.at[i]))
+        copies.append(pltpu.make_async_copy(group, out.at[pl.ds(start + i * size, size)], sems.at[i]))
         copies[-1].start()
     for copy in copies:
         copy.wait()

time: 68.9 us -> 68.9 us (level)
  transfers between devices with their start and end apart: 16 -> 16, of which waited for: 8 -> 8; matrix products, arithmetic and copies ran while one was open for 3% -> 3% of each run, Pallas kernels for 17% -> 16%
where the time goes in v5:
time: 68.9 us; the launch traced here: 67.9 us
  starting transfers between devices  28.6 us (42%)
  waiting for transfers between devices  23.8 us (35%)
  Pallas kernels  13.2 us (19%)
  local copies, waits for them, and re-layouts  1.11 us (2%)
  other arithmetic  0.87 us (1%)
    ppermute x16, starting transfers between devices, on_device(): send = lambda x, pairs: lax.ppermute(x, AXES, pairs)  28.6 us
    ppermute x16, waiting for transfers between devices, on_device(): send = lambda x, pairs: lax.ppermute(x, AXES, pairs)  23.8 us
    pallas_call x5, Pallas kernels, multiply(): pl.pallas_call(kernel, out_shape=jax.ShapeDtypeStruct((height, width), jn...  5.87 us
    pallas_call x1, Pallas kernels, on_device(): pl.pallas_call(prepare_kernel, out_shape=[matrix] * COLORS, in_specs=[SME...  3.69 us
    pallas_call x2, Pallas kernels, finish(): pl.pallas_call(finish_second_kernel if last else finish_first_kernel, out...  1.63 us
    pallas_call x1, Pallas kernels, on_device(): pl.pallas_call(functools.partial(scale_kernel, blocks), out_shape=[jax.Sh...  1.45 us
  transfers between devices with their start and end apart: 16, of which 8 were waited for; matrix products, arithmetic and copies ran while one was open for 3% of the time, Pallas kernels for 16%

profile of v5, /device:TPU:1, one launch (start us, length us, event | category | flops | bytes accessed | tf_op | source)
XLA Modules:
  0.0 67.9 jit_solution(17314750850862820771)
XLA Ops:
  0.0 3.2 %collective-permute-start.10 = (bf16[8,11,256,256]{3,2,1,0:T(8,128)(2,1)}, bf16[8,11,256,256]{3,2,1,0:T(8,128)(2,1)}, u32[]{:S(2)}, u32[]{:S(2)}) collective-permute-start(bf16[8,11,256,256]{3,2,1,0:T(8,128)(2,1)} %bitcast.15), channel_id=1, source_target_pairs={{0,1},{1,0},{2,3},{3,2},{4,5},{5,4},{6,7},{7,6},{8,9},{9,8},{10,11... | collective-permute-start | bytes 34603016 | tf_op jit(solution)/shard_map/ppermute | solution.py:240
  3.2 1.5 %shard_map.76 = (bf16[384,256]{1,0:T(8,128)(2,1)S(1)}, bf16[384,256]{1,0:T(8,128)(2,1)S(1)}, bf16[384,256]{1,0:T(8,128)(2,1)S(1)}, bf16[384,256]{1,0:T(8,128)(2,1)S(1)}) custom-call(bf16[1536,256]{1,0:T(8,128)(2,1)} %features.5, s32[12,128]{1,0:T(8,128)} %bitcast.12), custom_call_target="tpu_custom_call" | custom-call | tf_op jit(solution)/shard_map/pallas_call | solution.py:255
  4.7 0.7 collective-permute-start
  5.4 2.5 %collective-permute-start.1 = (bf16[384,256]{1,0:T(8,128)(2,1)S(1)}, bf16[384,256]{1,0:T(8,128)(2,1)S(1)}, u32[]{:S(2)}, u32[]{:S(2)}) collective-permute-start(bf16[384,256]{1,0:T(8,128)(2,1)S(1)} %get-tuple-element.18), channel_id=1, source_target_pairs={{0,16},{1,12},{129,133},{128,147},{32,48},{33,60},{161,165},{160,1... | collective-permute-start | bytes 589832 | tf_op jit(solution)/shard_map/ppermute | solution.py:240
  7.9 2.0 %collective-permute-start.2 = (bf16[384,256]{1,0:T(8,128)(2,1)S(1)}, bf16[384,256]{1,0:T(8,128)(2,1)S(1)}, u32[]{:S(2)}, u32[]{:S(2)}) collective-permute-start(bf16[384,256]{1,0:T(8,128)(2,1)S(1)} %get-tuple-element.19), channel_id=1, source_target_pairs={{0,250},{1,88},{129,111},{128,199},{32,10},{33,104},{161,139},{160... | collective-permute-start | bytes 589832 | tf_op jit(solution)/shard_map/ppermute | solution.py:240
  9.9 1.3 %collective-permute-start.3 = (bf16[384,256]{1,0:T(8,128)(2,1)S(1)}, bf16[384,256]{1,0:T(8,128)(2,1)S(1)}, u32[]{:S(2)}, u32[]{:S(2)}) collective-permute-start(bf16[384,256]{1,0:T(8,128)(2,1)S(1)} %get-tuple-element.20), channel_id=1, source_target_pairs={{0,230},{1,34},{129,121},{128,169},{32,6},{33,66},{161,153},{160,2... | collective-permute-start | bytes 589832 | tf_op jit(solution)/shard_map/ppermute | solution.py:240
  11.2 0.8 %fusion.2 = (s32[1,8,22]{2,1,0:T(8,128)S(1)}, s32[1,8,22]{2,1,0:T(8,128)S(1)}) fusion(s32[1,8,22]{2,1,0:T(8,128)} %param.11, s32[8]{0:T(128)} %bitcast.21), kind=kLoop, calls=%fused_computation.9 | loop fusion | flops 2816 | bytes 2144 | tf_op jit(solution)/shard_map/mul | solution.py:270
  12.3 0.7 %constant_dynamic-slice_fusion = s32[1,9]{1,0:T(1,128)S(1)} fusion(s32[256,9]{1,0:T(8,128)} %constant.45.clone, s32[]{:T(128)S(6)} %select_n.39), kind=kLoop, calls=%fused_computation.16 | loop fusion | bytes 76 | tf_op jit(solution)/shard_map/jit(dynamic_index_in_dim)/dynamic_slice | solution.py:246
  13.1 1.2 %collective-permute-done.2 = bf16[384,256]{1,0:T(8,128)(2,1)S(1)} collective-permute-done((bf16[384,256]{1,0:T(8,128)(2,1)S(1)}, bf16[384,256]{1,0:T(8,128)(2,1)S(1)}, u32[]{:S(2)}, u32[]{:S(2)}) %collective-permute-start.2) | collective-permute-done | bytes 196640 | tf_op jit(solution)/shard_map/ppermute | solution.py:240
  14.3 2.4 %collective-permute-done.3 = bf16[384,256]{1,0:T(8,128)(2,1)S(1)} collective-permute-done((bf16[384,256]{1,0:T(8,128)(2,1)S(1)}, bf16[384,256]{1,0:T(8,128)(2,1)S(1)}, u32[]{:S(2)}, u32[]{:S(2)}) %collective-permute-start.3) | collective-permute-done | bytes 196640 | tf_op jit(solution)/shard_map/ppermute | solution.py:240
  16.8 0.7 collective-permute-start.4
  17.4 0.7 collective-permute-start.5
  18.1 1.3 %collective-permute-start.6 = (bf16[384,256]{1,0:T(8,128)(2,1)S(1)}, bf16[384,256]{1,0:T(8,128)(2,1)S(1)}, u32[]{:S(2)}, u32[]{:S(2)}) collective-permute-start(bf16[384,256]{1,0:T(8,128)(2,1)S(1)} %add_add_fusion.1), channel_id=1, source_target_pairs={{0,200},{62,156},{16,46},{12,84},{250,212},{88,128},{230,190},{34,... | collective-permute-start | bytes 589832 | tf_op jit(solution)/shard_map/ppermute | solution.py:240
  19.4 11.8 %collective-permute-done.6 = bf16[384,256]{1,0:T(8,128)(2,1)S(1)} collective-permute-done((bf16[384,256]{1,0:T(8,128)(2,1)S(1)}, bf16[384,256]{1,0:T(8,128)(2,1)S(1)}, u32[]{:S(2)}, u32[]{:S(2)}) %collective-permute-start.6) | collective-permute-done | bytes 196640 | tf_op jit(solution)/shard_map/ppermute | solution.py:240
  31.3 0.7 %collective-permute-start.8 = (bf16[384,256]{1,0:T(8,128)(2,1)S(1)}, bf16[384,256]{1,0:T(8,128)(2,1)S(1)}, u32[]{:S(2)}, u32[]{:S(2)}) collective-permute-start(bf16[384,256]{1,0:T(8,128)(2,1)S(1)} %add_add_fusion.refs_0_), channel_id=1, source_target_pairs={{12,0},{0,12},{28,16},{16,28},{46,34},{34,46},{62,50},{50,62},{72,... | collective-permute-start | bytes 589832 | tf_op jit(solution)/shard_map/ppermute | solution.py:240
  32.1 5.5 %collective-permute-start.9 = (bf16[384,256]{1,0:T(8,128)(2,1)S(1)}, bf16[384,256]{1,0:T(8,128)(2,1)S(1)}, u32[]{:S(2)}, u32[]{:S(2)}) collective-permute-start(bf16[384,256]{1,0:T(8,128)(2,1)S(1)} %add_add_fusion.refs_0_), channel_id=1, source_target_pairs={{234,0},{230,12},{250,16},{246,28},{72,34},{68,46},{88,50},{84,62}... | collective-permute-start | bytes 589832 | tf_op jit(solution)/shard_map/ppermute | solution.py:240
  37.7 2.6 %collective-permute-done.7.refs_1_ = bf16[384,256]{1,0:T(8,128)(2,1)S(1)} collective-permute-done((bf16[384,256]{1,0:T(8,128)(2,1)S(1)}, bf16[384,256]{1,0:T(8,128)(2,1)S(1)}, u32[]{:S(2)}, u32[]{:S(2)}) %collective-permute-start.7) | collective-permute-done | bytes 196640 | tf_op jit(solution)/shard_map/ppermute | solution.py:240
  40.2 3.0 %collective-permute-done.9.refs_3_ = bf16[384,256]{1,0:T(8,128)(2,1)S(1)} collective-permute-done((bf16[384,256]{1,0:T(8,128)(2,1)S(1)}, bf16[384,256]{1,0:T(8,128)(2,1)S(1)}, u32[]{:S(2)}, u32[]{:S(2)}) %collective-permute-start.9) | collective-permute-done | bytes 196640 | tf_op jit(solution)/shard_map/ppermute | solution.py:240
  43.2 0.6 shard_map.77.source
  43.8 1.9 %collective-permute-start.13 = (bf16[1536,256]{1,0:T(8,128)(2,1)S(1)}, bf16[1536,256]{1,0:T(8,128)(2,1)S(1)}, u32[]{:S(2)}, u32[]{:S(2)}) collective-permute-start(bf16[1536,256]{1,0:T(8,128)(2,1)S(1)} %shard_map.77.source), channel_id=1, source_target_pairs={{0,32},{1,225},{2,34},{3,227},{4,36},{5,229},{6,38},{7,231},{8,40}... | collective-permute-start | bytes 2359304 | tf_op jit(solution)/shard_map/ppermute | solution.py:240
  45.7 3.3 %collective-permute-start.12 = (bf16[1536,256]{1,0:T(8,128)(2,1)S(1)}, bf16[1536,256]{1,0:T(8,128)(2,1)S(1)}, u32[]{:S(2)}, u32[]{:S(2)}) collective-permute-start(bf16[1536,256]{1,0:T(8,128)(2,1)S(1)} %shard_map.77.source), channel_id=1, source_target_pairs={{0,8},{1,25},{2,10},{3,27},{4,12},{5,29},{6,14},{7,31},{8,16},{9,1... | collective-permute-start | bytes 2359304 | tf_op jit(solution)/shard_map/ppermute | solution.py:240
  49.1 2.3 %collective-permute-start.11 = (bf16[1536,256]{1,0:T(8,128)(2,1)S(1)}, bf16[1536,256]{1,0:T(8,128)(2,1)S(1)}, u32[]{:S(2)}, u32[]{:S(2)}) collective-permute-start(bf16[1536,256]{1,0:T(8,128)(2,1)S(1)} %shard_map.77.source), channel_id=1, source_target_pairs={{0,2},{1,7},{2,4},{3,1},{4,6},{5,3},{6,0},{7,5},{8,10},{9,15},{10,... | collective-permute-start | bytes 2359304 | tf_op jit(solution)/shard_map/ppermute | solution.py:240
  51.4 3.7 %shard_map.78 = (bf16[1536,1536]{1,0:T(8,128)(2,1)S(1)}, bf16[1536,1536]{1,0:T(8,128)(2,1)S(1)}, bf16[1536,1536]{1,0:T(8,128)(2,1)S(1)}, bf16[1536,1536]{1,0:T(8,128)(2,1)S(1)}) custom-call(s32[4]{0:T(128)S(1)} %get-tuple-element.22.order, s32[352]{0:T(512)S(1)} %reshape.51.table, bf16[8,11,256,256]{3,2,1,0:T(8,128)(2,1)} %bitcast.16, ...), custom_call_target="tpu_custom_call" | custom-call | bytes 23068672 | tf_op jit(solution)/shard_map/pallas_call | solution.py:291
  55.1 1.4 %shard_map.79.refs_0_ = f32[1536,256]{1,0:T(8,128)S(1)} custom-call(bf16[1536,1536]{1,0:T(8,128)(2,1)S(1)} %get-tuple-element.28.mat, bf16[1536,256]{1,0:T(8,128)(2,1)S(1)} %shard_map.77.source), custom_call_target="tpu_custom_call" | custom-call | flops 1207959552 | bytes 4718592 | tf_op jit(solution)/shard_map/pallas_call | solution.py:172
  56.5 1.1 %collective-permute-done.13.source = bf16[1536,256]{1,0:T(8,128)(2,1)S(1)} collective-permute-done((bf16[1536,256]{1,0:T(8,128)(2,1)S(1)}, bf16[1536,256]{1,0:T(8,128)(2,1)S(1)}, u32[]{:S(2)}, u32[]{:S(2)}) %collective-permute-start.13) | collective-permute-done | bytes 786464 | tf_op jit(solution)/shard_map/ppermute | solution.py:240
  57.6 1.5 %shard_map.80.refs_0_ = f32[1536,256]{1,0:T(8,128)S(1)} custom-call(bf16[1536,1536]{1,0:T(8,128)(2,1)S(1)} %get-tuple-element.27.mat, bf16[1536,256]{1,0:T(8,128)(2,1)S(1)} %collective-permute-done.13.source, f32[1536,256]{1,0:T(8,128)S(1)} %shard_map.79.refs_0_), custom_call_target="tpu_custom_call", output_to_operand_aliasing={{}: (2, {})} | custom-call | flops 1207959552 | bytes 4718592 | tf_op jit(solution)/shard_map/pallas_call | solution.py:172
  59.0 1.5 %shard_map.81.before = f32[1536,256]{1,0:T(8,128)S(1)} custom-call(bf16[1536,1536]{1,0:T(8,128)(2,1)S(1)} %get-tuple-element.26.mat, bf16[1536,256]{1,0:T(8,128)(2,1)S(1)} %collective-permute-done.12.source, f32[1536,256]{1,0:T(8,128)S(1)} %shard_map.80.refs_0_), custom_call_target="tpu_custom_call", output_to_operand_aliasing={{}: (2, {})} | custom-call | flops 1207959552 | bytes 4718592 | tf_op jit(solution)/shard_map/pallas_call | solution.py:172
  60.5 1.0 %shard_map.83.mine = f32[1024,256]{1,0:T(8,128)S(1)} custom-call(bf16[1536,1536]{1,0:T(8,128)(2,1)S(1)} %get-tuple-element.24.mat, bf16[1536,256]{1,0:T(8,128)(2,1)S(1)} %collective-permute-done.11.source, f32[1536,256]{1,0:T(8,128)S(1)} %shard_map.81.before), custom_call_target="tpu_custom_call" | custom-call | flops 805306368 | bytes 4718592 | tf_op jit(solution)/shard_map/pallas_call | solution.py:172
  61.5 2.2 %collective-permute-start.15 = (f32[1024,256]{1,0:T(8,128)S(1)}, f32[1024,256]{1,0:T(8,128)S(1)}, u32[]{:S(2)}, u32[]{:S(2)}) collective-permute-start(f32[1024,256]{1,0:T(8,128)S(1)} %shard_map.83.mine), channel_id=1, source_target_pairs={{0,1},{1,0},{2,3},{3,2},{4,5},{5,4},{6,7},{7,6},{8,9},{9,8},{10,11... | collective-permute-start | bytes 3145736 | tf_op jit(solution)/shard_map/ppermute | solution.py:240
  63.7 0.6 shard_map.82.mine
  64.4 1.6 %collective-permute-done.15.other = f32[1024,256]{1,0:T(8,128)S(1)} collective-permute-done((f32[1024,256]{1,0:T(8,128)S(1)}, f32[1024,256]{1,0:T(8,128)S(1)}, u32[]{:S(2)}, u32[]{:S(2)}) %collective-permute-start.15) | collective-permute-done | bytes 1048608 | tf_op jit(solution)/shard_map/ppermute | solution.py:240
  66.8 1.1 %shard_map.85 = bf16[1536,256]{1,0:T(8,128)(2,1)} custom-call(f32[512,256]{1,0:T(8,128)S(1)} %shard_map.82.mine, f32[512,256]{1,0:T(8,128)S(1)} %collective-permute-done.14.other, s32[12,128]{1,0:T(8,128)S(1)} %bitcast.14, bf16[1536,256]{1,0:T(8,128)(2,1)S(1)} %copy-done, bf16[256,256]{1,0:T(8,128)(2,1)S(1)} %copy-done.1, bf16[1024,256]{1,0:T(8,128)(2,1)S(1)} %shard_map.84.first), custom_call_target="tpu_custom_call" | custom-call | flops 67108864 | bytes 1572864 | tf_op jit(solution)/shard_map/pallas_call | solution.py:219
  (28 shorter events, 1.5 us)
Async XLA Ops:
  0.0 51.4 %collective-permute-start.10 = (bf16[8,11,256,256]{3,2,1,0:T(8,128)(2,1)}, bf16[8,11,256,256]{3,2,1,0:T(8,128)(2,1)}, u32[]{:S(2)}, u32[]{:S(2)}) collective-permute-start(bf16[8,11,256,256]{3,2,1,0:T(8,128)(2,1)} %bitcast.15), channel_id=1, source_target_pairs={{0,1},{1,0},{2,3},{3,2},{4,5},{5,4},{6,7},{7,6},{8,9},{9,8},{10,11... | collective-permute-start | bytes 34603016 | tf_op jit(solution)/shard_map/ppermute | solution.py:240
  4.7 8.4 %collective-permute-start = (bf16[384,256]{1,0:T(8,128)(2,1)S(1)}, bf16[384,256]{1,0:T(8,128)(2,1)S(1)}, u32[]{:S(2)}, u32[]{:S(2)}) collective-permute-start(bf16[384,256]{1,0:T(8,128)(2,1)S(1)} %get-tuple-element.17), channel_id=1, source_target_pairs={{0,62},{129,191},{32,78},{161,219},{64,58},{193,175},{96,74},{225,... | collective-permute-start | bytes 589832 | tf_op jit(solution)/shard_map/ppermute | solution.py:240
  5.4 7.7 %collective-permute-start.1 = (bf16[384,256]{1,0:T(8,128)(2,1)S(1)}, bf16[384,256]{1,0:T(8,128)(2,1)S(1)}, u32[]{:S(2)}, u32[]{:S(2)}) collective-permute-start(bf16[384,256]{1,0:T(8,128)(2,1)S(1)} %get-tuple-element.18), channel_id=1, source_target_pairs={{0,16},{1,12},{129,133},{128,147},{32,48},{33,60},{161,165},{160,1... | collective-permute-start | bytes 589832 | tf_op jit(solution)/shard_map/ppermute | solution.py:240
  7.9 6.4 %collective-permute-start.2 = (bf16[384,256]{1,0:T(8,128)(2,1)S(1)}, bf16[384,256]{1,0:T(8,128)(2,1)S(1)}, u32[]{:S(2)}, u32[]{:S(2)}) collective-permute-start(bf16[384,256]{1,0:T(8,128)(2,1)S(1)} %get-tuple-element.19), channel_id=1, source_target_pairs={{0,250},{1,88},{129,111},{128,199},{32,10},{33,104},{161,139},{160... | collective-permute-start | bytes 589832 | tf_op jit(solution)/shard_map/ppermute | solution.py:240
  9.9 6.8 %collective-permute-start.3 = (bf16[384,256]{1,0:T(8,128)(2,1)S(1)}, bf16[384,256]{1,0:T(8,128)(2,1)S(1)}, u32[]{:S(2)}, u32[]{:S(2)}) collective-permute-start(bf16[384,256]{1,0:T(8,128)(2,1)S(1)} %get-tuple-element.20), channel_id=1, source_target_pairs={{0,230},{1,34},{129,121},{128,169},{32,6},{33,66},{161,153},{160,2... | collective-permute-start | bytes 589832 | tf_op jit(solution)/shard_map/ppermute | solution.py:240
  16.8 2.7 %collective-permute-start.4 = (bf16[384,256]{1,0:T(8,128)(2,1)S(1)}, bf16[384,256]{1,0:T(8,128)(2,1)S(1)}, u32[]{:S(2)}, u32[]{:S(2)}) collective-permute-start(bf16[384,256]{1,0:T(8,128)(2,1)S(1)} %add_add_fusion.1), channel_id=1, source_target_pairs={{0,72},{62,102},{16,118},{12,140},{250,162},{88,68},{230,246},{34,... | collective-permute-start | bytes 589832 | tf_op jit(solution)/shard_map/ppermute | solution.py:240
  17.4 2.0 %collective-permute-start.5 = (bf16[384,256]{1,0:T(8,128)(2,1)S(1)}, bf16[384,256]{1,0:T(8,128)(2,1)S(1)}, u32[]{:S(2)}, u32[]{:S(2)}) collective-permute-start(bf16[384,256]{1,0:T(8,128)(2,1)S(1)} %add_add_fusion.1), channel_id=1, source_target_pairs={{0,28},{62,216},{16,178},{12,174},{250,234},{88,144},{230,196},{34... | collective-permute-start | bytes 589832 | tf_op jit(solution)/shard_map/ppermute | solution.py:240
  18.1 13.1 %collective-permute-start.6 = (bf16[384,256]{1,0:T(8,128)(2,1)S(1)}, bf16[384,256]{1,0:T(8,128)(2,1)S(1)}, u32[]{:S(2)}, u32[]{:S(2)}) collective-permute-start(bf16[384,256]{1,0:T(8,128)(2,1)S(1)} %add_add_fusion.1), channel_id=1, source_target_pairs={{0,200},{62,156},{16,46},{12,84},{250,212},{88,128},{230,190},{34,... | collective-permute-start | bytes 589832 | tf_op jit(solution)/shard_map/ppermute | solution.py:240
  31.2 9.0 %collective-permute-start.7 = (bf16[384,256]{1,0:T(8,128)(2,1)S(1)}, bf16[384,256]{1,0:T(8,128)(2,1)S(1)}, u32[]{:S(2)}, u32[]{:S(2)}) collective-permute-start(bf16[384,256]{1,0:T(8,128)(2,1)S(1)} %add_add_fusion.refs_0_), channel_id=1, source_target_pairs={{230,0},{234,12},{246,16},{250,28},{68,34},{72,46},{84,50},{88,62}... | collective-permute-start | bytes 589832 | tf_op jit(solution)/shard_map/ppermute | solution.py:240
  31.3 8.9 %collective-permute-start.8 = (bf16[384,256]{1,0:T(8,128)(2,1)S(1)}, bf16[384,256]{1,0:T(8,128)(2,1)S(1)}, u32[]{:S(2)}, u32[]{:S(2)}) collective-permute-start(bf16[384,256]{1,0:T(8,128)(2,1)S(1)} %add_add_fusion.refs_0_), channel_id=1, source_target_pairs={{12,0},{0,12},{28,16},{16,28},{46,34},{34,46},{62,50},{50,62},{72,... | collective-permute-start | bytes 589832 | tf_op jit(solution)/shard_map/ppermute | solution.py:240
  32.1 11.1 %collective-permute-start.9 = (bf16[384,256]{1,0:T(8,128)(2,1)S(1)}, bf16[384,256]{1,0:T(8,128)(2,1)S(1)}, u32[]{:S(2)}, u32[]{:S(2)}) collective-permute-start(bf16[384,256]{1,0:T(8,128)(2,1)S(1)} %add_add_fusion.refs_0_), channel_id=1, source_target_pairs={{234,0},{230,12},{250,16},{246,28},{72,34},{68,46},{88,50},{84,62}... | collective-permute-start | bytes 589832 | tf_op jit(solution)/shard_map/ppermute | solution.py:240
  43.8 13.8 %collective-permute-start.13 = (bf16[1536,256]{1,0:T(8,128)(2,1)S(1)}, bf16[1536,256]{1,0:T(8,128)(2,1)S(1)}, u32[]{:S(2)}, u32[]{:S(2)}) collective-permute-start(bf16[1536,256]{1,0:T(8,128)(2,1)S(1)} %shard_map.77.source), channel_id=1, source_target_pairs={{0,32},{1,225},{2,34},{3,227},{4,36},{5,229},{6,38},{7,231},{8,40}... | collective-permute-start | bytes 2359304 | tf_op jit(solution)/shard_map/ppermute | solution.py:240
  45.7 13.3 %collective-permute-start.12 = (bf16[1536,256]{1,0:T(8,128)(2,1)S(1)}, bf16[1536,256]{1,0:T(8,128)(2,1)S(1)}, u32[]{:S(2)}, u32[]{:S(2)}) collective-permute-start(bf16[1536,256]{1,0:T(8,128)(2,1)S(1)} %shard_map.77.source), channel_id=1, source_target_pairs={{0,8},{1,25},{2,10},{3,27},{4,12},{5,29},{6,14},{7,31},{8,16},{9,1... | collective-permute-start | bytes 2359304 | tf_op jit(solution)/shard_map/ppermute | solution.py:240
  49.1 11.5 %collective-permute-start.11 = (bf16[1536,256]{1,0:T(8,128)(2,1)S(1)}, bf16[1536,256]{1,0:T(8,128)(2,1)S(1)}, u32[]{:S(2)}, u32[]{:S(2)}) collective-permute-start(bf16[1536,256]{1,0:T(8,128)(2,1)S(1)} %shard_map.77.source), channel_id=1, source_target_pairs={{0,2},{1,7},{2,4},{3,1},{4,6},{5,3},{6,0},{7,5},{8,10},{9,15},{10,... | collective-permute-start | bytes 2359304 | tf_op jit(solution)/shard_map/ppermute | solution.py:240
  61.5 4.5 %copy-start = (bf16[1536,256]{1,0:T(8,128)(2,1)S(1)}, bf16[1536,256]{1,0:T(8,128)(2,1)}, u32[]{:S(2)}) copy-start(bf16[1536,256]{1,0:T(8,128)(2,1)} %features.5) | copy-start | bytes 2359300
  61.5 4.5 %copy-start.1 = (bf16[256,256]{1,0:T(8,128)(2,1)S(1)}, bf16[256,256]{1,0:T(8,128)(2,1)}, u32[]{:S(2)}) copy-start(bf16[256,256]{1,0:T(8,128)(2,1)} %weight.3) | copy-start | bytes 393220
  61.5 4.5 %copy-start.2 = (s32[1536]{0:T(1024)S(1)}, s32[1536]{0:T(1024)}, u32[]{:S(2)}) copy-start(s32[1536]{0:T(1024)} %param.8) | copy-start | bytes 18436
  61.5 4.5 %collective-permute-start.15 = (f32[1024,256]{1,0:T(8,128)S(1)}, f32[1024,256]{1,0:T(8,128)S(1)}, u32[]{:S(2)}, u32[]{:S(2)}) collective-permute-start(f32[1024,256]{1,0:T(8,128)S(1)} %shard_map.83.mine), channel_id=1, source_target_pairs={{0,1},{1,0},{2,3},{3,2},{4,5},{5,4},{6,7},{7,6},{8,9},{9,8},{10,11... | collective-permute-start | bytes 3145736 | tf_op jit(solution)/shard_map/ppermute | solution.py:240
  64.3 2.5 %collective-permute-start.14 = (f32[512,256]{1,0:T(8,128)S(1)}, f32[512,256]{1,0:T(8,128)S(1)}, u32[]{:S(2)}, u32[]{:S(2)}) collective-permute-start(f32[512,256]{1,0:T(8,128)S(1)} %shard_map.82.mine), channel_id=1, source_target_pairs={{0,1},{1,0},{2,3},{3,2},{4,5},{5,4},{6,7},{7,6},{8,9},{9,8},{10,11... | collective-permute-start | bytes 1572872 | tf_op jit(solution)/shard_map/ppermute | solution.py:240
